TPU v7x, 32 devices: a whole 2x2x4 slice. The times are simulated.
32 devices in a mesh: groups: 2 (over x), tensor: 16 (over z, y, core).
Axes of the slice: x: 2, y: 2, z: 4, core: 2. Of those that a mesh axis runs over, the one named last changes fastest.
Arguments:
- tokens: bfloat16 [256, 4096], P(('groups', 'tensor')), parts along dimension 0, may hold values from -6 to 6
- gate_weight: bfloat16 [14336, 4096], P('tensor'), may hold values from -0.09375 to 0.09375
- up_weight: bfloat16 [14336, 4096], P('tensor'), may hold values from -0.09375 to 0.09375
- down_weight: bfloat16 [14336, 4096], P('tensor'), may hold values from -0.046875 to 0.046875
- cotangent: bfloat16 [256, 4096], P(('groups', 'tensor')), parts along dimension 0, may hold values from -6 to 6
Outputs:
- output: bfloat16 [256, 4096], P(('groups', 'tensor')), parts along dimension 0
- input_grad: bfloat16 [256, 4096], P(('groups', 'tensor')), parts along dimension 0
- gate_grad: bfloat16 [14336, 8192], P('tensor', 'groups'), parts along dimension 1
- up_grad: bfloat16 [14336, 8192], P('tensor', 'groups'), parts along dimension 1
- down_grad: bfloat16 [14336, 8192], P('tensor', 'groups'), parts along dimension 1
There are 2 independent parts, one for each index of `groups`. A program takes and returns all parts, laid end to end along the dimension named above; an argument that names none is the same for every part. Nothing has to cross between parts.
All inputs are finite; a program needn't handle non-finite values.
Results may differ from a plain program's by a relative error of at most 0.0052.
Values may be sent and summed in bfloat16 or wider, within the bound.
No kernel may reach another device: no remote copies, remote signals or barrier semaphores. Data moves between devices by JAX's collectives and lax.ppermute only.
A program may use at most 128 MiB of HBM per device.

v0:
```python
import jax
import jax.numpy as jnp
from jax import lax
from jax.sharding import PartitionSpec as P


def rows_by_weight(left, weight):
    return lax.dot_general(
        left, weight, (((1,), (1,)), ((), ())), preferred_element_type=jnp.float32
    )


def over_tokens(left, right):
    return lax.dot_general(
        left, right, (((0,), (0,)), ((), ())), preferred_element_type=jnp.float32
    )


def per_device(tokens, gate_weight, up_weight, down_weight, cotangent):
    whole = lax.all_gather(tokens, "tensor", axis=0, tiled=True)
    gate = rows_by_weight(whole, gate_weight)
    up = rows_by_weight(whole, up_weight)
    sig = jax.nn.sigmoid(gate)
    act = gate * sig
    hidden = (act * up).astype(jnp.bfloat16)
    terms = jnp.dot(hidden, down_weight, preferred_element_type=jnp.float32)
    mixed = lax.psum_scatter(terms, "tensor", scatter_dimension=0, tiled=True)
    output = mixed.astype(jnp.bfloat16)
    grads = lax.all_gather(cotangent, "tensor", axis=0, tiled=True)
    d_hidden = rows_by_weight(grads, down_weight)
    d_gate = (d_hidden * up * sig * (1.0 + gate * (1.0 - sig))).astype(jnp.bfloat16)
    d_up = (d_hidden * act).astype(jnp.bfloat16)
    down_grad = over_tokens(hidden, grads).astype(jnp.bfloat16)
    gate_grad = over_tokens(d_gate, whole).astype(jnp.bfloat16)
    up_grad = over_tokens(d_up, whole).astype(jnp.bfloat16)
    back_terms = jnp.dot(d_gate, gate_weight, preferred_element_type=jnp.float32)
    back_terms = back_terms + jnp.dot(d_up, up_weight, preferred_element_type=jnp.float32)
    summed = lax.psum_scatter(back_terms, "tensor", scatter_dimension=0, tiled=True)
    input_grad = summed.astype(jnp.bfloat16)
    return (output, input_grad, gate_grad, up_grad, down_grad)


def solution(mesh):
    return jax.shard_map(
        per_device,
        mesh=mesh,
        in_specs=(
            P(("groups", "tensor"), None),
            P("tensor", None),
            P("tensor", None),
            P("tensor", None),
            P(("groups", "tensor"), None),
        ),
        out_specs=(
            P(("groups", "tensor"), None),
            P(("groups", "tensor"), None),
            P("tensor", "groups"),
            P("tensor", "groups"),
            P("tensor", "groups"),
        ),
        check_vma=False,
    )
```

profile of v0, /device:TPU:0, one launch (start us, length us, event | category | flops | bytes accessed | tf_op | source)
XLA Modules:
  0.0 236.5 jit_solution(5552260410614296767)
XLA Ops:
  7.2 0.0 all-gather.3.cloned.1.call-start
  7.2 0.7 all-gather.3.cloned.1.call-update
  7.9 0.0 all-gather.5.cloned.1.call-start
  7.9 0.7 all-gather.5.cloned.1.call-update
  8.6 0.0 reduce-scatter.5.cloned.1.call-start
  8.7 42.1 %all-gather.3.cloned.1.call-done = bf16[128,4096]{1,0:T(8,128)(2,1)} async-done(((bf16[8,4096]{1,0:T(8,128)(2,1)}), bf16[128,4096]{1,0:T(8,128)(2,1)}) %all-gather.3.cloned.1.call-update) | async-done | bytes 1048592 | tf_op jit(solution)/shard_map/all_gather | solution.py:20
  50.8 0.0 copy-start
  50.8 0.0 copy-start.1
  50.8 6.0 %fusion.2 = f32[128,896]{1,0:T(8,128)S(1)} fusion(bf16[128,4096]{1,0:T(8,128)(2,1)} %all-gather.3.cloned.1.call-done, bf16[896,4096]{1,0:T(8,128)(2,1)} %param.7), kind=kOutput, calls=%fused_computation.10 | convolution fusion | flops 939524096 | bytes 8847360 | tf_op jit(solution)/shard_map/dot_general | solution.py:8
  56.8 0.0 copy-done
  56.8 0.0 copy-done.1
  56.9 2.5 %fusion.1 = f32[128,896]{1,0:T(8,128)S(1)} fusion(bf16[128,4096]{1,0:T(8,128)(2,1)S(1)} %copy-done.1, bf16[896,4096]{1,0:T(8,128)(2,1)S(1)} %copy-done), kind=kOutput, calls=%fused_computation.9 | convolution fusion | flops 939524096 | bytes 8847360 | tf_op jit(solution)/shard_map/dot_general | solution.py:8
  59.3 30.6 %all-gather.5.cloned.1.call-done = bf16[128,4096]{1,0:T(8,128)(2,1)} async-done(((bf16[8,4096]{1,0:T(8,128)(2,1)}), bf16[128,4096]{1,0:T(8,128)(2,1)}) %all-gather.5.cloned.1.call-update) | async-done | bytes 1048592 | tf_op jit(solution)/shard_map/all_gather | solution.py:29
  89.9 6.0 %multiply_convert_fusion = (bf16[128,896]{1,0:T(8,128)(2,1)S(1)}, bf16[128,896]{1,0:T(8,128)(2,1)S(1)}, bf16[128,896]{1,0:T(8,128)(2,1)S(1)}) fusion(f32[128,896]{1,0:T(8,128)S(1)} %fusion.1, f32[128,896]{1,0:T(8,128)S(1)} %fusion.2, bf16[128,4096]{1,0:T(8,128)(2,1)} %all-gather.5.cloned.1.call-done, bf16[896,4096]{1,0:T(8,128)(2,1)} %param.8), kind=kOutput, calls=%fused_computation.4 | convolution fusion | flops 941244416 | bytes 9994240 | tf_op jit(solution)/shard_map/dot_general | solution.py:8
  95.9 0.0 slice-start.1
  95.9 4.5 %fusion.4 = f32[128,4096]{1,0:T(8,128)S(1)} fusion(bf16[128,896]{1,0:T(8,128)(2,1)S(1)} %get-tuple-element.6, bf16[896,4096]{1,0:T(8,128)(2,1)} %param.6), kind=kOutput, calls=%fused_computation.12 | convolution fusion | flops 939524096 | bytes 9666560 | tf_op jit(solution)/shard_map/dot_general | solution.py:36
  100.4 0.0 slice-done
  100.4 0.0 slice-done.1
  100.5 2.7 %convolution_add_fusion = f32[128,4096]{1,0:T(8,128)} fusion(f32[128,4096]{1,0:T(8,128)S(1)} %fusion.4, bf16[128,896]{1,0:T(8,128)(2,1)S(1)} %get-tuple-element.5, bf16[896,4096]{1,0:T(8,128)(2,1)S(1)} %bitcast.19), kind=kOutput, calls=%fused_computation.3 | convolution fusion | flops 940048384 | bytes 11763712 | tf_op jit(solution)/shard_map/dot_general | solution.py:37
  103.1 0.0 reduce-scatter.5.cloned.1.call-update
  103.2 0.2 reduce-scatter.3.cloned.1.call-start
  103.4 0.0 copy-start.2
  103.4 5.8 %fusion.3 = f32[128,4096]{1,0:T(8,128)} fusion(bf16[128,896]{1,0:T(8,128)(2,1)S(1)} %get-tuple-element.7, bf16[896,4096]{1,0:T(8,128)(2,1)} %param.8), kind=kOutput, calls=%fused_computation.11 | convolution fusion | flops 939524096 | bytes 9666560 | tf_op jit(solution)/shard_map/dot_general | solution.py:26
  109.2 0.0 reduce-scatter.3.cloned.1.call-update
  109.2 0.0 copy-done.2
  109.2 5.1 %convolution_convert_fusion = bf16[896,4096]{1,0:T(8,128)(2,1)} fusion(bf16[128,896]{1,0:T(8,128)(2,1)S(1)} %get-tuple-element.7, bf16[128,4096]{1,0:T(8,128)(2,1)S(1)} %copy-done.2), kind=kOutput, calls=%fused_computation | convolution fusion | flops 943194112 | bytes 8617984 | tf_op jit(solution)/shard_map/dot_general | solution.py:14
  114.4 5.1 %convolution_convert_fusion.1 = bf16[896,4096]{1,0:T(8,128)(2,1)} fusion(bf16[128,896]{1,0:T(8,128)(2,1)S(1)} %get-tuple-element.5, bf16[128,4096]{1,0:T(8,128)(2,1)S(1)} %copy-done.1), kind=kOutput, calls=%fused_computation.1 | convolution fusion | flops 943194112 | bytes 8617984 | tf_op jit(solution)/shard_map/dot_general | solution.py:14
  119.5 5.1 %convolution_convert_fusion.2 = bf16[896,4096]{1,0:T(8,128)(2,1)} fusion(bf16[128,896]{1,0:T(8,128)(2,1)S(1)} %get-tuple-element.6, bf16[128,4096]{1,0:T(8,128)(2,1)S(1)} %copy-done.1), kind=kOutput, calls=%fused_computation.2 | convolution fusion | flops 943194112 | bytes 8617984 | tf_op jit(solution)/shard_map/dot_general | solution.py:14
  124.7 39.1 %reduce-scatter.5.cloned.1.call-done = f32[8,4096]{1,0:T(8,128)} async-done(((f32[128,4096]{1,0:T(8,128)}), f32[8,4096]{1,0:T(8,128)}) %reduce-scatter.5.cloned.1.call-update) | async-done | bytes 131088 | tf_op jit(solution)/shard_map/reduce_scatter | solution.py:38
  163.7 1.5 convert_element_type.28
  165.3 63.1 %reduce-scatter.3.cloned.1.call-done = f32[8,4096]{1,0:T(8,128)} async-done(((f32[128,4096]{1,0:T(8,128)}), f32[8,4096]{1,0:T(8,128)}) %reduce-scatter.3.cloned.1.call-update) | async-done | bytes 131088 | tf_op jit(solution)/shard_map/reduce_scatter | solution.py:27
  228.4 1.5 convert_element_type.25
  (2 shorter events, 0.0 us)
Async XLA Ops:
  7.2 43.7 %all-gather.3.cloned.1.call-start = ((), (), s32[]{:S(2)}) async-start(), calls=%async_computation.2 | async-start | bytes 1114112 | tf_op jit(solution)/shard_map/all_gather | solution.py:20
  7.9 82.0 %all-gather.5.cloned.1.call-start = ((), (), s32[]{:S(2)}) async-start(), calls=%async_computation.4 | async-start | bytes 1114112 | tf_op jit(solution)/shard_map/all_gather | solution.py:29
  8.6 155.1 %reduce-scatter.5.cloned.1.call-start = ((), (), s32[]{:S(2)}) async-start(), calls=%async_computation.5 | async-start | bytes 2228224 | tf_op jit(solution)/shard_map/reduce_scatter | solution.py:38
  50.8 6.0 %copy-start = (bf16[896,4096]{1,0:T(8,128)(2,1)S(1)}, bf16[896,4096]{1,0:T(8,128)(2,1)}, u32[]{:S(2)}) copy-start(bf16[896,4096]{1,0:T(8,128)(2,1)} %param.6) | copy-start | bytes 22020100
  50.8 6.0 %copy-start.1 = (bf16[128,4096]{1,0:T(8,128)(2,1)S(1)}, bf16[128,4096]{1,0:T(8,128)(2,1)}, u32[]{:S(2)}) copy-start(bf16[128,4096]{1,0:T(8,128)(2,1)} %all-gather.3.cloned.1.call-done) | copy-start | bytes 3145732
  89.9 10.5 %slice-start = ((s8[7340032]{0:T(1024)(128)(4,1)}), s8[3145728]{0:T(1024)(128)(4,1)S(1)}, s32[]{:S(2)}) async-start(s8[7340032]{0:T(1024)(128)(4,1)} %bitcast.18), calls=%async_computation.6 | async-start | bytes 6291456
  95.9 4.5 %slice-start.1 = ((s8[7340032]{0:T(1024)(128)(4,1)}), s8[4194304]{0:T(1024)(128)(4,1)S(1)}, s32[]{:S(2)}) async-start(s8[7340032]{0:T(1024)(128)(4,1)} %bitcast.18), calls=%async_computation.7 | async-start | bytes 8388608
  103.2 125.2 %reduce-scatter.3.cloned.1.call-start = ((), (), s32[]{:S(2)}) async-start(), calls=%async_computation.3 | async-start | bytes 2228224 | tf_op jit(solution)/shard_map/reduce_scatter | solution.py:27
  103.4 5.8 %copy-start.2 = (bf16[128,4096]{1,0:T(8,128)(2,1)S(1)}, bf16[128,4096]{1,0:T(8,128)(2,1)}, u32[]{:S(2)}) copy-start(bf16[128,4096]{1,0:T(8,128)(2,1)} %all-gather.5.cloned.1.call-done) | copy-start | bytes 3145732
Sparse Core Ops, SparseCore 0:
  10.2 40.6 all-gather.2
  53.0 36.8 all-gather.4
  103.3 60.4 reduce-scatter.4
  167.8 60.5 reduce-scatter.2
where the time goes:
time: 237 us; the launch traced here: 236 us
  waiting for transfers between devices  176 us (74%)
  matrix products  42.9 us (18%)
  between operations  13.9 us (6%)
  other arithmetic  3.08 us (1%)
    reduce_scatter x1, waiting for transfers between devices, per_device(): mixed = lax.psum_scatter(terms, 'tensor', scatter_dimension=0, tiled=True)  63.1 us
    all_gather x1, waiting for transfers between devices, per_device(): whole = lax.all_gather(tokens, 'tensor', axis=0, tiled=True)  42.1 us
    reduce_scatter x1, waiting for transfers between devices, per_device(): lax.psum_scatter(back_terms, 'tensor', scatter_dimension=0, tiled=True)  39.1 us
    all_gather x1, waiting for transfers between devices, per_device(): grads = lax.all_gather(cotangent, 'tensor', axis=0, tiled=True)  30.6 us
    dot_general x3, matrix products, over_tokens(): lax.dot_general(left, right, (((0,), (0,)), ((), ())), preferred_element_...  15.4 us
    dot_general x3, matrix products, rows_by_weight(): lax.dot_general(left, weight, (((1,), (1,)), ((), ())), preferred_element...  14.5 us
    dot_general x1, matrix products, per_device(): terms = jnp.dot(hidden, down_weight, preferred_element_type=jnp.float32)  5.78 us
  transfers between devices with their start and end apart: 4, of which 4 were waited for; matrix products, arithmetic and copies ran while one was open for 13% of the time, Pallas kernels for 0%

commit v1 on v0

v1 whole, which is shorter than its diff:
```python
import jax
import jax.numpy as jnp
from jax import lax
from jax.sharding import PartitionSpec as P

F32 = jnp.float32
BF16 = jnp.bfloat16
CORE = 1


def rows_by_weight(left, weight):
    return lax.dot_general(left, weight, (((1,), (1,)), ((), ())), preferred_element_type=F32)


def over_tokens(left, right):
    return lax.dot_general(left, right, (((0,), (0,)), ((), ())), preferred_element_type=F32)


def stages(n):
    bits = []
    b = n // 2
    while b > 1:
        bits.append(b)
        b //= 2
    return [(e, o) for e, o in zip(bits, bits[-1:] + bits[:-1])] + [(CORE, CORE)]


def swap(x, n, stage):
    return lax.ppermute(x, "tensor", [(i, i ^ stage[i % 2]) for i in range(n)])


def gather(x, n):
    for stage in stages(n):
        x = jnp.concatenate([x, swap(x, n, stage)], 0)
    return x


def scatter_sum(x, n):
    for stage in reversed(stages(n)):
        half = x.shape[0] // 2
        x = x[:half] + swap(x[half:].astype(BF16), n, stage).astype(F32)
    return x.astype(BF16)


def solution(mesh):
    n = mesh.shape["tensor"]

    def per_device(tokens, gate_weight, up_weight, down_weight, cotangent):
        whole = gather(tokens, n)
        grads = gather(cotangent, n)
        gate = rows_by_weight(whole, gate_weight)
        up = rows_by_weight(whole, up_weight)
        sig = jax.nn.sigmoid(gate)
        act = gate * sig
        hidden = (act * up).astype(BF16)
        output = scatter_sum(jnp.dot(hidden, down_weight, preferred_element_type=F32), n)
        d_hidden = rows_by_weight(grads, down_weight)
        d_gate = (d_hidden * up * sig * (1.0 + gate * (1.0 - sig))).astype(BF16)
        d_up = (d_hidden * act).astype(BF16)
        back = jnp.dot(d_gate, gate_weight, preferred_element_type=F32)
        back = back + jnp.dot(d_up, up_weight, preferred_element_type=F32)
        input_grad = scatter_sum(back, n)
        down_grad = over_tokens(hidden, grads).astype(BF16)
        gate_grad = over_tokens(d_gate, whole).astype(BF16)
        up_grad = over_tokens(d_up, whole).astype(BF16)
        return (output, input_grad, gate_grad, up_grad, down_grad)

    rows = P(("groups", "tensor"), None)
    weights = P("tensor", None)
    grads = P("tensor", "groups")
    return jax.shard_map(
        per_device,
        mesh=mesh,
        in_specs=(rows, weights, weights, weights, rows),
        out_specs=(rows, rows, grads, grads, grads),
        check_vma=False,
    )
```

time: 237 us -> 83.1 us (0.35)
  waiting for transfers between devices: 176 us -> 27.1 us
  starting transfers between devices: 0.34 us -> 14.1 us
  between operations: 13.9 us -> 1.02 us
  matrix products: 42.9 us -> 30.1 us
  other arithmetic: 3.08 us -> 6.78 us
  local copies, waits for them, and re-layouts: 0.02 us -> 3.52 us
    reduce_scatter x2 -> x0, waiting for transfers between devices: 102 us -> none  [the longest x1 63.1 us: per_device(): mixed = lax.psum_scatter(terms, 'tensor', scatter_dimension=0, tiled=True)]
    all_gather x2 -> x0, waiting for transfers between devices: 72.7 us -> none  [the longest x1 42.1 us: per_device(): whole = lax.all_gather(tokens, 'tensor', axis=0, tiled=True)]
    ppermute x0 -> x16, waiting for transfers between devices: none -> 27.1 us  [swap(): return lax.ppermute(x, 'tensor', [(i, i ^ stage[i % 2]) for i in range(n)])]
    ppermute x0 -> x16, starting transfers between devices: none -> 14.1 us  [swap(): return lax.ppermute(x, 'tensor', [(i, i ^ stage[i % 2]) for i in range(n)])]
    dot_general x3, matrix products: 13 us -> 3.78 us  [the longest x1 1.26 us: per_device(): back = back + jnp.dot(d_up, up_weight, preferred_element_type=F32)]
    concatenate x0 -> x6, other arithmetic: none -> 5.16 us  [gather(): x = jnp.concatenate([x, swap(x, n, stage)], 0)]
    dot_general x3, matrix products: 14.5 us -> 10.7 us  [rows_by_weight(): lax.dot_general(left, weight, (((1,), (1,)), ((), ())), preferred_element...]
    unnamed x10 -> x20, local copies, waits for them, and re-layouts: 0.02 us -> 3.23 us
  transfers between devices with their start and end apart: 4 -> 16, of which waited for: 4 -> 12; matrix products, arithmetic and copies ran while one was open for 13% -> 35% of each run, Pallas kernels for 0% -> 0%
where the time goes in v1:
time: 83.1 us; the launch traced here: 82.7 us
  matrix products  30.1 us (36%)
  waiting for transfers between devices  27.1 us (33%)
  starting transfers between devices  14.1 us (17%)
  other arithmetic  6.78 us (8%)
  local copies, waits for them, and re-layouts  3.52 us (4%)
  between operations  1.02 us (1%)
    ppermute x16, waiting for transfers between devices, swap(): return lax.ppermute(x, 'tensor', [(i, i ^ stage[i % 2]) for i in range(n)])  27.1 us
    dot_general x3, matrix products, over_tokens(): lax.dot_general(left, right, (((0,), (0,)), ((), ())), preferred_element_...  15.6 us
    ppermute x16, starting transfers between devices, swap(): return lax.ppermute(x, 'tensor', [(i, i ^ stage[i % 2]) for i in range(n)])  14.1 us
    dot_general x3, matrix products, rows_by_weight(): lax.dot_general(left, weight, (((1,), (1,)), ((), ())), preferred_element...  10.7 us
    concatenate x6, other arithmetic, gather(): x = jnp.concatenate([x, swap(x, n, stage)], 0)  5.16 us
    unnamed x20, local copies, waits for them, and re-layouts  3.23 us
  transfers between devices with their start and end apart: 16, of which 12 were waited for; matrix products, arithmetic and copies ran while one was open for 35% of the time, Pallas kernels for 0%

profile of v1, /device:TPU:0, one launch (start us, length us, event | category | flops | bytes accessed | tf_op | source)
XLA Modules:
  0.0 82.7 jit_solution(1093676205663052222)
XLA Ops:
  0.6 4.1 %collective-permute-start = (bf16[8,4096]{1,0:T(8,128)(2,1)}, bf16[8,4096]{1,0:T(8,128)(2,1)S(1)}, u32[]{:S(2)}, u32[]{:S(2)}) collective-permute-start(bf16[8,4096]{1,0:T(8,128)(2,1)} %param.5), channel_id=1, source_target_pairs={{0,8},{1,3},{2,10},{3,1},{4,12},{5,7},{6,14},{7,5},{8,0},{9,11},{1... | collective-permute-start | bytes 196616 | tf_op jit(solution)/shard_map/ppermute | solution.py:29
  7.2 0.8 %pad_maximum_fusion.4 = bf16[16,4096]{1,0:T(8,128)(2,1)S(1)} fusion(bf16[8,4096]{1,0:T(8,128)(2,1)S(1)} %collective-permute-done, bf16[8,4096]{1,0:T(8,128)(2,1)} %param.5), kind=kLoop, calls=%fused_computation.31 | loop fusion | flops 262144 | bytes 262144 | tf_op jit(solution)/shard_map/concatenate | solution.py:34
  8.0 2.6 %collective-permute-start.1 = (bf16[16,4096]{1,0:T(8,128)(2,1)S(1)}, bf16[16,4096]{1,0:T(8,128)(2,1)S(1)}, u32[]{:S(2)}, u32[]{:S(2)}) collective-permute-start(bf16[16,4096]{1,0:T(8,128)(2,1)S(1)} %pad_maximum_fusion.4), channel_id=1, source_target_pairs={{0,4},{1,9},{2,6},{3,11},{4,0},{5,13},{6,2},{7,15},{8,12},{9,1},{1... | collective-permute-start | bytes 393224 | tf_op jit(solution)/shard_map/ppermute | solution.py:29
  10.6 2.1 %collective-permute-done.8 = bf16[8,4096]{1,0:T(8,128)(2,1)S(1)} collective-permute-done((bf16[8,4096]{1,0:T(8,128)(2,1)}, bf16[8,4096]{1,0:T(8,128)(2,1)S(1)}, u32[]{:S(2)}, u32[]{:S(2)}) %collective-permute-start.8) | collective-permute-done | bytes 65568 | tf_op jit(solution)/shard_map/ppermute | solution.py:29
  13.7 1.3 %collective-permute-done.1 = bf16[16,4096]{1,0:T(8,128)(2,1)S(1)} collective-permute-done((bf16[16,4096]{1,0:T(8,128)(2,1)S(1)}, bf16[16,4096]{1,0:T(8,128)(2,1)S(1)}, u32[]{:S(2)}, u32[]{:S(2)}) %collective-permute-start.1) | collective-permute-done | bytes 131104 | tf_op jit(solution)/shard_map/ppermute | solution.py:29
  15.0 0.9 %pad_maximum_fusion.2 = bf16[32,4096]{1,0:T(8,128)(2,1)S(1)} fusion(bf16[16,4096]{1,0:T(8,128)(2,1)S(1)} %collective-permute-done.1, bf16[8,4096]{1,0:T(8,128)(2,1)S(1)} %collective-permute-done, bf16[8,4096]{1,0:T(8,128)(2,1)} %param.5), kind=kLoop, calls=%fused_computation.23 | loop fusion | flops 786432 | bytes 524288 | tf_op jit(solution)/shard_map/concatenate | solution.py:34
  15.8 1.6 %collective-permute-start.2 = (bf16[32,4096]{1,0:T(8,128)(2,1)S(1)}, bf16[32,4096]{1,0:T(8,128)(2,1)S(1)}, u32[]{:S(2)}, u32[]{:S(2)}) collective-permute-start(bf16[32,4096]{1,0:T(8,128)(2,1)S(1)} %pad_maximum_fusion.2), channel_id=1, source_target_pairs={{0,2},{1,5},{2,0},{3,7},{4,6},{5,1},{6,4},{7,3},{8,10},{9,13},{10,... | collective-permute-start | bytes 786440 | tf_op jit(solution)/shard_map/ppermute | solution.py:29
  17.4 2.6 %collective-permute-done.9 = bf16[16,4096]{1,0:T(8,128)(2,1)S(1)} collective-permute-done((bf16[16,4096]{1,0:T(8,128)(2,1)S(1)}, bf16[16,4096]{1,0:T(8,128)(2,1)S(1)}, u32[]{:S(2)}, u32[]{:S(2)}) %collective-permute-start.9) | collective-permute-done | bytes 131104 | tf_op jit(solution)/shard_map/ppermute | solution.py:29
  20.0 0.9 %pad_maximum_fusion.3 = bf16[32,4096]{1,0:T(8,128)(2,1)S(1)} fusion(bf16[16,4096]{1,0:T(8,128)(2,1)S(1)} %collective-permute-done.9, bf16[8,4096]{1,0:T(8,128)(2,1)S(1)} %collective-permute-done.8, bf16[8,4096]{1,0:T(8,128)(2,1)} %param.9), kind=kLoop, calls=%fused_computation.24 | loop fusion | flops 786432 | bytes 524288 | tf_op jit(solution)/shard_map/concatenate | solution.py:34
  21.0 1.3 %collective-permute-done.2 = bf16[32,4096]{1,0:T(8,128)(2,1)S(1)} collective-permute-done((bf16[32,4096]{1,0:T(8,128)(2,1)S(1)}, bf16[32,4096]{1,0:T(8,128)(2,1)S(1)}, u32[]{:S(2)}, u32[]{:S(2)}) %collective-permute-start.2) | collective-permute-done | bytes 262176 | tf_op jit(solution)/shard_map/ppermute | solution.py:29
  22.3 0.9 %pad_maximum_fusion = bf16[64,4096]{1,0:T(8,128)(2,1)S(1)} fusion(bf16[32,4096]{1,0:T(8,128)(2,1)S(1)} %collective-permute-done.2, bf16[16,4096]{1,0:T(8,128)(2,1)S(1)} %collective-permute-done.1, bf16[8,4096]{1,0:T(8,128)(2,1)S(1)} %collective-permute-done, bf16[8,4096]{1,0:T(8,128)(2,1)} %param.5), kind=kLoop, calls=%fused_computation.12 | loop fusion | flops 2097152 | bytes 1048576 | tf_op jit(solution)/shard_map/concatenate | solution.py:34
  23.2 4.1 %collective-permute-done.10 = bf16[32,4096]{1,0:T(8,128)(2,1)S(1)} collective-permute-done((bf16[32,4096]{1,0:T(8,128)(2,1)S(1)}, bf16[32,4096]{1,0:T(8,128)(2,1)S(1)}, u32[]{:S(2)}, u32[]{:S(2)}) %collective-permute-start.10) | collective-permute-done | bytes 262176 | tf_op jit(solution)/shard_map/ppermute | solution.py:29
  27.3 0.9 %pad_maximum_fusion.1 = bf16[64,4096]{1,0:T(8,128)(2,1)S(1)} fusion(bf16[32,4096]{1,0:T(8,128)(2,1)S(1)} %collective-permute-done.10, bf16[16,4096]{1,0:T(8,128)(2,1)S(1)} %collective-permute-done.9, bf16[8,4096]{1,0:T(8,128)(2,1)S(1)} %collective-permute-done.8, bf16[8,4096]{1,0:T(8,128)(2,1)} %param.9), kind=kLoop, calls=%fused_computation.13 | loop fusion | flops 2097152 | bytes 1048576 | tf_op jit(solution)/shard_map/concatenate | solution.py:34
  28.4 5.8 %fusion.4 = f32[128,896]{1,0:T(8,128)S(1)} fusion(bf16[128,4096]{1,0:T(8,128)(2,1)S(1)} %constant_dynamic-update-slice_fusion, bf16[896,4096]{1,0:T(8,128)(2,1)} %param.7), kind=kOutput, calls=%fused_computation.44 | convolution fusion | flops 939524096 | bytes 8847360 | tf_op jit(solution)/shard_map/dot_general | solution.py:12
  34.2 2.5 %fusion.3 = f32[128,896]{1,0:T(8,128)S(1)} fusion(bf16[128,4096]{1,0:T(8,128)(2,1)S(1)} %constant_dynamic-update-slice_fusion, bf16[896,4096]{1,0:T(8,128)(2,1)S(1)} %bitcast.19), kind=kOutput, calls=%fused_computation.43 | convolution fusion | flops 939524096 | bytes 8847360 | tf_op jit(solution)/shard_map/dot_general | solution.py:12
  36.8 2.5 %multiply_convert_fusion = (bf16[128,896]{1,0:T(8,128)(2,1)S(1)}, bf16[128,896]{1,0:T(8,128)(2,1)S(1)}, bf16[128,896]{1,0:T(8,128)(2,1)S(1)}) fusion(f32[128,896]{1,0:T(8,128)S(1)} %fusion.3, f32[128,896]{1,0:T(8,128)S(1)} %fusion.4, bf16[128,4096]{1,0:T(8,128)(2,1)S(1)} %constant_dynamic-update-slice_fusion.5, bf16[896,4096]{1,0:T(8,128)(2,1)S(1)} %bitcast.23), kind=kOutput, calls=%fused_computation.14 | convolution fusion | flops 941244416 | bytes 9994240 | tf_op jit(solution)/shard_map/dot_general | solution.py:12
  39.3 1.3 %fusion.5 = f32[128,4096]{1,0:T(8,128)S(1)} fusion(bf16[128,896]{1,0:T(8,128)(2,1)S(1)} %get-tuple-element.7, bf16[896,4096]{1,0:T(8,128)(2,1)S(1)} %bitcast.23), kind=kOutput, calls=%fused_computation.45 | convolution fusion | flops 939524096 | bytes 9666560 | tf_op jit(solution)/shard_map/dot_general | solution.py:56
  40.6 5.1 %convolution_convert_fusion = bf16[896,4096]{1,0:T(8,128)(2,1)} fusion(bf16[128,896]{1,0:T(8,128)(2,1)S(1)} %get-tuple-element.7, bf16[128,4096]{1,0:T(8,128)(2,1)S(1)} %constant_dynamic-update-slice_fusion.5), kind=kOutput, calls=%fused_computation | convolution fusion | flops 943194112 | bytes 8617984 | tf_op jit(solution)/shard_map/dot_general | solution.py:16
  46.3 1.3 %fusion.6 = f32[128,4096]{1,0:T(8,128)S(1)} fusion(bf16[128,896]{1,0:T(8,128)(2,1)S(1)} %get-tuple-element.6, bf16[896,4096]{1,0:T(8,128)(2,1)S(1)} %bitcast.19), kind=kOutput, calls=%fused_computation.46 | convolution fusion | flops 939524096 | bytes 9666560 | tf_op jit(solution)/shard_map/dot_general | solution.py:60
  47.9 1.1 %slice-done.3 = s8[3145728]{0:T(1024)(128)(4,1)S(1)} async-done(((s8[7340032]{0:T(1024)(128)(4,1)}), s8[3145728]{0:T(1024)(128)(4,1)S(1)}, s32[]{:S(2)}) %slice-start.3) | async-done | bytes 3145752
  49.0 1.3 %convolution_add_fusion = f32[128,4096]{1,0:T(8,128)S(1)} fusion(f32[128,4096]{1,0:T(8,128)S(1)} %fusion.6, bf16[128,896]{1,0:T(8,128)(2,1)S(1)} %get-tuple-element.5, bf16[896,4096]{1,0:T(8,128)(2,1)S(1)} %bitcast.21), kind=kOutput, calls=%fused_computation.3 | convolution fusion | flops 940048384 | bytes 11763712 | tf_op jit(solution)/shard_map/dot_general | solution.py:61
  50.3 5.3 %convolution_convert_fusion.1 = bf16[896,4096]{1,0:T(8,128)(2,1)} fusion(bf16[128,896]{1,0:T(8,128)(2,1)S(1)} %get-tuple-element.5, bf16[128,4096]{1,0:T(8,128)(2,1)S(1)} %constant_dynamic-update-slice_fusion), kind=kOutput, calls=%fused_computation.1 | convolution fusion | flops 943194112 | bytes 8617984 | tf_op jit(solution)/shard_map/dot_general | solution.py:16
  56.2 5.1 %convolution_convert_fusion.2 = bf16[896,4096]{1,0:T(8,128)(2,1)} fusion(bf16[128,896]{1,0:T(8,128)(2,1)S(1)} %get-tuple-element.6, bf16[128,4096]{1,0:T(8,128)(2,1)S(1)} %constant_dynamic-update-slice_fusion), kind=kOutput, calls=%fused_computation.2 | convolution fusion | flops 943194112 | bytes 8617984 | tf_op jit(solution)/shard_map/dot_general | solution.py:16
  61.7 2.1 %collective-permute-start.13 = (bf16[32,4096]{1,0:T(8,128)(2,1)S(1)}, bf16[32,4096]{1,0:T(8,128)(2,1)S(1)}, u32[]{:S(2)}, u32[]{:S(2)}) collective-permute-start(bf16[32,4096]{1,0:T(8,128)(2,1)S(1)} %slice.110), channel_id=1, source_target_pairs={{0,2},{1,5},{2,0},{3,7},{4,6},{5,1},{6,4},{7,3},{8,10},{9,13},{10,... | collective-permute-start | bytes 786440 | tf_op jit(solution)/shard_map/ppermute | solution.py:29
  63.7 4.1 %collective-permute-done.5 = bf16[32,4096]{1,0:T(8,128)(2,1)S(1)} collective-permute-done((bf16[32,4096]{1,0:T(8,128)(2,1)S(1)}, bf16[32,4096]{1,0:T(8,128)(2,1)S(1)}, u32[]{:S(2)}, u32[]{:S(2)}) %collective-permute-start.5) | collective-permute-done | bytes 262176 | tf_op jit(solution)/shard_map/ppermute | solution.py:29
  68.0 2.7 %collective-permute-done.13 = bf16[32,4096]{1,0:T(8,128)(2,1)S(1)} collective-permute-done((bf16[32,4096]{1,0:T(8,128)(2,1)S(1)}, bf16[32,4096]{1,0:T(8,128)(2,1)S(1)}, u32[]{:S(2)}, u32[]{:S(2)}) %collective-permute-start.13) | collective-permute-done | bytes 262176 | tf_op jit(solution)/shard_map/ppermute | solution.py:29
  70.9 3.5 %collective-permute-done.6 = bf16[16,4096]{1,0:T(8,128)(2,1)S(1)} collective-permute-done((bf16[16,4096]{1,0:T(8,128)(2,1)S(1)}, bf16[16,4096]{1,0:T(8,128)(2,1)S(1)}, u32[]{:S(2)}, u32[]{:S(2)}) %collective-permute-start.6) | collective-permute-done | bytes 131104 | tf_op jit(solution)/shard_map/ppermute | solution.py:29
  74.4 1.0 %collective-permute-start.7 = (bf16[8,4096]{1,0:T(8,128)(2,1)S(1)}, bf16[8,4096]{1,0:T(8,128)(2,1)S(1)}, u32[]{:S(2)}, u32[]{:S(2)}) collective-permute-start(bf16[8,4096]{1,0:T(8,128)(2,1)S(1)} %slice.115), channel_id=1, source_target_pairs={{0,8},{1,3},{2,10},{3,1},{4,12},{5,7},{6,14},{7,5},{8,0},{9,11},{1... | collective-permute-start | bytes 196616 | tf_op jit(solution)/shard_map/ppermute | solution.py:29
  75.4 1.4 %collective-permute-done.14 = bf16[16,4096]{1,0:T(8,128)(2,1)S(1)} collective-permute-done((bf16[16,4096]{1,0:T(8,128)(2,1)S(1)}, bf16[16,4096]{1,0:T(8,128)(2,1)S(1)}, u32[]{:S(2)}, u32[]{:S(2)}) %collective-permute-start.14) | collective-permute-done | bytes 131104 | tf_op jit(solution)/shard_map/ppermute | solution.py:29
  76.8 1.2 %collective-permute-start.15 = (bf16[8,4096]{1,0:T(8,128)(2,1)S(1)}, bf16[8,4096]{1,0:T(8,128)(2,1)S(1)}, u32[]{:S(2)}, u32[]{:S(2)}) collective-permute-start(bf16[8,4096]{1,0:T(8,128)(2,1)S(1)} %slice.114), channel_id=1, source_target_pairs={{0,8},{1,3},{2,10},{3,1},{4,12},{5,7},{6,14},{7,5},{8,0},{9,11},{1... | collective-permute-start | bytes 196616 | tf_op jit(solution)/shard_map/ppermute | solution.py:29
  78.0 2.3 %collective-permute-done.7 = bf16[8,4096]{1,0:T(8,128)(2,1)S(1)} collective-permute-done((bf16[8,4096]{1,0:T(8,128)(2,1)S(1)}, bf16[8,4096]{1,0:T(8,128)(2,1)S(1)}, u32[]{:S(2)}, u32[]{:S(2)}) %collective-permute-start.7) | collective-permute-done | bytes 65568 | tf_op jit(solution)/shard_map/ppermute | solution.py:29
  81.0 1.0 %collective-permute-done.15 = bf16[8,4096]{1,0:T(8,128)(2,1)S(1)} collective-permute-done((bf16[8,4096]{1,0:T(8,128)(2,1)S(1)}, bf16[8,4096]{1,0:T(8,128)(2,1)S(1)}, u32[]{:S(2)}, u32[]{:S(2)}) %collective-permute-start.15) | collective-permute-done | bytes 65568 | tf_op jit(solution)/shard_map/ppermute | solution.py:29
  (56 shorter events, 7.1 us)
Async XLA Ops:
  0.6 6.6 %collective-permute-start = (bf16[8,4096]{1,0:T(8,128)(2,1)}, bf16[8,4096]{1,0:T(8,128)(2,1)S(1)}, u32[]{:S(2)}, u32[]{:S(2)}) collective-permute-start(bf16[8,4096]{1,0:T(8,128)(2,1)} %param.5), channel_id=1, source_target_pairs={{0,8},{1,3},{2,10},{3,1},{4,12},{5,7},{6,14},{7,5},{8,0},{9,11},{1... | collective-permute-start | bytes 196616 | tf_op jit(solution)/shard_map/ppermute | solution.py:29
  4.7 8.0 %collective-permute-start.8 = (bf16[8,4096]{1,0:T(8,128)(2,1)}, bf16[8,4096]{1,0:T(8,128)(2,1)S(1)}, u32[]{:S(2)}, u32[]{:S(2)}) collective-permute-start(bf16[8,4096]{1,0:T(8,128)(2,1)} %param.9), channel_id=1, source_target_pairs={{0,8},{1,3},{2,10},{3,1},{4,12},{5,7},{6,14},{7,5},{8,0},{9,11},{1... | collective-permute-start | bytes 196616 | tf_op jit(solution)/shard_map/ppermute | solution.py:29
  8.0 6.9 %collective-permute-start.1 = (bf16[16,4096]{1,0:T(8,128)(2,1)S(1)}, bf16[16,4096]{1,0:T(8,128)(2,1)S(1)}, u32[]{:S(2)}, u32[]{:S(2)}) collective-permute-start(bf16[16,4096]{1,0:T(8,128)(2,1)S(1)} %pad_maximum_fusion.4), channel_id=1, source_target_pairs={{0,4},{1,9},{2,6},{3,11},{4,0},{5,13},{6,2},{7,15},{8,12},{9,1},{1... | collective-permute-start | bytes 393224 | tf_op jit(solution)/shard_map/ppermute | solution.py:29
  13.6 6.4 %collective-permute-start.9 = (bf16[16,4096]{1,0:T(8,128)(2,1)S(1)}, bf16[16,4096]{1,0:T(8,128)(2,1)S(1)}, u32[]{:S(2)}, u32[]{:S(2)}) collective-permute-start(bf16[16,4096]{1,0:T(8,128)(2,1)S(1)} %pad_maximum_fusion.5), channel_id=1, source_target_pairs={{0,4},{1,9},{2,6},{3,11},{4,0},{5,13},{6,2},{7,15},{8,12},{9,1},{1... | collective-permute-start | bytes 393224 | tf_op jit(solution)/shard_map/ppermute | solution.py:29
  13.7 20.5 %slice-start = ((s8[7340032]{0:T(1024)(128)(4,1)}), s8[4194304]{0:T(1024)(128)(4,1)S(1)}, s32[]{:S(2)}) async-start(s8[7340032]{0:T(1024)(128)(4,1)} %bitcast.18), calls=%async_computation | async-start | bytes 8388608
  15.8 6.4 %collective-permute-start.2 = (bf16[32,4096]{1,0:T(8,128)(2,1)S(1)}, bf16[32,4096]{1,0:T(8,128)(2,1)S(1)}, u32[]{:S(2)}, u32[]{:S(2)}) collective-permute-start(bf16[32,4096]{1,0:T(8,128)(2,1)S(1)} %pad_maximum_fusion.2), channel_id=1, source_target_pairs={{0,2},{1,5},{2,0},{3,7},{4,6},{5,1},{6,4},{7,3},{8,10},{9,13},{10,... | collective-permute-start | bytes 786440 | tf_op jit(solution)/shard_map/ppermute | solution.py:29
  20.9 6.4 %collective-permute-start.10 = (bf16[32,4096]{1,0:T(8,128)(2,1)S(1)}, bf16[32,4096]{1,0:T(8,128)(2,1)S(1)}, u32[]{:S(2)}, u32[]{:S(2)}) collective-permute-start(bf16[32,4096]{1,0:T(8,128)(2,1)S(1)} %pad_maximum_fusion.3), channel_id=1, source_target_pairs={{0,2},{1,5},{2,0},{3,7},{4,6},{5,1},{6,4},{7,3},{8,10},{9,13},{10,... | collective-permute-start | bytes 786440 | tf_op jit(solution)/shard_map/ppermute | solution.py:29
  23.2 5.2 %collective-permute-start.3 = (bf16[64,4096]{1,0:T(8,128)(2,1)S(1)}, bf16[64,4096]{1,0:T(8,128)(2,1)S(1)}, u32[]{:S(2)}, u32[]{:S(2)}) collective-permute-start(bf16[64,4096]{1,0:T(8,128)(2,1)S(1)} %pad_maximum_fusion), channel_id=1, source_target_pairs={{0,1},{1,0},{2,3},{3,2},{4,5},{5,4},{6,7},{7,6},{8,9},{9,8},{10,11... | collective-permute-start | bytes 1572872 | tf_op jit(solution)/shard_map/ppermute | solution.py:29
  28.2 8.5 %collective-permute-start.11 = (bf16[64,4096]{1,0:T(8,128)(2,1)S(1)}, bf16[64,4096]{1,0:T(8,128)(2,1)S(1)}, u32[]{:S(2)}, u32[]{:S(2)}) collective-permute-start(bf16[64,4096]{1,0:T(8,128)(2,1)S(1)} %pad_maximum_fusion.1), channel_id=1, source_target_pairs={{0,1},{1,0},{2,3},{3,2},{4,5},{5,4},{6,7},{7,6},{8,9},{9,8},{10,11... | collective-permute-start | bytes 1572872 | tf_op jit(solution)/shard_map/ppermute | solution.py:29
  28.4 5.8 %slice-start.1 = ((s8[7340032]{0:T(1024)(128)(4,1)}), s8[3145728]{0:T(1024)(128)(4,1)S(1)}, s32[]{:S(2)}) async-start(s8[7340032]{0:T(1024)(128)(4,1)} %bitcast.18), calls=%async_computation.1 | async-start | bytes 6291456
  28.4 8.3 %slice-start.4 = ((s8[7340032]{0:T(1024)(128)(4,1)}), s8[4194304]{0:T(1024)(128)(4,1)S(1)}, s32[]{:S(2)}) async-start(s8[7340032]{0:T(1024)(128)(4,1)} %bitcast.22), calls=%async_computation.4 | async-start | bytes 8388608
  34.2 2.5 %slice-start.5 = ((s8[7340032]{0:T(1024)(128)(4,1)}), s8[3145728]{0:T(1024)(128)(4,1)S(1)}, s32[]{:S(2)}) async-start(s8[7340032]{0:T(1024)(128)(4,1)} %bitcast.22), calls=%async_computation.5 | async-start | bytes 6291456
  45.7 2.2 %slice-start.2 = ((s8[7340032]{0:T(1024)(128)(4,1)}), s8[4194304]{0:T(1024)(128)(4,1)S(1)}, s32[]{:S(2)}) async-start(s8[7340032]{0:T(1024)(128)(4,1)} %bitcast.20), calls=%async_computation.2 | async-start | bytes 8388608
  45.8 15.5 %collective-permute-start.4 = (bf16[64,4096]{1,0:T(8,128)(2,1)S(1)}, bf16[64,4096]{1,0:T(8,128)(2,1)S(1)}, u32[]{:S(2)}, u32[]{:S(2)}) collective-permute-start(bf16[64,4096]{1,0:T(8,128)(2,1)S(1)} %slice.109), channel_id=1, source_target_pairs={{0,1},{1,0},{2,3},{3,2},{4,5},{5,4},{6,7},{7,6},{8,9},{9,8},{10,11... | collective-permute-start | bytes 1572872 | tf_op jit(solution)/shard_map/ppermute | solution.py:29
  46.3 2.7 %slice-start.3 = ((s8[7340032]{0:T(1024)(128)(4,1)}), s8[3145728]{0:T(1024)(128)(4,1)S(1)}, s32[]{:S(2)}) async-start(s8[7340032]{0:T(1024)(128)(4,1)} %bitcast.20), calls=%async_computation.3 | async-start | bytes 6291456
  55.7 5.8 %collective-permute-start.12 = (bf16[64,4096]{1,0:T(8,128)(2,1)S(1)}, bf16[64,4096]{1,0:T(8,128)(2,1)S(1)}, u32[]{:S(2)}, u32[]{:S(2)}) collective-permute-start(bf16[64,4096]{1,0:T(8,128)(2,1)S(1)} %slice.108), channel_id=1, source_target_pairs={{0,1},{1,0},{2,3},{3,2},{4,5},{5,4},{6,7},{7,6},{8,9},{9,8},{10,11... | collective-permute-start | bytes 1572872 | tf_op jit(solution)/shard_map/ppermute | solution.py:29
  61.4 6.4 %collective-permute-start.5 = (bf16[32,4096]{1,0:T(8,128)(2,1)S(1)}, bf16[32,4096]{1,0:T(8,128)(2,1)S(1)}, u32[]{:S(2)}, u32[]{:S(2)}) collective-permute-start(bf16[32,4096]{1,0:T(8,128)(2,1)S(1)} %slice.111), channel_id=1, source_target_pairs={{0,2},{1,5},{2,0},{3,7},{4,6},{5,1},{6,4},{7,3},{8,10},{9,13},{10,... | collective-permute-start | bytes 786440 | tf_op jit(solution)/shard_map/ppermute | solution.py:29
  61.7 9.0 %collective-permute-start.13 = (bf16[32,4096]{1,0:T(8,128)(2,1)S(1)}, bf16[32,4096]{1,0:T(8,128)(2,1)S(1)}, u32[]{:S(2)}, u32[]{:S(2)}) collective-permute-start(bf16[32,4096]{1,0:T(8,128)(2,1)S(1)} %slice.110), channel_id=1, source_target_pairs={{0,2},{1,5},{2,0},{3,7},{4,6},{5,1},{6,4},{7,3},{8,10},{9,13},{10,... | collective-permute-start | bytes 786440 | tf_op jit(solution)/shard_map/ppermute | solution.py:29
  68.0 6.4 %collective-permute-start.6 = (bf16[16,4096]{1,0:T(8,128)(2,1)S(1)}, bf16[16,4096]{1,0:T(8,128)(2,1)S(1)}, u32[]{:S(2)}, u32[]{:S(2)}) collective-permute-start(bf16[16,4096]{1,0:T(8,128)(2,1)S(1)} %slice.113), channel_id=1, source_target_pairs={{0,4},{1,9},{2,6},{3,11},{4,0},{5,13},{6,2},{7,15},{8,12},{9,1},{1... | collective-permute-start | bytes 393224 | tf_op jit(solution)/shard_map/ppermute | solution.py:29
  70.8 6.0 %collective-permute-start.14 = (bf16[16,4096]{1,0:T(8,128)(2,1)S(1)}, bf16[16,4096]{1,0:T(8,128)(2,1)S(1)}, u32[]{:S(2)}, u32[]{:S(2)}) collective-permute-start(bf16[16,4096]{1,0:T(8,128)(2,1)S(1)} %slice.112), channel_id=1, source_target_pairs={{0,4},{1,9},{2,6},{3,11},{4,0},{5,13},{6,2},{7,15},{8,12},{9,1},{1... | collective-permute-start | bytes 393224 | tf_op jit(solution)/shard_map/ppermute | solution.py:29
  74.4 5.9 %collective-permute-start.7 = (bf16[8,4096]{1,0:T(8,128)(2,1)S(1)}, bf16[8,4096]{1,0:T(8,128)(2,1)S(1)}, u32[]{:S(2)}, u32[]{:S(2)}) collective-permute-start(bf16[8,4096]{1,0:T(8,128)(2,1)S(1)} %slice.115), channel_id=1, source_target_pairs={{0,8},{1,3},{2,10},{3,1},{4,12},{5,7},{6,14},{7,5},{8,0},{9,11},{1... | collective-permute-start | bytes 196616 | tf_op jit(solution)/shard_map/ppermute | solution.py:29
  76.8 5.2 %collective-permute-start.15 = (bf16[8,4096]{1,0:T(8,128)(2,1)S(1)}, bf16[8,4096]{1,0:T(8,128)(2,1)S(1)}, u32[]{:S(2)}, u32[]{:S(2)}) collective-permute-start(bf16[8,4096]{1,0:T(8,128)(2,1)S(1)} %slice.114), channel_id=1, source_target_pairs={{0,8},{1,3},{2,10},{3,1},{4,12},{5,7},{6,14},{7,5},{8,0},{9,11},{1... | collective-permute-start | bytes 196616 | tf_op jit(solution)/shard_map/ppermute | solution.py:29

commit v2 on v1

v2 whole, which is shorter than its diff:
```python
import jax
import jax.numpy as jnp
from jax import lax
from jax.experimental import pallas as pl
from jax.experimental.pallas import tpu as pltpu
from jax.sharding import PartitionSpec as P

F32 = jnp.float32
BF16 = jnp.bfloat16
CORE = 1
CHUNK = 128


def rows_by_weight(left, weight):
    return lax.dot_general(left, weight, (((1,), (1,)), ((), ())), preferred_element_type=F32)


def over_tokens(left, right):
    return lax.dot_general(left, right, (((0,), (0,)), ((), ())), preferred_element_type=F32)


def fetch_kernel(weight, after, held, sem):
    del after
    copy = pltpu.make_async_copy(weight, held, sem)
    copy.start()
    copy.wait()


def fetch(weight, after):
    size = weight.size * weight.dtype.itemsize
    return pl.pallas_call(
        fetch_kernel,
        out_shape=pltpu.VMEM(weight.shape, weight.dtype),
        in_specs=[pl.BlockSpec(memory_space=pl.ANY)] * 2,
        out_specs=pl.BlockSpec(memory_space=pltpu.VMEM),
        scratch_shapes=[pltpu.SemaphoreType.DMA],
        compiler_params=pltpu.CompilerParams(vmem_limit_bytes=16 * 2**20),
        cost_estimate=pl.CostEstimate(flops=0, bytes_accessed=size, transcendentals=0),
    )(weight, after)


def stages(n):
    bits = []
    b = n // 2
    while b > 1:
        bits.append(b)
        b //= 2
    return [(e, o) for e, o in zip(bits, bits[-1:] + bits[:-1])] + [(CORE, CORE)]


def swap(x, n, stage):
    return lax.ppermute(x, "tensor", [(i, i ^ stage[i % 2]) for i in range(n)])


tie = lax.optimization_barrier


def join(own, got):
    return jnp.concatenate([own, got], 0)


def lower(x):
    return x[: x.shape[0] // 2]


def upper(x):
    return x[x.shape[0] // 2 :].astype(BF16)


def add(x, got):
    return lower(x) + got.astype(F32)


def gradient_kernel(left, right, out, held, sems):
    rows = left.shape[1]
    copies = []
    for k, at in enumerate(range(0, rows, CHUNK)):
        part = pl.ds(at, min(CHUNK, rows - at))
        held[part, :] = over_tokens(left[:, part], right[...]).astype(BF16)
        copies.append(pltpu.make_async_copy(held.at[part, :], out.at[part, :], sems.at[k]))
        copies[-1].start()
    for copy in copies:
        copy.wait()


def gradient(left, right):
    rows, width = left.shape[1], right.shape[1]
    return pl.pallas_call(
        gradient_kernel,
        out_shape=jax.ShapeDtypeStruct((rows, width), BF16),
        in_specs=[pl.BlockSpec(memory_space=pltpu.VMEM)] * 2,
        out_specs=pl.BlockSpec(memory_space=pl.ANY),
        scratch_shapes=[pltpu.VMEM((rows, width), BF16), pltpu.SemaphoreType.DMA((pl.cdiv(rows, CHUNK),))],
        compiler_params=pltpu.CompilerParams(vmem_limit_bytes=20 * 2**20),
        cost_estimate=pl.CostEstimate(
            flops=2 * rows * width * left.shape[0], bytes_accessed=2 * rows * width, transcendentals=0
        ),
    )(left, right)


def solution(mesh):
    n = mesh.shape["tensor"]
    there = stages(n)
    back = there[::-1]

    def per_device(tokens, gate_weight, up_weight, down_weight, cotangent):
        t, c = tokens, cotangent
        got, own_t, own_c = tie((swap(t, n, there[0]), fetch(t, t), fetch(c, c)))
        t, c = tie((join(own_t, got), own_c))
        first = True
        for k, (stage, late) in enumerate(zip(there[1:-1], there)):
            got_t, got_c = tie((swap(t, n, stage), swap(cotangent if first else c, n, late)))
            if k == 1:
                got_t, got_c, gate_weight = tie((got_t, got_c, fetch(gate_weight, t)))
            t, c = tie((join(t, got_t), join(c, got_c)))
            first = False
        got_c = swap(c, n, there[-2])
        up_weight = fetch(up_weight, t)
        t = join(t, swap(t, n, there[-1]))
        gate = rows_by_weight(t, gate_weight)
        up = rows_by_weight(t, up_weight)
        sig = jax.nn.sigmoid(gate)
        act = gate * sig
        hidden = (act * up).astype(BF16)
        hidden, got_c = tie((hidden, got_c))
        c = join(c, got_c)
        out, got_c = tie((jnp.dot(hidden, down_weight, preferred_element_type=F32), swap(c, n, there[-1])))
        c = join(c, got_c)

        got = swap(upper(out), n, back[0])
        d_hidden = rows_by_weight(c, down_weight)
        d_gate = (d_hidden * up * sig * (1.0 + gate * (1.0 - sig))).astype(BF16)
        d_up = (d_hidden * act).astype(BF16)
        got, d_gate, d_up = tie((got, d_gate, d_up))
        out = add(out, got)
        out, d_gate, d_up = tie((out, d_gate, d_up))

        got_out = swap(upper(out), n, back[1])
        terms = jnp.dot(d_gate, gate_weight, preferred_element_type=F32)
        terms = terms + jnp.dot(d_up, up_weight, preferred_element_type=F32)
        jobs = [(hidden, c), (d_gate, t), (d_up, t)]
        made = []
        for k, stage in enumerate(back):
            terms, job = tie((terms, jobs[k] if k < 3 else ()))
            got = swap(upper(terms), n, stage)
            work = (gradient(*job),) if job else ()
            got, work, got_out = tie((got, work, got_out))
            made += work
            terms = add(terms, got)
            if k + 1 < len(back):
                out = add(out, got_out)
            got_out = ()
            if k + 2 < len(back):
                terms, out = tie((terms, out))
                got_out = swap(upper(out), n, back[k + 2])
        down_grad, gate_grad, up_grad = made
        return (out.astype(BF16), terms.astype(BF16), gate_grad, up_grad, down_grad)

    rows = P(("groups", "tensor"), None)
    weights = P("tensor", None)
    grads = P("tensor", "groups")
    return jax.shard_map(
        per_device,
        mesh=mesh,
        in_specs=(rows, weights, weights, weights, rows),
        out_specs=(rows, rows, grads, grads, grads),
        check_vma=False,
    )
```

time: 83.1 us -> 65.8 us (0.79)
  matrix products: 30.1 us -> 11.2 us
  waiting for transfers between devices: 27.1 us -> 11.2 us
  Pallas kernels: 0 us -> 11.6 us
  starting transfers between devices: 14.1 us -> 22.7 us
  other arithmetic: 6.78 us -> 1.81 us
  local copies, waits for them, and re-layouts: 3.52 us -> 5.96 us
    ppermute x16, waiting for transfers between devices: 27.1 us -> 11.2 us  [swap(): return lax.ppermute(x, 'tensor', [(i, i ^ stage[i % 2]) for i in range(n)])]
    dot_general x5 -> x2, matrix products: 18.2 us -> 2.56 us  [the longest x1 1.3 us: per_device(): terms = terms + jnp.dot(d_up, up_weight, preferred_element_type=F32)]
    pallas_call x0 -> x7, Pallas kernels: none -> 11.6 us  [the longest x3 10.5 us: gradient(): pl.pallas_call(gradient_kernel, out_shape=jax.ShapeDtypeStruct((rows, wid...]
    ppermute x16, starting transfers between devices: 14.1 us -> 22.7 us  [swap(): return lax.ppermute(x, 'tensor', [(i, i ^ stage[i % 2]) for i in range(n)])]
    concatenate x6, other arithmetic: 5.16 us -> 0.13 us  [join(): return jnp.concatenate([own, got], 0)]
    dot_general x3, matrix products: 10.7 us -> 7.42 us  [rows_by_weight(): lax.dot_general(left, weight, (((1,), (1,)), ((), ())), preferred_element...]
    unnamed x20 -> x15, local copies, waits for them, and re-layouts: 3.23 us -> 5.67 us
  transfers between devices with their start and end apart: 16 -> 16, of which waited for: 12 -> 7; matrix products, arithmetic and copies ran while one was open for 35% -> 15% of each run, Pallas kernels for 0% -> 18%
where the time goes in v2:
time: 65.8 us; the launch traced here: 65.5 us
  starting transfers between devices  22.7 us (34%)
  Pallas kernels  11.6 us (18%)
  waiting for transfers between devices  11.2 us (17%)
  matrix products  11.2 us (17%)
  local copies, waits for them, and re-layouts  5.96 us (9%)
  other arithmetic  1.81 us (3%)
  between operations  0.98 us (1%)
    ppermute x16, starting transfers between devices, swap(): return lax.ppermute(x, 'tensor', [(i, i ^ stage[i % 2]) for i in range(n)])  22.7 us
    ppermute x16, waiting for transfers between devices, swap(): return lax.ppermute(x, 'tensor', [(i, i ^ stage[i % 2]) for i in range(n)])  11.2 us
    pallas_call x3, Pallas kernels, gradient(): pl.pallas_call(gradient_kernel, out_shape=jax.ShapeDtypeStruct((rows, wid...  10.5 us
    dot_general x3, matrix products, rows_by_weight(): lax.dot_general(left, weight, (((1,), (1,)), ((), ())), preferred_element...  7.42 us
    unnamed x15, local copies, waits for them, and re-layouts  5.67 us
  transfers between devices with their start and end apart: 16, of which 7 were waited for; matrix products, arithmetic and copies ran while one was open for 15% of the time, Pallas kernels for 18%

profile of v2, /device:TPU:0, one launch (start us, length us, event | category | flops | bytes accessed | tf_op | source)
XLA Modules:
  0.0 65.5 jit_solution(2555356411084333694)
XLA Ops:
  0.6 4.1 %collective-permute-start = (bf16[8,4096]{1,0:T(8,128)(2,1)}, bf16[8,4096]{1,0:T(8,128)(2,1)S(1)}, u32[]{:S(2)}, u32[]{:S(2)}) collective-permute-start(bf16[8,4096]{1,0:T(8,128)(2,1)} %after.2), channel_id=1, source_target_pairs={{0,8},{1,3},{2,10},{3,1},{4,12},{5,7},{6,14},{7,5},{8,0},{9,11},{1... | collective-permute-start | bytes 196616 | tf_op jit(solution)/shard_map/ppermute | solution.py:52
  4.7 0.9 %copy-done.2 = bf16[8,4096]{1,0:T(8,128)(2,1)S(1)} copy-done((bf16[8,4096]{1,0:T(8,128)(2,1)S(1)}, bf16[8,4096]{1,0:T(8,128)(2,1)}, u32[]{:S(2)}) %copy-start.2) | copy-done | bytes 65560
  5.7 0.8 %copy-done.3 = bf16[8,4096]{1,0:T(8,128)(2,1)S(1)} copy-done((bf16[8,4096]{1,0:T(8,128)(2,1)S(1)}, bf16[8,4096]{1,0:T(8,128)(2,1)}, u32[]{:S(2)}) %copy-start.3) | copy-done | bytes 65560
  6.6 0.6 collective-permute-done
  7.2 2.0 %collective-permute-start.1 = (bf16[16,4096]{1,0:T(8,128)(2,1)S(1)}, bf16[16,4096]{1,0:T(8,128)(2,1)S(1)}, u32[]{:S(2)}, u32[]{:S(2)}) collective-permute-start(bf16[16,4096]{1,0:T(8,128)(2,1)S(1)} %pad_maximum_fusion.4), channel_id=1, source_target_pairs={{0,4},{1,9},{2,6},{3,11},{4,0},{5,13},{6,2},{7,15},{8,12},{9,1},{1... | collective-permute-start | bytes 393224 | tf_op jit(solution)/shard_map/ppermute | solution.py:52
  9.2 3.2 %collective-permute-start.2 = (bf16[8,4096]{1,0:T(8,128)(2,1)S(1)}, bf16[8,4096]{1,0:T(8,128)(2,1)S(1)}, u32[]{:S(2)}, u32[]{:S(2)}) collective-permute-start(bf16[8,4096]{1,0:T(8,128)(2,1)S(1)} %copy-done.3), channel_id=1, source_target_pairs={{0,8},{1,3},{2,10},{3,1},{4,12},{5,7},{6,14},{7,5},{8,0},{9,11},{1... | collective-permute-start | bytes 196616 | tf_op jit(solution)/shard_map/ppermute | solution.py:52
  12.4 2.4 %collective-permute-done.2 = bf16[8,4096]{1,0:T(8,128)(2,1)S(1)} collective-permute-done((bf16[8,4096]{1,0:T(8,128)(2,1)S(1)}, bf16[8,4096]{1,0:T(8,128)(2,1)S(1)}, u32[]{:S(2)}, u32[]{:S(2)}) %collective-permute-start.2) | collective-permute-done | bytes 65568 | tf_op jit(solution)/shard_map/ppermute | solution.py:52
  14.8 1.6 %collective-permute-start.3 = (bf16[32,4096]{1,0:T(8,128)(2,1)S(1)}, bf16[32,4096]{1,0:T(8,128)(2,1)S(1)}, u32[]{:S(2)}, u32[]{:S(2)}) collective-permute-start(bf16[32,4096]{1,0:T(8,128)(2,1)S(1)} %pad_maximum_fusion.2.after), channel_id=1, source_target_pairs={{0,2},{1,5},{2,0},{3,7},{4,6},{5,1},{6,4},{7,3},{8,10},{9,13},{10,... | collective-permute-start | bytes 786440 | tf_op jit(solution)/shard_map/ppermute | solution.py:52
  16.4 1.2 %collective-permute-start.4 = (bf16[16,4096]{1,0:T(8,128)(2,1)S(1)}, bf16[16,4096]{1,0:T(8,128)(2,1)S(1)}, u32[]{:S(2)}, u32[]{:S(2)}) collective-permute-start(bf16[16,4096]{1,0:T(8,128)(2,1)S(1)} %pad_maximum_fusion.5), channel_id=1, source_target_pairs={{0,4},{1,9},{2,6},{3,11},{4,0},{5,13},{6,2},{7,15},{8,12},{9,1},{1... | collective-permute-start | bytes 393224 | tf_op jit(solution)/shard_map/ppermute | solution.py:52
  17.6 3.1 %copy-done = bf16[896,4096]{1,0:T(8,128)(2,1)S(1)} copy-done((bf16[896,4096]{1,0:T(8,128)(2,1)S(1)}, bf16[896,4096]{1,0:T(8,128)(2,1)}, u32[]{:S(2)}) %copy-start) | copy-done | bytes 7340056
  21.5 1.5 %collective-permute-start.6 = (bf16[32,4096]{1,0:T(8,128)(2,1)S(1)}, bf16[32,4096]{1,0:T(8,128)(2,1)S(1)}, u32[]{:S(2)}, u32[]{:S(2)}) collective-permute-start(bf16[32,4096]{1,0:T(8,128)(2,1)S(1)} %pad_maximum_fusion.3), channel_id=1, source_target_pairs={{0,2},{1,5},{2,0},{3,7},{4,6},{5,1},{6,4},{7,3},{8,10},{9,13},{10,... | collective-permute-start | bytes 786440 | tf_op jit(solution)/shard_map/ppermute | solution.py:52
  23.0 0.8 %copy-done.1 = bf16[896,4096]{1,0:T(8,128)(2,1)S(1)} copy-done((bf16[896,4096]{1,0:T(8,128)(2,1)S(1)}, bf16[896,4096]{1,0:T(8,128)(2,1)}, u32[]{:S(2)}) %copy-start.1) | copy-done | bytes 7340056
  24.4 2.5 %fusion.2 = f32[128,896]{1,0:T(8,128)S(1)} fusion(bf16[128,4096]{1,0:T(8,128)(2,1)S(1)} %constant_dynamic-update-slice_fusion.right, bf16[896,4096]{1,0:T(8,128)(2,1)S(1)} %shard_map.94), kind=kOutput, calls=%fused_computation.34 | convolution fusion | flops 939524096 | bytes 8847360 | tf_op jit(solution)/shard_map/dot_general | solution.py:15
  26.9 2.4 %multiply_convert_fusion.2 = (bf16[128,896]{1,0:T(8,128)(2,1)S(1)}, f32[128,896]{1,0:T(8,128)S(1)}) fusion(f32[128,896]{1,0:T(8,128)S(1)} %fusion.2, bf16[128,4096]{1,0:T(8,128)(2,1)S(1)} %constant_dynamic-update-slice_fusion.right, bf16[896,4096]{1,0:T(8,128)(2,1)S(1)} %shard_map.95), kind=kOutput, calls=%fused_computation.13 | convolution fusion | flops 940212224 | bytes 9535488 | tf_op jit(solution)/shard_map/dot_general | solution.py:15
  29.6 1.3 %fusion.3 = f32[128,4096]{1,0:T(8,128)S(1)} fusion(bf16[128,896]{1,0:T(8,128)(2,1)S(1)} %get-tuple-element.79.left, bf16[896,4096]{1,0:T(8,128)(2,1)S(1)} %bitcast.13), kind=kOutput, calls=%fused_computation.35 | convolution fusion | flops 939524096 | bytes 9666560 | tf_op jit(solution)/shard_map/dot_general | solution.py:127
  30.8 0.6 collective-permute-done.7
  31.7 2.5 %multiply_convert_fusion = (bf16[128,896]{1,0:T(8,128)(2,1)S(1)}, bf16[128,896]{1,0:T(8,128)(2,1)S(1)}) fusion(f32[128,896]{1,0:T(8,128)S(1)} %fusion.2, f32[128,896]{1,0:T(8,128)S(1)} %get-tuple-element.104, bf16[128,4096]{1,0:T(8,128)(2,1)S(1)} %constant_dynamic-update-slice_fusion.2.right, bf16[896,4096]{1,0:T(8,128)(2,1)S(1)} %bitcast.13), kind=kOutput, calls=%fused_computation.11 | convolution fusion | flops 941015040 | bytes 9764864 | tf_op jit(solution)/shard_map/dot_general | solution.py:15
  34.3 1.3 %fusion.4 = f32[128,4096]{1,0:T(8,128)S(1)} fusion(bf16[128,896]{1,0:T(8,128)(2,1)S(1)} %get-tuple-element.86.left, bf16[896,4096]{1,0:T(8,128)(2,1)S(1)} %shard_map.94), kind=kOutput, calls=%fused_computation.36 | convolution fusion | flops 939524096 | bytes 9666560 | tf_op jit(solution)/shard_map/dot_general | solution.py:139
  35.6 1.3 %convolution_add_fusion = f32[128,4096]{1,0:T(8,128)S(1)} fusion(f32[128,4096]{1,0:T(8,128)S(1)} %fusion.4, bf16[128,896]{1,0:T(8,128)(2,1)S(1)} %get-tuple-element.94.left, bf16[896,4096]{1,0:T(8,128)(2,1)S(1)} %shard_map.95), kind=kOutput, calls=%fused_computation | convolution fusion | flops 940048384 | bytes 11763712 | tf_op jit(solution)/shard_map/dot_general | solution.py:140
  37.4 0.6 collective-permute-start.10
  38.0 3.5 %shard_map.96 = bf16[896,4096]{1,0:T(8,128)(2,1)} custom-call(bf16[128,896]{1,0:T(8,128)(2,1)S(1)} %get-tuple-element.79.left, bf16[128,4096]{1,0:T(8,128)(2,1)S(1)} %constant_dynamic-update-slice_fusion.2.right), custom_call_target="tpu_custom_call" | custom-call | flops 939524096 | bytes 7340032 | tf_op jit(solution)/shard_map/pallas_call | solution.py:88
  41.5 2.4 %collective-permute-done.10 = bf16[32,4096]{1,0:T(8,128)(2,1)S(1)} collective-permute-done((bf16[32,4096]{1,0:T(8,128)(2,1)S(1)}, bf16[32,4096]{1,0:T(8,128)(2,1)S(1)}, u32[]{:S(2)}, u32[]{:S(2)}) %collective-permute-start.10) | collective-permute-done | bytes 262176 | tf_op jit(solution)/shard_map/ppermute | solution.py:52
  44.1 0.6 collective-permute-start.11
  44.7 1.2 %collective-permute-start.12 = (bf16[16,4096]{1,0:T(8,128)(2,1)S(1)}, bf16[16,4096]{1,0:T(8,128)(2,1)S(1)}, u32[]{:S(2)}, u32[]{:S(2)}) collective-permute-start(bf16[16,4096]{1,0:T(8,128)(2,1)S(1)} %slice.104), channel_id=1, source_target_pairs={{0,4},{1,9},{2,6},{3,11},{4,0},{5,13},{6,2},{7,15},{8,12},{9,1},{1... | collective-permute-start | bytes 393224 | tf_op jit(solution)/shard_map/ppermute | solution.py:52
  45.9 3.5 %shard_map.97 = bf16[896,4096]{1,0:T(8,128)(2,1)} custom-call(bf16[128,896]{1,0:T(8,128)(2,1)S(1)} %get-tuple-element.86.left, bf16[128,4096]{1,0:T(8,128)(2,1)S(1)} %constant_dynamic-update-slice_fusion.right), custom_call_target="tpu_custom_call" | custom-call | flops 939524096 | bytes 7340032 | tf_op jit(solution)/shard_map/pallas_call | solution.py:88
  49.4 2.2 %collective-permute-done.12 = bf16[16,4096]{1,0:T(8,128)(2,1)S(1)} collective-permute-done((bf16[16,4096]{1,0:T(8,128)(2,1)S(1)}, bf16[16,4096]{1,0:T(8,128)(2,1)S(1)}, u32[]{:S(2)}, u32[]{:S(2)}) %collective-permute-start.12) | collective-permute-done | bytes 131104 | tf_op jit(solution)/shard_map/ppermute | solution.py:52
  52.4 3.7 %collective-permute-start.14 = (bf16[8,4096]{1,0:T(8,128)(2,1)S(1)}, bf16[8,4096]{1,0:T(8,128)(2,1)S(1)}, u32[]{:S(2)}, u32[]{:S(2)}) collective-permute-start(bf16[8,4096]{1,0:T(8,128)(2,1)S(1)} %slice.106), channel_id=1, source_target_pairs={{0,8},{1,3},{2,10},{3,1},{4,12},{5,7},{6,14},{7,5},{8,0},{9,11},{1... | collective-permute-start | bytes 196616 | tf_op jit(solution)/shard_map/ppermute | solution.py:52
  56.0 3.5 %shard_map.98 = bf16[896,4096]{1,0:T(8,128)(2,1)} custom-call(bf16[128,896]{1,0:T(8,128)(2,1)S(1)} %get-tuple-element.94.left, bf16[128,4096]{1,0:T(8,128)(2,1)S(1)} %constant_dynamic-update-slice_fusion.right), custom_call_target="tpu_custom_call" | custom-call | flops 939524096 | bytes 7340032 | tf_op jit(solution)/shard_map/pallas_call | solution.py:88
  59.6 1.8 %collective-permute-start.15 = (bf16[8,4096]{1,0:T(8,128)(2,1)S(1)}, bf16[8,4096]{1,0:T(8,128)(2,1)S(1)}, u32[]{:S(2)}, u32[]{:S(2)}) collective-permute-start(bf16[8,4096]{1,0:T(8,128)(2,1)S(1)} %slice.105), channel_id=1, source_target_pairs={{0,8},{1,3},{2,10},{3,1},{4,12},{5,7},{6,14},{7,5},{8,0},{9,11},{1... | collective-permute-start | bytes 196616 | tf_op jit(solution)/shard_map/ppermute | solution.py:52
  61.4 0.6 add_convert_fusion
  62.0 2.8 %collective-permute-done.15 = bf16[8,4096]{1,0:T(8,128)(2,1)S(1)} collective-permute-done((bf16[8,4096]{1,0:T(8,128)(2,1)S(1)}, bf16[8,4096]{1,0:T(8,128)(2,1)S(1)}, u32[]{:S(2)}, u32[]{:S(2)}) %collective-permute-start.15) | collective-permute-done | bytes 65568 | tf_op jit(solution)/shard_map/ppermute | solution.py:52
  64.8 0.6 fusion.1
  (53 shorter events, 3.6 us)
Async XLA Ops:
  0.6 6.6 %collective-permute-start = (bf16[8,4096]{1,0:T(8,128)(2,1)}, bf16[8,4096]{1,0:T(8,128)(2,1)S(1)}, u32[]{:S(2)}, u32[]{:S(2)}) collective-permute-start(bf16[8,4096]{1,0:T(8,128)(2,1)} %after.2), channel_id=1, source_target_pairs={{0,8},{1,3},{2,10},{3,1},{4,12},{5,7},{6,14},{7,5},{8,0},{9,11},{1... | collective-permute-start | bytes 196616 | tf_op jit(solution)/shard_map/ppermute | solution.py:52
  4.7 0.9 %copy-start.2 = (bf16[8,4096]{1,0:T(8,128)(2,1)S(1)}, bf16[8,4096]{1,0:T(8,128)(2,1)}, u32[]{:S(2)}) copy-start(bf16[8,4096]{1,0:T(8,128)(2,1)} %after.2) | copy-start | bytes 196612
  5.7 0.8 %copy-start.3 = (bf16[8,4096]{1,0:T(8,128)(2,1)S(1)}, bf16[8,4096]{1,0:T(8,128)(2,1)}, u32[]{:S(2)}) copy-start(bf16[8,4096]{1,0:T(8,128)(2,1)} %after.3) | copy-start | bytes 196612
  7.2 7.6 %collective-permute-start.1 = (bf16[16,4096]{1,0:T(8,128)(2,1)S(1)}, bf16[16,4096]{1,0:T(8,128)(2,1)S(1)}, u32[]{:S(2)}, u32[]{:S(2)}) collective-permute-start(bf16[16,4096]{1,0:T(8,128)(2,1)S(1)} %pad_maximum_fusion.4), channel_id=1, source_target_pairs={{0,4},{1,9},{2,6},{3,11},{4,0},{5,13},{6,2},{7,15},{8,12},{9,1},{1... | collective-permute-start | bytes 393224 | tf_op jit(solution)/shard_map/ppermute | solution.py:52
  9.2 5.6 %collective-permute-start.2 = (bf16[8,4096]{1,0:T(8,128)(2,1)S(1)}, bf16[8,4096]{1,0:T(8,128)(2,1)S(1)}, u32[]{:S(2)}, u32[]{:S(2)}) collective-permute-start(bf16[8,4096]{1,0:T(8,128)(2,1)S(1)} %copy-done.3), channel_id=1, source_target_pairs={{0,8},{1,3},{2,10},{3,1},{4,12},{5,7},{6,14},{7,5},{8,0},{9,11},{1... | collective-permute-start | bytes 196616 | tf_op jit(solution)/shard_map/ppermute | solution.py:52
  14.8 6.6 %collective-permute-start.3 = (bf16[32,4096]{1,0:T(8,128)(2,1)S(1)}, bf16[32,4096]{1,0:T(8,128)(2,1)S(1)}, u32[]{:S(2)}, u32[]{:S(2)}) collective-permute-start(bf16[32,4096]{1,0:T(8,128)(2,1)S(1)} %pad_maximum_fusion.2.after), channel_id=1, source_target_pairs={{0,2},{1,5},{2,0},{3,7},{4,6},{5,1},{6,4},{7,3},{8,10},{9,13},{10,... | collective-permute-start | bytes 786440 | tf_op jit(solution)/shard_map/ppermute | solution.py:52
  16.4 5.0 %collective-permute-start.4 = (bf16[16,4096]{1,0:T(8,128)(2,1)S(1)}, bf16[16,4096]{1,0:T(8,128)(2,1)S(1)}, u32[]{:S(2)}, u32[]{:S(2)}) collective-permute-start(bf16[16,4096]{1,0:T(8,128)(2,1)S(1)} %pad_maximum_fusion.5), channel_id=1, source_target_pairs={{0,4},{1,9},{2,6},{3,11},{4,0},{5,13},{6,2},{7,15},{8,12},{9,1},{1... | collective-permute-start | bytes 393224 | tf_op jit(solution)/shard_map/ppermute | solution.py:52
  17.6 3.1 %copy-start = (bf16[896,4096]{1,0:T(8,128)(2,1)S(1)}, bf16[896,4096]{1,0:T(8,128)(2,1)}, u32[]{:S(2)}) copy-start(bf16[896,4096]{1,0:T(8,128)(2,1)} %weight.6) | copy-start | bytes 22020100
  20.7 3.1 %copy-start.1 = (bf16[896,4096]{1,0:T(8,128)(2,1)S(1)}, bf16[896,4096]{1,0:T(8,128)(2,1)}, u32[]{:S(2)}) copy-start(bf16[896,4096]{1,0:T(8,128)(2,1)} %weight.7) | copy-start | bytes 22020100
  21.5 2.9 %collective-permute-start.5 = (bf16[64,4096]{1,0:T(8,128)(2,1)S(1)}, bf16[64,4096]{1,0:T(8,128)(2,1)S(1)}, u32[]{:S(2)}, u32[]{:S(2)}) collective-permute-start(bf16[64,4096]{1,0:T(8,128)(2,1)S(1)} %pad_maximum_fusion.after), channel_id=1, source_target_pairs={{0,1},{1,0},{2,3},{3,2},{4,5},{5,4},{6,7},{7,6},{8,9},{9,8},{10,11... | collective-permute-start | bytes 1572872 | tf_op jit(solution)/shard_map/ppermute | solution.py:52
  21.5 7.8 %collective-permute-start.6 = (bf16[32,4096]{1,0:T(8,128)(2,1)S(1)}, bf16[32,4096]{1,0:T(8,128)(2,1)S(1)}, u32[]{:S(2)}, u32[]{:S(2)}) collective-permute-start(bf16[32,4096]{1,0:T(8,128)(2,1)S(1)} %pad_maximum_fusion.3), channel_id=1, source_target_pairs={{0,2},{1,5},{2,0},{3,7},{4,6},{5,1},{6,4},{7,3},{8,10},{9,13},{10,... | collective-permute-start | bytes 786440 | tf_op jit(solution)/shard_map/ppermute | solution.py:52
  24.4 5.1 %slice-start = ((s8[7340032]{0:T(1024)(128)(4,1)}), s8[4194304]{0:T(1024)(128)(4,1)S(1)}, s32[]{:S(2)}) async-start(s8[7340032]{0:T(1024)(128)(4,1)} %bitcast.12), calls=%async_computation | async-start | bytes 8388608
  26.9 2.6 %slice-start.1 = ((s8[7340032]{0:T(1024)(128)(4,1)}), s8[3145728]{0:T(1024)(128)(4,1)S(1)}, s32[]{:S(2)}) async-start(s8[7340032]{0:T(1024)(128)(4,1)} %bitcast.12), calls=%async_computation.1 | async-start | bytes 6291456
  29.4 2.0 %collective-permute-start.7 = (bf16[64,4096]{1,0:T(8,128)(2,1)S(1)}, bf16[64,4096]{1,0:T(8,128)(2,1)S(1)}, u32[]{:S(2)}, u32[]{:S(2)}) collective-permute-start(bf16[64,4096]{1,0:T(8,128)(2,1)S(1)} %pad_maximum_fusion.1), channel_id=1, source_target_pairs={{0,1},{1,0},{2,3},{3,2},{4,5},{5,4},{6,7},{7,6},{8,9},{9,8},{10,11... | collective-permute-start | bytes 1572872 | tf_op jit(solution)/shard_map/ppermute | solution.py:52
  31.5 2.8 %collective-permute-start.8 = (bf16[64,4096]{1,0:T(8,128)(2,1)S(1)}, bf16[64,4096]{1,0:T(8,128)(2,1)S(1)}, u32[]{:S(2)}, u32[]{:S(2)}) collective-permute-start(bf16[64,4096]{1,0:T(8,128)(2,1)S(1)} %slice.100), channel_id=1, source_target_pairs={{0,1},{1,0},{2,3},{3,2},{4,5},{5,4},{6,7},{7,6},{8,9},{9,8},{10,11... | collective-permute-start | bytes 1572872 | tf_op jit(solution)/shard_map/ppermute | solution.py:52
  37.0 6.9 %collective-permute-start.9 = (bf16[64,4096]{1,0:T(8,128)(2,1)S(1)}, bf16[64,4096]{1,0:T(8,128)(2,1)S(1)}, u32[]{:S(2)}, u32[]{:S(2)}) collective-permute-start(bf16[64,4096]{1,0:T(8,128)(2,1)S(1)} %slice.99), channel_id=1, source_target_pairs={{0,1},{1,0},{2,3},{3,2},{4,5},{5,4},{6,7},{7,6},{8,9},{9,8},{10,11... | collective-permute-start | bytes 1572872 | tf_op jit(solution)/shard_map/ppermute | solution.py:52
  37.4 6.4 %collective-permute-start.10 = (bf16[32,4096]{1,0:T(8,128)(2,1)S(1)}, bf16[32,4096]{1,0:T(8,128)(2,1)S(1)}, u32[]{:S(2)}, u32[]{:S(2)}) collective-permute-start(bf16[32,4096]{1,0:T(8,128)(2,1)S(1)} %slice.102), channel_id=1, source_target_pairs={{0,2},{1,5},{2,0},{3,7},{4,6},{5,1},{6,4},{7,3},{8,10},{9,13},{10,... | collective-permute-start | bytes 786440 | tf_op jit(solution)/shard_map/ppermute | solution.py:52
  44.1 7.6 %collective-permute-start.11 = (bf16[32,4096]{1,0:T(8,128)(2,1)S(1)}, bf16[32,4096]{1,0:T(8,128)(2,1)S(1)}, u32[]{:S(2)}, u32[]{:S(2)}) collective-permute-start(bf16[32,4096]{1,0:T(8,128)(2,1)S(1)} %slice.101), channel_id=1, source_target_pairs={{0,2},{1,5},{2,0},{3,7},{4,6},{5,1},{6,4},{7,3},{8,10},{9,13},{10,... | collective-permute-start | bytes 786440 | tf_op jit(solution)/shard_map/ppermute | solution.py:52
  44.7 7.0 %collective-permute-start.12 = (bf16[16,4096]{1,0:T(8,128)(2,1)S(1)}, bf16[16,4096]{1,0:T(8,128)(2,1)S(1)}, u32[]{:S(2)}, u32[]{:S(2)}) collective-permute-start(bf16[16,4096]{1,0:T(8,128)(2,1)S(1)} %slice.104), channel_id=1, source_target_pairs={{0,4},{1,9},{2,6},{3,11},{4,0},{5,13},{6,2},{7,15},{8,12},{9,1},{1... | collective-permute-start | bytes 393224 | tf_op jit(solution)/shard_map/ppermute | solution.py:52
  51.8 7.8 %collective-permute-start.13 = (bf16[16,4096]{1,0:T(8,128)(2,1)S(1)}, bf16[16,4096]{1,0:T(8,128)(2,1)S(1)}, u32[]{:S(2)}, u32[]{:S(2)}) collective-permute-start(bf16[16,4096]{1,0:T(8,128)(2,1)S(1)} %slice.103), channel_id=1, source_target_pairs={{0,4},{1,9},{2,6},{3,11},{4,0},{5,13},{6,2},{7,15},{8,12},{9,1},{1... | collective-permute-start | bytes 393224 | tf_op jit(solution)/shard_map/ppermute | solution.py:52
  52.4 7.2 %collective-permute-start.14 = (bf16[8,4096]{1,0:T(8,128)(2,1)S(1)}, bf16[8,4096]{1,0:T(8,128)(2,1)S(1)}, u32[]{:S(2)}, u32[]{:S(2)}) collective-permute-start(bf16[8,4096]{1,0:T(8,128)(2,1)S(1)} %slice.106), channel_id=1, source_target_pairs={{0,8},{1,3},{2,10},{3,1},{4,12},{5,7},{6,14},{7,5},{8,0},{9,11},{1... | collective-permute-start | bytes 196616 | tf_op jit(solution)/shard_map/ppermute | solution.py:52
  59.6 5.2 %collective-permute-start.15 = (bf16[8,4096]{1,0:T(8,128)(2,1)S(1)}, bf16[8,4096]{1,0:T(8,128)(2,1)S(1)}, u32[]{:S(2)}, u32[]{:S(2)}) collective-permute-start(bf16[8,4096]{1,0:T(8,128)(2,1)S(1)} %slice.105), channel_id=1, source_target_pairs={{0,8},{1,3},{2,10},{3,1},{4,12},{5,7},{6,14},{7,5},{8,0},{9,11},{1... | collective-permute-start | bytes 196616 | tf_op jit(solution)/shard_map/ppermute | solution.py:52

commit v3 on v2

--- a/solution.py
+++ b/solution.py
@@ -135,24 +135,17 @@
         out = add(out, got)
         out, d_gate, d_up = tie((out, d_gate, d_up))
 
-        got_out = swap(upper(out), n, back[1])
         terms = jnp.dot(d_gate, gate_weight, preferred_element_type=F32)
         terms = terms + jnp.dot(d_up, up_weight, preferred_element_type=F32)
-        jobs = [(hidden, c), (d_gate, t), (d_up, t)]
+        terms = add(terms, swap(upper(terms), n, back[0]))
+        jobs = [((hidden, c), (d_gate, t)), ((d_up, t),)]
         made = []
-        for k, stage in enumerate(back):
-            terms, job = tie((terms, jobs[k] if k < 3 else ()))
-            got = swap(upper(terms), n, stage)
-            work = (gradient(*job),) if job else ()
-            got, work, got_out = tie((got, work, got_out))
+        for k in range(1, len(back)):
+            terms, job = tie((terms, jobs[k - 1] if k <= 2 else ()))
+            sent = jnp.stack([upper(terms), upper(out)])
+            got, work = tie((swap(sent, n, back[k]), tuple(gradient(*one) for one in job)))
             made += work
-            terms = add(terms, got)
-            if k + 1 < len(back):
-                out = add(out, got_out)
-            got_out = ()
-            if k + 2 < len(back):
-                terms, out = tie((terms, out))
-                got_out = swap(upper(out), n, back[k + 2])
+            terms, out = tie((add(terms, got[0]), add(out, got[1])))
         down_grad, gate_grad, up_grad = made
         return (out.astype(BF16), terms.astype(BF16), gate_grad, up_grad, down_grad)
 

time: 65.8 us -> 63.7 us (0.968)
  starting transfers between devices: 22.7 us -> 18 us
  waiting for transfers between devices: 11.2 us -> 14.2 us
    ppermute x16 -> x13, starting transfers between devices: 22.7 us -> 18 us  [swap(): return lax.ppermute(x, 'tensor', [(i, i ^ stage[i % 2]) for i in range(n)])]
    ppermute x16 -> x13, waiting for transfers between devices: 11.2 us -> 14.2 us  [swap(): return lax.ppermute(x, 'tensor', [(i, i ^ stage[i % 2]) for i in range(n)])]
    convert_element_type x2 -> x0, other arithmetic: 1.29 us -> none  [per_device(): return (out.astype(BF16), terms.astype(BF16), gate_grad, up_grad, down_grad)]
  transfers between devices with their start and end apart: 16 -> 13, of which waited for: 7 -> 8; matrix products, arithmetic and copies ran while one was open for 15% -> 14% of each run, Pallas kernels for 18% -> 19%
where the time goes in v3:
time: 63.7 us; the launch traced here: 63.4 us
  starting transfers between devices  18 us (28%)
  waiting for transfers between devices  14.2 us (22%)
  Pallas kernels  11.8 us (19%)
  matrix products  11.2 us (18%)
  local copies, waits for them, and re-layouts  5.96 us (9%)
  other arithmetic  1.26 us (2%)
  between operations  0.99 us (2%)
    ppermute x13, starting transfers between devices, swap(): return lax.ppermute(x, 'tensor', [(i, i ^ stage[i % 2]) for i in range(n)])  18 us
    ppermute x13, waiting for transfers between devices, swap(): return lax.ppermute(x, 'tensor', [(i, i ^ stage[i % 2]) for i in range(n)])  14.2 us
    pallas_call x3, Pallas kernels, gradient(): pl.pallas_call(gradient_kernel, out_shape=jax.ShapeDtypeStruct((rows, wid...  10.7 us
    dot_general x3, matrix products, rows_by_weight(): lax.dot_general(left, weight, (((1,), (1,)), ((), ())), preferred_element...  7.42 us
    unnamed x15, local copies, waits for them, and re-layouts  5.67 us
    dot_general x1, matrix products, per_device(): terms = terms + jnp.dot(d_up, up_weight, preferred_element_type=F32)  1.3 us
  transfers between devices with their start and end apart: 13, of which 8 were waited for; matrix products, arithmetic and copies ran while one was open for 14% of the time, Pallas kernels for 19%

profile of v3, /device:TPU:0, one launch (start us, length us, event | category | flops | bytes accessed | tf_op | source)
XLA Modules:
  0.0 63.4 jit_solution(17444555339140114724)
XLA Ops:
  0.6 4.1 %collective-permute-start = (bf16[8,4096]{1,0:T(8,128)(2,1)}, bf16[8,4096]{1,0:T(8,128)(2,1)S(1)}, u32[]{:S(2)}, u32[]{:S(2)}) collective-permute-start(bf16[8,4096]{1,0:T(8,128)(2,1)} %after.2), channel_id=1, source_target_pairs={{0,8},{1,3},{2,10},{3,1},{4,12},{5,7},{6,14},{7,5},{8,0},{9,11},{1... | collective-permute-start | bytes 196616 | tf_op jit(solution)/shard_map/ppermute | solution.py:52
  4.7 0.9 %copy-done.2 = bf16[8,4096]{1,0:T(8,128)(2,1)S(1)} copy-done((bf16[8,4096]{1,0:T(8,128)(2,1)S(1)}, bf16[8,4096]{1,0:T(8,128)(2,1)}, u32[]{:S(2)}) %copy-start.2) | copy-done | bytes 65560
  5.7 0.8 %copy-done.3 = bf16[8,4096]{1,0:T(8,128)(2,1)S(1)} copy-done((bf16[8,4096]{1,0:T(8,128)(2,1)S(1)}, bf16[8,4096]{1,0:T(8,128)(2,1)}, u32[]{:S(2)}) %copy-start.3) | copy-done | bytes 65560
  6.6 0.6 collective-permute-done
  7.2 2.0 %collective-permute-start.1 = (bf16[16,4096]{1,0:T(8,128)(2,1)S(1)}, bf16[16,4096]{1,0:T(8,128)(2,1)S(1)}, u32[]{:S(2)}, u32[]{:S(2)}) collective-permute-start(bf16[16,4096]{1,0:T(8,128)(2,1)S(1)} %pad_maximum_fusion.6), channel_id=1, source_target_pairs={{0,4},{1,9},{2,6},{3,11},{4,0},{5,13},{6,2},{7,15},{8,12},{9,1},{1... | collective-permute-start | bytes 393224 | tf_op jit(solution)/shard_map/ppermute | solution.py:52
  9.2 3.2 %collective-permute-start.2 = (bf16[8,4096]{1,0:T(8,128)(2,1)S(1)}, bf16[8,4096]{1,0:T(8,128)(2,1)S(1)}, u32[]{:S(2)}, u32[]{:S(2)}) collective-permute-start(bf16[8,4096]{1,0:T(8,128)(2,1)S(1)} %copy-done.3), channel_id=1, source_target_pairs={{0,8},{1,3},{2,10},{3,1},{4,12},{5,7},{6,14},{7,5},{8,0},{9,11},{1... | collective-permute-start | bytes 196616 | tf_op jit(solution)/shard_map/ppermute | solution.py:52
  12.4 2.4 %collective-permute-done.2 = bf16[8,4096]{1,0:T(8,128)(2,1)S(1)} collective-permute-done((bf16[8,4096]{1,0:T(8,128)(2,1)S(1)}, bf16[8,4096]{1,0:T(8,128)(2,1)S(1)}, u32[]{:S(2)}, u32[]{:S(2)}) %collective-permute-start.2) | collective-permute-done | bytes 65568 | tf_op jit(solution)/shard_map/ppermute | solution.py:52
  14.8 1.6 %collective-permute-start.3 = (bf16[32,4096]{1,0:T(8,128)(2,1)S(1)}, bf16[32,4096]{1,0:T(8,128)(2,1)S(1)}, u32[]{:S(2)}, u32[]{:S(2)}) collective-permute-start(bf16[32,4096]{1,0:T(8,128)(2,1)S(1)} %pad_maximum_fusion.3.after), channel_id=1, source_target_pairs={{0,2},{1,5},{2,0},{3,7},{4,6},{5,1},{6,4},{7,3},{8,10},{9,13},{10,... | collective-permute-start | bytes 786440 | tf_op jit(solution)/shard_map/ppermute | solution.py:52
  16.4 1.2 %collective-permute-start.4 = (bf16[16,4096]{1,0:T(8,128)(2,1)S(1)}, bf16[16,4096]{1,0:T(8,128)(2,1)S(1)}, u32[]{:S(2)}, u32[]{:S(2)}) collective-permute-start(bf16[16,4096]{1,0:T(8,128)(2,1)S(1)} %pad_maximum_fusion.7), channel_id=1, source_target_pairs={{0,4},{1,9},{2,6},{3,11},{4,0},{5,13},{6,2},{7,15},{8,12},{9,1},{1... | collective-permute-start | bytes 393224 | tf_op jit(solution)/shard_map/ppermute | solution.py:52
  17.6 3.1 %copy-done = bf16[896,4096]{1,0:T(8,128)(2,1)S(1)} copy-done((bf16[896,4096]{1,0:T(8,128)(2,1)S(1)}, bf16[896,4096]{1,0:T(8,128)(2,1)}, u32[]{:S(2)}) %copy-start) | copy-done | bytes 7340056
  20.7 0.5 shard_map.94
  21.5 1.5 %collective-permute-start.6 = (bf16[32,4096]{1,0:T(8,128)(2,1)S(1)}, bf16[32,4096]{1,0:T(8,128)(2,1)S(1)}, u32[]{:S(2)}, u32[]{:S(2)}) collective-permute-start(bf16[32,4096]{1,0:T(8,128)(2,1)S(1)} %pad_maximum_fusion.4), channel_id=1, source_target_pairs={{0,2},{1,5},{2,0},{3,7},{4,6},{5,1},{6,4},{7,3},{8,10},{9,13},{10,... | collective-permute-start | bytes 786440 | tf_op jit(solution)/shard_map/ppermute | solution.py:52
  23.0 0.8 %copy-done.1 = bf16[896,4096]{1,0:T(8,128)(2,1)S(1)} copy-done((bf16[896,4096]{1,0:T(8,128)(2,1)S(1)}, bf16[896,4096]{1,0:T(8,128)(2,1)}, u32[]{:S(2)}) %copy-start.1) | copy-done | bytes 7340056
  23.8 0.5 shard_map.95
  24.4 2.5 %fusion.7 = f32[128,896]{1,0:T(8,128)S(1)} fusion(bf16[128,4096]{1,0:T(8,128)(2,1)S(1)} %constant_dynamic-update-slice_fusion.right, bf16[896,4096]{1,0:T(8,128)(2,1)S(1)} %shard_map.94), kind=kOutput, calls=%fused_computation.44 | convolution fusion | flops 939524096 | bytes 8847360 | tf_op jit(solution)/shard_map/dot_general | solution.py:15
  26.9 2.4 %multiply_convert_fusion.2 = (bf16[128,896]{1,0:T(8,128)(2,1)S(1)}, f32[128,896]{1,0:T(8,128)S(1)}) fusion(f32[128,896]{1,0:T(8,128)S(1)} %fusion.7, bf16[128,4096]{1,0:T(8,128)(2,1)S(1)} %constant_dynamic-update-slice_fusion.right, bf16[896,4096]{1,0:T(8,128)(2,1)S(1)} %shard_map.95), kind=kOutput, calls=%fused_computation.14 | convolution fusion | flops 940212224 | bytes 9535488 | tf_op jit(solution)/shard_map/dot_general | solution.py:15
  29.6 1.3 %fusion.8 = f32[128,4096]{1,0:T(8,128)S(1)} fusion(bf16[128,896]{1,0:T(8,128)(2,1)S(1)} %get-tuple-element.77.left, bf16[896,4096]{1,0:T(8,128)(2,1)S(1)} %bitcast.47), kind=kOutput, calls=%fused_computation.45 | convolution fusion | flops 939524096 | bytes 9666560 | tf_op jit(solution)/shard_map/dot_general | solution.py:127
  30.8 0.6 collective-permute-done.7
  31.7 2.5 %multiply_convert_fusion = (bf16[128,896]{1,0:T(8,128)(2,1)S(1)}, bf16[128,896]{1,0:T(8,128)(2,1)S(1)}) fusion(f32[128,896]{1,0:T(8,128)S(1)} %fusion.7, f32[128,896]{1,0:T(8,128)S(1)} %get-tuple-element.104, bf16[128,4096]{1,0:T(8,128)(2,1)S(1)} %constant_dynamic-update-slice_fusion.2.right, bf16[896,4096]{1,0:T(8,128)(2,1)S(1)} %bitcast.47), kind=kOutput, calls=%fused_computation.12 | convolution fusion | flops 941015040 | bytes 9764864 | tf_op jit(solution)/shard_map/dot_general | solution.py:15
  34.3 1.3 %fusion.9 = f32[128,4096]{1,0:T(8,128)S(1)} fusion(bf16[128,896]{1,0:T(8,128)(2,1)S(1)} %get-tuple-element.79.left, bf16[896,4096]{1,0:T(8,128)(2,1)S(1)} %shard_map.94), kind=kOutput, calls=%fused_computation.46 | convolution fusion | flops 939524096 | bytes 9666560 | tf_op jit(solution)/shard_map/dot_general | solution.py:138
  35.6 1.3 %convolution_add_fusion = f32[128,4096]{1,0:T(8,128)S(1)} fusion(f32[128,4096]{1,0:T(8,128)S(1)} %fusion.9, bf16[128,896]{1,0:T(8,128)(2,1)S(1)} %get-tuple-element.85.left, bf16[896,4096]{1,0:T(8,128)(2,1)S(1)} %shard_map.95), kind=kOutput, calls=%fused_computation | convolution fusion | flops 940048384 | bytes 11763712 | tf_op jit(solution)/shard_map/dot_general | solution.py:139
  37.4 1.5 %collective-permute-done.9 = bf16[64,4096]{1,0:T(8,128)(2,1)S(1)} collective-permute-done((bf16[64,4096]{1,0:T(8,128)(2,1)S(1)}, bf16[64,4096]{1,0:T(8,128)(2,1)S(1)}, u32[]{:S(2)}, u32[]{:S(2)}) %collective-permute-start.9) | collective-permute-done | bytes 524320 | tf_op jit(solution)/shard_map/ppermute | solution.py:52
  39.2 0.6 collective-permute-start.10
  39.7 3.5 %shard_map.97 = bf16[896,4096]{1,0:T(8,128)(2,1)} custom-call(bf16[128,896]{1,0:T(8,128)(2,1)S(1)} %get-tuple-element.79.left, bf16[128,4096]{1,0:T(8,128)(2,1)S(1)} %constant_dynamic-update-slice_fusion.right), custom_call_target="tpu_custom_call" | custom-call | flops 939524096 | bytes 7340032 | tf_op jit(solution)/shard_map/pallas_call | solution.py:88
  43.2 3.7 %shard_map.96 = bf16[896,4096]{1,0:T(8,128)(2,1)} custom-call(bf16[128,896]{1,0:T(8,128)(2,1)S(1)} %get-tuple-element.77.left, bf16[128,4096]{1,0:T(8,128)(2,1)S(1)} %constant_dynamic-update-slice_fusion.2.right), custom_call_target="tpu_custom_call" | custom-call | flops 939524096 | bytes 7340032 | tf_op jit(solution)/shard_map/pallas_call | solution.py:88
  47.0 1.4 %collective-permute-done.10 = bf16[2,32,4096]{2,1,0:T(8,128)(2,1)S(1)} collective-permute-done((bf16[2,32,4096]{2,1,0:T(8,128)(2,1)S(1)}, bf16[2,32,4096]{2,1,0:T(8,128)(2,1)S(1)}, u32[]{:S(2)}, u32[]{:S(2)}) %collective-permute-start.10) | collective-permute-done | bytes 524320 | tf_op jit(solution)/shard_map/ppermute | solution.py:52
  48.6 0.9 %collective-permute-start.11 = (bf16[2,16,4096]{2,1,0:T(8,128)(2,1)S(1)}, bf16[2,16,4096]{2,1,0:T(8,128)(2,1)S(1)}, u32[]{:S(2)}, u32[]{:S(2)}) collective-permute-start(bf16[2,16,4096]{2,1,0:T(8,128)(2,1)S(1)} %pad_maximum_fusion.5), channel_id=1, source_target_pairs={{0,4},{1,9},{2,6},{3,11},{4,0},{5,13},{6,2},{7,15},{8,12},{9,1},{1... | collective-permute-start | bytes 786440 | tf_op jit(solution)/shard_map/ppermute | solution.py:52
  49.5 3.5 %shard_map.98 = bf16[896,4096]{1,0:T(8,128)(2,1)} custom-call(bf16[128,896]{1,0:T(8,128)(2,1)S(1)} %get-tuple-element.85.left, bf16[128,4096]{1,0:T(8,128)(2,1)S(1)} %constant_dynamic-update-slice_fusion.right), custom_call_target="tpu_custom_call" | custom-call | flops 939524096 | bytes 7340032 | tf_op jit(solution)/shard_map/pallas_call | solution.py:88
  53.0 3.7 %collective-permute-done.11 = bf16[2,16,4096]{2,1,0:T(8,128)(2,1)S(1)} collective-permute-done((bf16[2,16,4096]{2,1,0:T(8,128)(2,1)S(1)}, bf16[2,16,4096]{2,1,0:T(8,128)(2,1)S(1)}, u32[]{:S(2)}, u32[]{:S(2)}) %collective-permute-start.11) | collective-permute-done | bytes 262176 | tf_op jit(solution)/shard_map/ppermute | solution.py:52
  56.8 2.2 %collective-permute-start.12 = (bf16[2,8,4096]{2,1,0:T(8,128)(2,1)S(1)}, bf16[2,8,4096]{2,1,0:T(8,128)(2,1)S(1)}, u32[]{:S(2)}, u32[]{:S(2)}) collective-permute-start(bf16[2,8,4096]{2,1,0:T(8,128)(2,1)S(1)} %pad_maximum_fusion.8), channel_id=1, source_target_pairs={{0,8},{1,3},{2,10},{3,1},{4,12},{5,7},{6,14},{7,5},{8,0},{9,11},{1... | collective-permute-start | bytes 393224 | tf_op jit(solution)/shard_map/ppermute | solution.py:52
  59.1 3.7 %collective-permute-done.12 = bf16[2,8,4096]{2,1,0:T(8,128)(2,1)S(1)} collective-permute-done((bf16[2,8,4096]{2,1,0:T(8,128)(2,1)S(1)}, bf16[2,8,4096]{2,1,0:T(8,128)(2,1)S(1)}, u32[]{:S(2)}, u32[]{:S(2)}) %collective-permute-start.12) | collective-permute-done | bytes 131104 | tf_op jit(solution)/shard_map/ppermute | solution.py:52
  62.8 0.7 %convert_add_fusion.5 = (bf16[8,4096]{1,0:T(8,128)(2,1)}, bf16[8,4096]{1,0:T(8,128)(2,1)}) fusion(f32[16,4096]{1,0:T(8,128)S(1)} %get-tuple-element.89, bf16[2,8,4096]{2,1,0:T(8,128)(2,1)S(1)} %collective-permute-done.12, f32[16,4096]{1,0:T(8,128)S(1)} %get-tuple-element.88), kind=kLoop, calls=%fused_computation.34 | loop fusion | flops 196608 | bytes 524288 | tf_op jit(solution)/shard_map/add | solution.py:71
  (46 shorter events, 2.1 us)
Async XLA Ops:
  0.6 6.6 %collective-permute-start = (bf16[8,4096]{1,0:T(8,128)(2,1)}, bf16[8,4096]{1,0:T(8,128)(2,1)S(1)}, u32[]{:S(2)}, u32[]{:S(2)}) collective-permute-start(bf16[8,4096]{1,0:T(8,128)(2,1)} %after.2), channel_id=1, source_target_pairs={{0,8},{1,3},{2,10},{3,1},{4,12},{5,7},{6,14},{7,5},{8,0},{9,11},{1... | collective-permute-start | bytes 196616 | tf_op jit(solution)/shard_map/ppermute | solution.py:52
  4.7 0.9 %copy-start.2 = (bf16[8,4096]{1,0:T(8,128)(2,1)S(1)}, bf16[8,4096]{1,0:T(8,128)(2,1)}, u32[]{:S(2)}) copy-start(bf16[8,4096]{1,0:T(8,128)(2,1)} %after.2) | copy-start | bytes 196612
  5.7 0.8 %copy-start.3 = (bf16[8,4096]{1,0:T(8,128)(2,1)S(1)}, bf16[8,4096]{1,0:T(8,128)(2,1)}, u32[]{:S(2)}) copy-start(bf16[8,4096]{1,0:T(8,128)(2,1)} %after.3) | copy-start | bytes 196612
  7.2 7.6 %collective-permute-start.1 = (bf16[16,4096]{1,0:T(8,128)(2,1)S(1)}, bf16[16,4096]{1,0:T(8,128)(2,1)S(1)}, u32[]{:S(2)}, u32[]{:S(2)}) collective-permute-start(bf16[16,4096]{1,0:T(8,128)(2,1)S(1)} %pad_maximum_fusion.6), channel_id=1, source_target_pairs={{0,4},{1,9},{2,6},{3,11},{4,0},{5,13},{6,2},{7,15},{8,12},{9,1},{1... | collective-permute-start | bytes 393224 | tf_op jit(solution)/shard_map/ppermute | solution.py:52
  9.2 5.6 %collective-permute-start.2 = (bf16[8,4096]{1,0:T(8,128)(2,1)S(1)}, bf16[8,4096]{1,0:T(8,128)(2,1)S(1)}, u32[]{:S(2)}, u32[]{:S(2)}) collective-permute-start(bf16[8,4096]{1,0:T(8,128)(2,1)S(1)} %copy-done.3), channel_id=1, source_target_pairs={{0,8},{1,3},{2,10},{3,1},{4,12},{5,7},{6,14},{7,5},{8,0},{9,11},{1... | collective-permute-start | bytes 196616 | tf_op jit(solution)/shard_map/ppermute | solution.py:52
  14.8 6.6 %collective-permute-start.3 = (bf16[32,4096]{1,0:T(8,128)(2,1)S(1)}, bf16[32,4096]{1,0:T(8,128)(2,1)S(1)}, u32[]{:S(2)}, u32[]{:S(2)}) collective-permute-start(bf16[32,4096]{1,0:T(8,128)(2,1)S(1)} %pad_maximum_fusion.3.after), channel_id=1, source_target_pairs={{0,2},{1,5},{2,0},{3,7},{4,6},{5,1},{6,4},{7,3},{8,10},{9,13},{10,... | collective-permute-start | bytes 786440 | tf_op jit(solution)/shard_map/ppermute | solution.py:52
  16.4 5.0 %collective-permute-start.4 = (bf16[16,4096]{1,0:T(8,128)(2,1)S(1)}, bf16[16,4096]{1,0:T(8,128)(2,1)S(1)}, u32[]{:S(2)}, u32[]{:S(2)}) collective-permute-start(bf16[16,4096]{1,0:T(8,128)(2,1)S(1)} %pad_maximum_fusion.7), channel_id=1, source_target_pairs={{0,4},{1,9},{2,6},{3,11},{4,0},{5,13},{6,2},{7,15},{8,12},{9,1},{1... | collective-permute-start | bytes 393224 | tf_op jit(solution)/shard_map/ppermute | solution.py:52
  17.6 3.1 %copy-start = (bf16[896,4096]{1,0:T(8,128)(2,1)S(1)}, bf16[896,4096]{1,0:T(8,128)(2,1)}, u32[]{:S(2)}) copy-start(bf16[896,4096]{1,0:T(8,128)(2,1)} %weight.6) | copy-start | bytes 22020100
  20.7 3.1 %copy-start.1 = (bf16[896,4096]{1,0:T(8,128)(2,1)S(1)}, bf16[896,4096]{1,0:T(8,128)(2,1)}, u32[]{:S(2)}) copy-start(bf16[896,4096]{1,0:T(8,128)(2,1)} %weight.7) | copy-start | bytes 22020100
  21.5 2.9 %collective-permute-start.5 = (bf16[64,4096]{1,0:T(8,128)(2,1)S(1)}, bf16[64,4096]{1,0:T(8,128)(2,1)S(1)}, u32[]{:S(2)}, u32[]{:S(2)}) collective-permute-start(bf16[64,4096]{1,0:T(8,128)(2,1)S(1)} %pad_maximum_fusion.after), channel_id=1, source_target_pairs={{0,1},{1,0},{2,3},{3,2},{4,5},{5,4},{6,7},{7,6},{8,9},{9,8},{10,11... | collective-permute-start | bytes 1572872 | tf_op jit(solution)/shard_map/ppermute | solution.py:52
  21.5 7.8 %collective-permute-start.6 = (bf16[32,4096]{1,0:T(8,128)(2,1)S(1)}, bf16[32,4096]{1,0:T(8,128)(2,1)S(1)}, u32[]{:S(2)}, u32[]{:S(2)}) collective-permute-start(bf16[32,4096]{1,0:T(8,128)(2,1)S(1)} %pad_maximum_fusion.4), channel_id=1, source_target_pairs={{0,2},{1,5},{2,0},{3,7},{4,6},{5,1},{6,4},{7,3},{8,10},{9,13},{10,... | collective-permute-start | bytes 786440 | tf_op jit(solution)/shard_map/ppermute | solution.py:52
  24.4 5.1 %slice-start = ((s8[7340032]{0:T(1024)(128)(4,1)}), s8[4194304]{0:T(1024)(128)(4,1)S(1)}, s32[]{:S(2)}) async-start(s8[7340032]{0:T(1024)(128)(4,1)} %bitcast.46), calls=%async_computation | async-start | bytes 8388608
  26.9 2.6 %slice-start.1 = ((s8[7340032]{0:T(1024)(128)(4,1)}), s8[3145728]{0:T(1024)(128)(4,1)S(1)}, s32[]{:S(2)}) async-start(s8[7340032]{0:T(1024)(128)(4,1)} %bitcast.46), calls=%async_computation.1 | async-start | bytes 6291456
  29.4 2.0 %collective-permute-start.7 = (bf16[64,4096]{1,0:T(8,128)(2,1)S(1)}, bf16[64,4096]{1,0:T(8,128)(2,1)S(1)}, u32[]{:S(2)}, u32[]{:S(2)}) collective-permute-start(bf16[64,4096]{1,0:T(8,128)(2,1)S(1)} %pad_maximum_fusion.1), channel_id=1, source_target_pairs={{0,1},{1,0},{2,3},{3,2},{4,5},{5,4},{6,7},{7,6},{8,9},{9,8},{10,11... | collective-permute-start | bytes 1572872 | tf_op jit(solution)/shard_map/ppermute | solution.py:52
  31.5 2.8 %collective-permute-start.8 = (bf16[64,4096]{1,0:T(8,128)(2,1)S(1)}, bf16[64,4096]{1,0:T(8,128)(2,1)S(1)}, u32[]{:S(2)}, u32[]{:S(2)}) collective-permute-start(bf16[64,4096]{1,0:T(8,128)(2,1)S(1)} %slice.147), channel_id=1, source_target_pairs={{0,1},{1,0},{2,3},{3,2},{4,5},{5,4},{6,7},{7,6},{8,9},{9,8},{10,11... | collective-permute-start | bytes 1572872 | tf_op jit(solution)/shard_map/ppermute | solution.py:52
  37.0 2.0 %collective-permute-start.9 = (bf16[64,4096]{1,0:T(8,128)(2,1)S(1)}, bf16[64,4096]{1,0:T(8,128)(2,1)S(1)}, u32[]{:S(2)}, u32[]{:S(2)}) collective-permute-start(bf16[64,4096]{1,0:T(8,128)(2,1)S(1)} %slice.146), channel_id=1, source_target_pairs={{0,1},{1,0},{2,3},{3,2},{4,5},{5,4},{6,7},{7,6},{8,9},{9,8},{10,11... | collective-permute-start | bytes 1572872 | tf_op jit(solution)/shard_map/ppermute | solution.py:52
  39.2 9.2 %collective-permute-start.10 = (bf16[2,32,4096]{2,1,0:T(8,128)(2,1)S(1)}, bf16[2,32,4096]{2,1,0:T(8,128)(2,1)S(1)}, u32[]{:S(2)}, u32[]{:S(2)}) collective-permute-start(bf16[2,32,4096]{2,1,0:T(8,128)(2,1)S(1)} %pad_maximum_fusion.2), channel_id=1, source_target_pairs={{0,2},{1,5},{2,0},{3,7},{4,6},{5,1},{6,4},{7,3},{8,10},{9,13},{10,... | collective-permute-start | bytes 1572872 | tf_op jit(solution)/shard_map/ppermute | solution.py:52
  48.6 8.1 %collective-permute-start.11 = (bf16[2,16,4096]{2,1,0:T(8,128)(2,1)S(1)}, bf16[2,16,4096]{2,1,0:T(8,128)(2,1)S(1)}, u32[]{:S(2)}, u32[]{:S(2)}) collective-permute-start(bf16[2,16,4096]{2,1,0:T(8,128)(2,1)S(1)} %pad_maximum_fusion.5), channel_id=1, source_target_pairs={{0,4},{1,9},{2,6},{3,11},{4,0},{5,13},{6,2},{7,15},{8,12},{9,1},{1... | collective-permute-start | bytes 786440 | tf_op jit(solution)/shard_map/ppermute | solution.py:52
  56.8 5.9 %collective-permute-start.12 = (bf16[2,8,4096]{2,1,0:T(8,128)(2,1)S(1)}, bf16[2,8,4096]{2,1,0:T(8,128)(2,1)S(1)}, u32[]{:S(2)}, u32[]{:S(2)}) collective-permute-start(bf16[2,8,4096]{2,1,0:T(8,128)(2,1)S(1)} %pad_maximum_fusion.8), channel_id=1, source_target_pairs={{0,8},{1,3},{2,10},{3,1},{4,12},{5,7},{6,14},{7,5},{8,0},{9,11},{1... | collective-permute-start | bytes 393224 | tf_op jit(solution)/shard_map/ppermute | solution.py:52

commit v4 on v3

--- a/solution.py
+++ b/solution.py
@@ -107,13 +107,15 @@
         t, c = tokens, cotangent
         got, own_t, own_c = tie((swap(t, n, there[0]), fetch(t, t), fetch(c, c)))
         t, c = tie((join(own_t, got), own_c))
-        first = True
         for k, (stage, late) in enumerate(zip(there[1:-1], there)):
-            got_t, got_c = tie((swap(t, n, stage), swap(cotangent if first else c, n, late)))
+            got_c = swap(c if k else cotangent, n, late)
+            got_t = swap(t, n, stage)
             if k == 1:
                 got_t, got_c, gate_weight = tie((got_t, got_c, fetch(gate_weight, t)))
-            t, c = tie((join(t, got_t), join(c, got_c)))
-            first = False
+            t = tie(join(t, got_t))
+            c = join(c, got_c)
+            if k:
+                t, c = tie((t, c))
         got_c = swap(c, n, there[-2])
         up_weight = fetch(up_weight, t)
         t = join(t, swap(t, n, there[-1]))

time: 63.7 us -> 61.7 us (0.969)
  waiting for transfers between devices: 14.2 us -> 9.16 us
  starting transfers between devices: 18 us -> 21.3 us
    ppermute x13, waiting for transfers between devices: 14.2 us -> 9.16 us  [swap(): return lax.ppermute(x, 'tensor', [(i, i ^ stage[i % 2]) for i in range(n)])]
    ppermute x13, starting transfers between devices: 18 us -> 21.3 us  [swap(): return lax.ppermute(x, 'tensor', [(i, i ^ stage[i % 2]) for i in range(n)])]
  transfers between devices with their start and end apart: 13 -> 13, of which waited for: 8 -> 9; matrix products, arithmetic and copies ran while one was open for 14% -> 15% of each run, Pallas kernels for 19% -> 19%
where the time goes in v4:
time: 61.7 us; the launch traced here: 61.2 us
  starting transfers between devices  21.3 us (35%)
  Pallas kernels  11.8 us (19%)
  matrix products  11.2 us (18%)
  waiting for transfers between devices  9.16 us (15%)
  local copies, waits for them, and re-layouts  5.47 us (9%)
  other arithmetic  1.24 us (2%)
  between operations  0.98 us (2%)
    ppermute x13, starting transfers between devices, swap(): return lax.ppermute(x, 'tensor', [(i, i ^ stage[i % 2]) for i in range(n)])  21.3 us
    pallas_call x3, Pallas kernels, gradient(): pl.pallas_call(gradient_kernel, out_shape=jax.ShapeDtypeStruct((rows, wid...  10.7 us
    ppermute x13, waiting for transfers between devices, swap(): return lax.ppermute(x, 'tensor', [(i, i ^ stage[i % 2]) for i in range(n)])  9.16 us
    dot_general x3, matrix products, rows_by_weight(): lax.dot_general(left, weight, (((1,), (1,)), ((), ())), preferred_element...  7.42 us
    unnamed x15, local copies, waits for them, and re-layouts  5.18 us
    dot_general x1, matrix products, per_device(): terms = jnp.dot(d_gate, gate_weight, preferred_element_type=F32)  1.3 us
    dot_general x1, matrix products, per_device(): jnp.dot(hidden, down_weight, preferred_element_type=F32)  1.26 us
    dot_general x1, matrix products, per_device(): terms = terms + jnp.dot(d_up, up_weight, preferred_element_type=F32)  1.26 us
  transfers between devices with their start and end apart: 13, of which 9 were waited for; matrix products, arithmetic and copies ran while one was open for 15% of the time, Pallas kernels for 19%

profile of v4, /device:TPU:0, one launch (start us, length us, event | category | flops | bytes accessed | tf_op | source)
XLA Modules:
  0.0 61.2 jit_solution(17932446740756271573)
XLA Ops:
  0.6 4.1 %collective-permute-start = (bf16[8,4096]{1,0:T(8,128)(2,1)}, bf16[8,4096]{1,0:T(8,128)(2,1)S(1)}, u32[]{:S(2)}, u32[]{:S(2)}) collective-permute-start(bf16[8,4096]{1,0:T(8,128)(2,1)} %after.2), channel_id=1, source_target_pairs={{0,8},{1,3},{2,10},{3,1},{4,12},{5,7},{6,14},{7,5},{8,0},{9,11},{1... | collective-permute-start | bytes 196616 | tf_op jit(solution)/shard_map/ppermute | solution.py:52
  4.7 0.9 %copy-done.2 = bf16[8,4096]{1,0:T(8,128)(2,1)S(1)} copy-done((bf16[8,4096]{1,0:T(8,128)(2,1)S(1)}, bf16[8,4096]{1,0:T(8,128)(2,1)}, u32[]{:S(2)}) %copy-start.2) | copy-done | bytes 65560
  5.7 0.8 %copy-done.3 = bf16[8,4096]{1,0:T(8,128)(2,1)S(1)} copy-done((bf16[8,4096]{1,0:T(8,128)(2,1)S(1)}, bf16[8,4096]{1,0:T(8,128)(2,1)}, u32[]{:S(2)}) %copy-start.3) | copy-done | bytes 65560
  6.6 0.6 collective-permute-done
  7.2 2.0 %collective-permute-start.1 = (bf16[16,4096]{1,0:T(8,128)(2,1)S(1)}, bf16[16,4096]{1,0:T(8,128)(2,1)S(1)}, u32[]{:S(2)}, u32[]{:S(2)}) collective-permute-start(bf16[16,4096]{1,0:T(8,128)(2,1)S(1)} %pad_maximum_fusion.6), channel_id=1, source_target_pairs={{0,4},{1,9},{2,6},{3,11},{4,0},{5,13},{6,2},{7,15},{8,12},{9,1},{1... | collective-permute-start | bytes 393224 | tf_op jit(solution)/shard_map/ppermute | solution.py:52
  9.2 3.2 %collective-permute-start.3 = (bf16[8,4096]{1,0:T(8,128)(2,1)S(1)}, bf16[8,4096]{1,0:T(8,128)(2,1)S(1)}, u32[]{:S(2)}, u32[]{:S(2)}) collective-permute-start(bf16[8,4096]{1,0:T(8,128)(2,1)S(1)} %copy-done.3), channel_id=1, source_target_pairs={{0,8},{1,3},{2,10},{3,1},{4,12},{5,7},{6,14},{7,5},{8,0},{9,11},{1... | collective-permute-start | bytes 196616 | tf_op jit(solution)/shard_map/ppermute | solution.py:52
  12.5 2.0 %collective-permute-start.2 = (bf16[32,4096]{1,0:T(8,128)(2,1)S(1)}, bf16[32,4096]{1,0:T(8,128)(2,1)S(1)}, u32[]{:S(2)}, u32[]{:S(2)}) collective-permute-start(bf16[32,4096]{1,0:T(8,128)(2,1)S(1)} %pad_maximum_fusion.3.after), channel_id=1, source_target_pairs={{0,2},{1,5},{2,0},{3,7},{4,6},{5,1},{6,4},{7,3},{8,10},{9,13},{10,... | collective-permute-start | bytes 786440 | tf_op jit(solution)/shard_map/ppermute | solution.py:52
  14.8 1.3 %collective-permute-start.4 = (bf16[16,4096]{1,0:T(8,128)(2,1)S(1)}, bf16[16,4096]{1,0:T(8,128)(2,1)S(1)}, u32[]{:S(2)}, u32[]{:S(2)}) collective-permute-start(bf16[16,4096]{1,0:T(8,128)(2,1)S(1)} %pad_maximum_fusion.7), channel_id=1, source_target_pairs={{0,4},{1,9},{2,6},{3,11},{4,0},{5,13},{6,2},{7,15},{8,12},{9,1},{1... | collective-permute-start | bytes 393224 | tf_op jit(solution)/shard_map/ppermute | solution.py:52
  16.1 3.1 %copy-done = bf16[896,4096]{1,0:T(8,128)(2,1)S(1)} copy-done((bf16[896,4096]{1,0:T(8,128)(2,1)S(1)}, bf16[896,4096]{1,0:T(8,128)(2,1)}, u32[]{:S(2)}) %copy-start) | copy-done | bytes 7340056
  19.2 0.5 shard_map.94
  19.7 0.5 collective-permute-done.4
  20.4 1.6 %collective-permute-start.6 = (bf16[32,4096]{1,0:T(8,128)(2,1)S(1)}, bf16[32,4096]{1,0:T(8,128)(2,1)S(1)}, u32[]{:S(2)}, u32[]{:S(2)}) collective-permute-start(bf16[32,4096]{1,0:T(8,128)(2,1)S(1)} %pad_maximum_fusion.4), channel_id=1, source_target_pairs={{0,2},{1,5},{2,0},{3,7},{4,6},{5,1},{6,4},{7,3},{8,10},{9,13},{10,... | collective-permute-start | bytes 786440 | tf_op jit(solution)/shard_map/ppermute | solution.py:52
  22.3 0.5 shard_map.95
  22.9 2.5 %fusion.7 = f32[128,896]{1,0:T(8,128)S(1)} fusion(bf16[128,4096]{1,0:T(8,128)(2,1)S(1)} %constant_dynamic-update-slice_fusion.right, bf16[896,4096]{1,0:T(8,128)(2,1)S(1)} %shard_map.94), kind=kOutput, calls=%fused_computation.44 | convolution fusion | flops 939524096 | bytes 8847360 | tf_op jit(solution)/shard_map/dot_general | solution.py:15
  25.4 2.4 %multiply_convert_fusion.2 = (bf16[128,896]{1,0:T(8,128)(2,1)S(1)}, f32[128,896]{1,0:T(8,128)S(1)}) fusion(f32[128,896]{1,0:T(8,128)S(1)} %fusion.7, bf16[128,4096]{1,0:T(8,128)(2,1)S(1)} %constant_dynamic-update-slice_fusion.right, bf16[896,4096]{1,0:T(8,128)(2,1)S(1)} %shard_map.95), kind=kOutput, calls=%fused_computation.14 | convolution fusion | flops 940212224 | bytes 9535488 | tf_op jit(solution)/shard_map/dot_general | solution.py:15
  28.0 1.3 %fusion.8 = f32[128,4096]{1,0:T(8,128)S(1)} fusion(bf16[128,896]{1,0:T(8,128)(2,1)S(1)} %get-tuple-element.65.left, bf16[896,4096]{1,0:T(8,128)(2,1)S(1)} %bitcast.47), kind=kOutput, calls=%fused_computation.45 | convolution fusion | flops 939524096 | bytes 9666560 | tf_op jit(solution)/shard_map/dot_general | solution.py:129
  29.3 0.6 collective-permute-done.7
  30.1 2.5 %multiply_convert_fusion = (bf16[128,896]{1,0:T(8,128)(2,1)S(1)}, bf16[128,896]{1,0:T(8,128)(2,1)S(1)}) fusion(f32[128,896]{1,0:T(8,128)S(1)} %fusion.7, f32[128,896]{1,0:T(8,128)S(1)} %get-tuple-element.92, bf16[128,4096]{1,0:T(8,128)(2,1)S(1)} %constant_dynamic-update-slice_fusion.2.right, bf16[896,4096]{1,0:T(8,128)(2,1)S(1)} %bitcast.47), kind=kOutput, calls=%fused_computation.12 | convolution fusion | flops 941015040 | bytes 9764864 | tf_op jit(solution)/shard_map/dot_general | solution.py:15
  32.8 1.3 %fusion.9 = f32[128,4096]{1,0:T(8,128)S(1)} fusion(bf16[128,896]{1,0:T(8,128)(2,1)S(1)} %get-tuple-element.73.left, bf16[896,4096]{1,0:T(8,128)(2,1)S(1)} %shard_map.95), kind=kOutput, calls=%fused_computation.46 | convolution fusion | flops 939524096 | bytes 9666560 | tf_op jit(solution)/shard_map/dot_general | solution.py:141
  34.0 1.3 %convolution_add_fusion = f32[128,4096]{1,0:T(8,128)S(1)} fusion(f32[128,4096]{1,0:T(8,128)S(1)} %fusion.9, bf16[128,896]{1,0:T(8,128)(2,1)S(1)} %get-tuple-element.67.left, bf16[896,4096]{1,0:T(8,128)(2,1)S(1)} %shard_map.94), kind=kOutput, calls=%fused_computation | convolution fusion | flops 940048384 | bytes 11763712 | tf_op jit(solution)/shard_map/dot_general | solution.py:140
  35.4 0.4 collective-permute-start.9
  35.9 1.5 %collective-permute-done.9 = bf16[64,4096]{1,0:T(8,128)(2,1)S(1)} collective-permute-done((bf16[64,4096]{1,0:T(8,128)(2,1)S(1)}, bf16[64,4096]{1,0:T(8,128)(2,1)S(1)}, u32[]{:S(2)}, u32[]{:S(2)}) %collective-permute-start.9) | collective-permute-done | bytes 524320 | tf_op jit(solution)/shard_map/ppermute | solution.py:52
  37.6 1.6 %collective-permute-start.10 = (bf16[2,32,4096]{2,1,0:T(8,128)(2,1)S(1)}, bf16[2,32,4096]{2,1,0:T(8,128)(2,1)S(1)}, u32[]{:S(2)}, u32[]{:S(2)}) collective-permute-start(bf16[2,32,4096]{2,1,0:T(8,128)(2,1)S(1)} %pad_maximum_fusion.2), channel_id=1, source_target_pairs={{0,2},{1,5},{2,0},{3,7},{4,6},{5,1},{6,4},{7,3},{8,10},{9,13},{10,... | collective-permute-start | bytes 1572872 | tf_op jit(solution)/shard_map/ppermute | solution.py:52
  39.2 3.5 %shard_map.97 = bf16[896,4096]{1,0:T(8,128)(2,1)} custom-call(bf16[128,896]{1,0:T(8,128)(2,1)S(1)} %get-tuple-element.67.left, bf16[128,4096]{1,0:T(8,128)(2,1)S(1)} %constant_dynamic-update-slice_fusion.right), custom_call_target="tpu_custom_call" | custom-call | flops 939524096 | bytes 7340032 | tf_op jit(solution)/shard_map/pallas_call | solution.py:88
  42.7 3.7 %shard_map.96 = bf16[896,4096]{1,0:T(8,128)(2,1)} custom-call(bf16[128,896]{1,0:T(8,128)(2,1)S(1)} %get-tuple-element.65.left, bf16[128,4096]{1,0:T(8,128)(2,1)S(1)} %constant_dynamic-update-slice_fusion.2.right), custom_call_target="tpu_custom_call" | custom-call | flops 939524096 | bytes 7340032 | tf_op jit(solution)/shard_map/pallas_call | solution.py:88
  46.4 0.4 collective-permute-done.10
  47.0 1.0 %collective-permute-start.11 = (bf16[2,16,4096]{2,1,0:T(8,128)(2,1)S(1)}, bf16[2,16,4096]{2,1,0:T(8,128)(2,1)S(1)}, u32[]{:S(2)}, u32[]{:S(2)}) collective-permute-start(bf16[2,16,4096]{2,1,0:T(8,128)(2,1)S(1)} %pad_maximum_fusion.5), channel_id=1, source_target_pairs={{0,4},{1,9},{2,6},{3,11},{4,0},{5,13},{6,2},{7,15},{8,12},{9,1},{1... | collective-permute-start | bytes 786440 | tf_op jit(solution)/shard_map/ppermute | solution.py:52
  48.0 3.5 %shard_map.98 = bf16[896,4096]{1,0:T(8,128)(2,1)} custom-call(bf16[128,896]{1,0:T(8,128)(2,1)S(1)} %get-tuple-element.73.left, bf16[128,4096]{1,0:T(8,128)(2,1)S(1)} %constant_dynamic-update-slice_fusion.right), custom_call_target="tpu_custom_call" | custom-call | flops 939524096 | bytes 7340032 | tf_op jit(solution)/shard_map/pallas_call | solution.py:88
  51.5 2.1 %collective-permute-done.11 = bf16[2,16,4096]{2,1,0:T(8,128)(2,1)S(1)} collective-permute-done((bf16[2,16,4096]{2,1,0:T(8,128)(2,1)S(1)}, bf16[2,16,4096]{2,1,0:T(8,128)(2,1)S(1)}, u32[]{:S(2)}, u32[]{:S(2)}) %collective-permute-start.11) | collective-permute-done | bytes 262176 | tf_op jit(solution)/shard_map/ppermute | solution.py:52
  53.8 3.8 %collective-permute-start.12 = (bf16[2,8,4096]{2,1,0:T(8,128)(2,1)S(1)}, bf16[2,8,4096]{2,1,0:T(8,128)(2,1)S(1)}, u32[]{:S(2)}, u32[]{:S(2)}) collective-permute-start(bf16[2,8,4096]{2,1,0:T(8,128)(2,1)S(1)} %pad_maximum_fusion.8), channel_id=1, source_target_pairs={{0,8},{1,3},{2,10},{3,1},{4,12},{5,7},{6,14},{7,5},{8,0},{9,11},{1... | collective-permute-start | bytes 393224 | tf_op jit(solution)/shard_map/ppermute | solution.py:52
  57.6 2.9 %collective-permute-done.12 = bf16[2,8,4096]{2,1,0:T(8,128)(2,1)S(1)} collective-permute-done((bf16[2,8,4096]{2,1,0:T(8,128)(2,1)S(1)}, bf16[2,8,4096]{2,1,0:T(8,128)(2,1)S(1)}, u32[]{:S(2)}, u32[]{:S(2)}) %collective-permute-start.12) | collective-permute-done | bytes 131104 | tf_op jit(solution)/shard_map/ppermute | solution.py:52
  60.5 0.7 %convert_add_fusion.5 = (bf16[8,4096]{1,0:T(8,128)(2,1)}, bf16[8,4096]{1,0:T(8,128)(2,1)}) fusion(f32[16,4096]{1,0:T(8,128)S(1)} %get-tuple-element.77, bf16[2,8,4096]{2,1,0:T(8,128)(2,1)S(1)} %collective-permute-done.12, f32[16,4096]{1,0:T(8,128)S(1)} %get-tuple-element.76), kind=kLoop, calls=%fused_computation.34 | loop fusion | flops 196608 | bytes 524288 | tf_op jit(solution)/shard_map/add | solution.py:71
  (46 shorter events, 2.2 us)
Async XLA Ops:
  0.6 6.6 %collective-permute-start = (bf16[8,4096]{1,0:T(8,128)(2,1)}, bf16[8,4096]{1,0:T(8,128)(2,1)S(1)}, u32[]{:S(2)}, u32[]{:S(2)}) collective-permute-start(bf16[8,4096]{1,0:T(8,128)(2,1)} %after.2), channel_id=1, source_target_pairs={{0,8},{1,3},{2,10},{3,1},{4,12},{5,7},{6,14},{7,5},{8,0},{9,11},{1... | collective-permute-start | bytes 196616 | tf_op jit(solution)/shard_map/ppermute | solution.py:52
  4.7 0.9 %copy-start.2 = (bf16[8,4096]{1,0:T(8,128)(2,1)S(1)}, bf16[8,4096]{1,0:T(8,128)(2,1)}, u32[]{:S(2)}) copy-start(bf16[8,4096]{1,0:T(8,128)(2,1)} %after.2) | copy-start | bytes 196612
  5.7 0.8 %copy-start.3 = (bf16[8,4096]{1,0:T(8,128)(2,1)S(1)}, bf16[8,4096]{1,0:T(8,128)(2,1)}, u32[]{:S(2)}) copy-start(bf16[8,4096]{1,0:T(8,128)(2,1)} %after.3) | copy-start | bytes 196612
  7.2 5.3 %collective-permute-start.1 = (bf16[16,4096]{1,0:T(8,128)(2,1)S(1)}, bf16[16,4096]{1,0:T(8,128)(2,1)S(1)}, u32[]{:S(2)}, u32[]{:S(2)}) collective-permute-start(bf16[16,4096]{1,0:T(8,128)(2,1)S(1)} %pad_maximum_fusion.6), channel_id=1, source_target_pairs={{0,4},{1,9},{2,6},{3,11},{4,0},{5,13},{6,2},{7,15},{8,12},{9,1},{1... | collective-permute-start | bytes 393224 | tf_op jit(solution)/shard_map/ppermute | solution.py:52
  9.2 5.6 %collective-permute-start.3 = (bf16[8,4096]{1,0:T(8,128)(2,1)S(1)}, bf16[8,4096]{1,0:T(8,128)(2,1)S(1)}, u32[]{:S(2)}, u32[]{:S(2)}) collective-permute-start(bf16[8,4096]{1,0:T(8,128)(2,1)S(1)} %copy-done.3), channel_id=1, source_target_pairs={{0,8},{1,3},{2,10},{3,1},{4,12},{5,7},{6,14},{7,5},{8,0},{9,11},{1... | collective-permute-start | bytes 196616 | tf_op jit(solution)/shard_map/ppermute | solution.py:52
  12.5 7.7 %collective-permute-start.2 = (bf16[32,4096]{1,0:T(8,128)(2,1)S(1)}, bf16[32,4096]{1,0:T(8,128)(2,1)S(1)}, u32[]{:S(2)}, u32[]{:S(2)}) collective-permute-start(bf16[32,4096]{1,0:T(8,128)(2,1)S(1)} %pad_maximum_fusion.3.after), channel_id=1, source_target_pairs={{0,2},{1,5},{2,0},{3,7},{4,6},{5,1},{6,4},{7,3},{8,10},{9,13},{10,... | collective-permute-start | bytes 786440 | tf_op jit(solution)/shard_map/ppermute | solution.py:52
  14.8 5.4 %collective-permute-start.4 = (bf16[16,4096]{1,0:T(8,128)(2,1)S(1)}, bf16[16,4096]{1,0:T(8,128)(2,1)S(1)}, u32[]{:S(2)}, u32[]{:S(2)}) collective-permute-start(bf16[16,4096]{1,0:T(8,128)(2,1)S(1)} %pad_maximum_fusion.7), channel_id=1, source_target_pairs={{0,4},{1,9},{2,6},{3,11},{4,0},{5,13},{6,2},{7,15},{8,12},{9,1},{1... | collective-permute-start | bytes 393224 | tf_op jit(solution)/shard_map/ppermute | solution.py:52
  16.1 3.1 %copy-start = (bf16[896,4096]{1,0:T(8,128)(2,1)S(1)}, bf16[896,4096]{1,0:T(8,128)(2,1)}, u32[]{:S(2)}) copy-start(bf16[896,4096]{1,0:T(8,128)(2,1)} %weight.6) | copy-start | bytes 22020100
  19.2 3.1 %copy-start.1 = (bf16[896,4096]{1,0:T(8,128)(2,1)S(1)}, bf16[896,4096]{1,0:T(8,128)(2,1)}, u32[]{:S(2)}) copy-start(bf16[896,4096]{1,0:T(8,128)(2,1)} %weight.7) | copy-start | bytes 22020100
  20.3 2.5 %collective-permute-start.5 = (bf16[64,4096]{1,0:T(8,128)(2,1)S(1)}, bf16[64,4096]{1,0:T(8,128)(2,1)S(1)}, u32[]{:S(2)}, u32[]{:S(2)}) collective-permute-start(bf16[64,4096]{1,0:T(8,128)(2,1)S(1)} %pad_maximum_fusion.after), channel_id=1, source_target_pairs={{0,1},{1,0},{2,3},{3,2},{4,5},{5,4},{6,7},{7,6},{8,9},{9,8},{10,11... | collective-permute-start | bytes 1572872 | tf_op jit(solution)/shard_map/ppermute | solution.py:52
  20.4 7.5 %collective-permute-start.6 = (bf16[32,4096]{1,0:T(8,128)(2,1)S(1)}, bf16[32,4096]{1,0:T(8,128)(2,1)S(1)}, u32[]{:S(2)}, u32[]{:S(2)}) collective-permute-start(bf16[32,4096]{1,0:T(8,128)(2,1)S(1)} %pad_maximum_fusion.4), channel_id=1, source_target_pairs={{0,2},{1,5},{2,0},{3,7},{4,6},{5,1},{6,4},{7,3},{8,10},{9,13},{10,... | collective-permute-start | bytes 786440 | tf_op jit(solution)/shard_map/ppermute | solution.py:52
  22.9 5.1 %slice-start = ((s8[7340032]{0:T(1024)(128)(4,1)}), s8[4194304]{0:T(1024)(128)(4,1)S(1)}, s32[]{:S(2)}) async-start(s8[7340032]{0:T(1024)(128)(4,1)} %bitcast.46), calls=%async_computation | async-start | bytes 8388608
  25.4 2.6 %slice-start.1 = ((s8[7340032]{0:T(1024)(128)(4,1)}), s8[3145728]{0:T(1024)(128)(4,1)S(1)}, s32[]{:S(2)}) async-start(s8[7340032]{0:T(1024)(128)(4,1)} %bitcast.46), calls=%async_computation.1 | async-start | bytes 6291456
  27.9 2.0 %collective-permute-start.7 = (bf16[64,4096]{1,0:T(8,128)(2,1)S(1)}, bf16[64,4096]{1,0:T(8,128)(2,1)S(1)}, u32[]{:S(2)}, u32[]{:S(2)}) collective-permute-start(bf16[64,4096]{1,0:T(8,128)(2,1)S(1)} %pad_maximum_fusion.1), channel_id=1, source_target_pairs={{0,1},{1,0},{2,3},{3,2},{4,5},{5,4},{6,7},{7,6},{8,9},{9,8},{10,11... | collective-permute-start | bytes 1572872 | tf_op jit(solution)/shard_map/ppermute | solution.py:52
  29.9 2.8 %collective-permute-start.8 = (bf16[64,4096]{1,0:T(8,128)(2,1)S(1)}, bf16[64,4096]{1,0:T(8,128)(2,1)S(1)}, u32[]{:S(2)}, u32[]{:S(2)}) collective-permute-start(bf16[64,4096]{1,0:T(8,128)(2,1)S(1)} %slice.147), channel_id=1, source_target_pairs={{0,1},{1,0},{2,3},{3,2},{4,5},{5,4},{6,7},{7,6},{8,9},{9,8},{10,11... | collective-permute-start | bytes 1572872 | tf_op jit(solution)/shard_map/ppermute | solution.py:52
  35.4 2.0 %collective-permute-start.9 = (bf16[64,4096]{1,0:T(8,128)(2,1)S(1)}, bf16[64,4096]{1,0:T(8,128)(2,1)S(1)}, u32[]{:S(2)}, u32[]{:S(2)}) collective-permute-start(bf16[64,4096]{1,0:T(8,128)(2,1)S(1)} %slice.146), channel_id=1, source_target_pairs={{0,1},{1,0},{2,3},{3,2},{4,5},{5,4},{6,7},{7,6},{8,9},{9,8},{10,11... | collective-permute-start | bytes 1572872 | tf_op jit(solution)/shard_map/ppermute | solution.py:52
  37.6 9.2 %collective-permute-start.10 = (bf16[2,32,4096]{2,1,0:T(8,128)(2,1)S(1)}, bf16[2,32,4096]{2,1,0:T(8,128)(2,1)S(1)}, u32[]{:S(2)}, u32[]{:S(2)}) collective-permute-start(bf16[2,32,4096]{2,1,0:T(8,128)(2,1)S(1)} %pad_maximum_fusion.2), channel_id=1, source_target_pairs={{0,2},{1,5},{2,0},{3,7},{4,6},{5,1},{6,4},{7,3},{8,10},{9,13},{10,... | collective-permute-start | bytes 1572872 | tf_op jit(solution)/shard_map/ppermute | solution.py:52
  47.0 6.6 %collective-permute-start.11 = (bf16[2,16,4096]{2,1,0:T(8,128)(2,1)S(1)}, bf16[2,16,4096]{2,1,0:T(8,128)(2,1)S(1)}, u32[]{:S(2)}, u32[]{:S(2)}) collective-permute-start(bf16[2,16,4096]{2,1,0:T(8,128)(2,1)S(1)} %pad_maximum_fusion.5), channel_id=1, source_target_pairs={{0,4},{1,9},{2,6},{3,11},{4,0},{5,13},{6,2},{7,15},{8,12},{9,1},{1... | collective-permute-start | bytes 786440 | tf_op jit(solution)/shard_map/ppermute | solution.py:52
  53.8 6.8 %collective-permute-start.12 = (bf16[2,8,4096]{2,1,0:T(8,128)(2,1)S(1)}, bf16[2,8,4096]{2,1,0:T(8,128)(2,1)S(1)}, u32[]{:S(2)}, u32[]{:S(2)}) collective-permute-start(bf16[2,8,4096]{2,1,0:T(8,128)(2,1)S(1)} %pad_maximum_fusion.8), channel_id=1, source_target_pairs={{0,8},{1,3},{2,10},{3,1},{4,12},{5,7},{6,14},{7,5},{8,0},{9,11},{1... | collective-permute-start | bytes 393224 | tf_op jit(solution)/shard_map/ppermute | solution.py:52

commit v5 on v4

--- a/solution.py
+++ b/solution.py
@@ -111,13 +111,12 @@
             got_c = swap(c if k else cotangent, n, late)
             got_t = swap(t, n, stage)
             if k == 1:
-                got_t, got_c, gate_weight = tie((got_t, got_c, fetch(gate_weight, t)))
+                got_t, got_c, up_weight = tie((got_t, got_c, fetch(up_weight, t)))
             t = tie(join(t, got_t))
             c = join(c, got_c)
             if k:
                 t, c = tie((t, c))
         got_c = swap(c, n, there[-2])
-        up_weight = fetch(up_weight, t)
         t = join(t, swap(t, n, there[-1]))
         gate = rows_by_weight(t, gate_weight)
         up = rows_by_weight(t, up_weight)

time: 61.7 us -> 61.4 us (level)
  Pallas kernels: 11.8 us -> 11.1 us
  transfers between devices with their start and end apart: 13 -> 13, of which waited for: 9 -> 10; matrix products, arithmetic and copies ran while one was open for 15% -> 15% of each run, Pallas kernels for 19% -> 18%
where the time goes in v5:
time: 61.4 us; the launch traced here: 60.8 us
  starting transfers between devices  21.3 us (35%)
  matrix products  11.2 us (18%)
  Pallas kernels  11.1 us (18%)
  waiting for transfers between devices  9.74 us (16%)
  local copies, waits for them, and re-layouts  5.19 us (8%)
  other arithmetic  1.27 us (2%)
  between operations  0.96 us (2%)
    ppermute x13, starting transfers between devices, swap(): return lax.ppermute(x, 'tensor', [(i, i ^ stage[i % 2]) for i in range(n)])  21.3 us
    pallas_call x3, Pallas kernels, gradient(): pl.pallas_call(gradient_kernel, out_shape=jax.ShapeDtypeStruct((rows, wid...  10.5 us
    ppermute x13, waiting for transfers between devices, swap(): return lax.ppermute(x, 'tensor', [(i, i ^ stage[i % 2]) for i in range(n)])  9.74 us
    dot_general x3, matrix products, rows_by_weight(): lax.dot_general(left, weight, (((1,), (1,)), ((), ())), preferred_element...  7.42 us
    unnamed x15, local copies, waits for them, and re-layouts  4.9 us
    dot_general x1, matrix products, per_device(): terms = terms + jnp.dot(d_up, up_weight, preferred_element_type=F32)  1.3 us
    dot_general x1, matrix products, per_device(): terms = jnp.dot(d_gate, gate_weight, preferred_element_type=F32)  1.26 us
    dot_general x1, matrix products, per_device(): jnp.dot(hidden, down_weight, preferred_element_type=F32)  1.26 us
  transfers between devices with their start and end apart: 13, of which 10 were waited for; matrix products, arithmetic and copies ran while one was open for 15% of the time, Pallas kernels for 18%

profile of v5, /device:TPU:0, one launch (start us, length us, event | category | flops | bytes accessed | tf_op | source)
XLA Modules:
  0.0 60.8 jit_solution(6652513428497458105)
XLA Ops:
  0.6 4.1 %collective-permute-start = (bf16[8,4096]{1,0:T(8,128)(2,1)}, bf16[8,4096]{1,0:T(8,128)(2,1)S(1)}, u32[]{:S(2)}, u32[]{:S(2)}) collective-permute-start(bf16[8,4096]{1,0:T(8,128)(2,1)} %after.2), channel_id=1, source_target_pairs={{0,8},{1,3},{2,10},{3,1},{4,12},{5,7},{6,14},{7,5},{8,0},{9,11},{1... | collective-permute-start | bytes 196616 | tf_op jit(solution)/shard_map/ppermute | solution.py:52
  4.7 0.9 %copy-done.1 = bf16[8,4096]{1,0:T(8,128)(2,1)S(1)} copy-done((bf16[8,4096]{1,0:T(8,128)(2,1)S(1)}, bf16[8,4096]{1,0:T(8,128)(2,1)}, u32[]{:S(2)}) %copy-start.1) | copy-done | bytes 65560
  5.7 0.8 %copy-done.2 = bf16[8,4096]{1,0:T(8,128)(2,1)S(1)} copy-done((bf16[8,4096]{1,0:T(8,128)(2,1)S(1)}, bf16[8,4096]{1,0:T(8,128)(2,1)}, u32[]{:S(2)}) %copy-start.2) | copy-done | bytes 65560
  6.6 0.6 collective-permute-done
  7.2 2.0 %collective-permute-start.1 = (bf16[16,4096]{1,0:T(8,128)(2,1)S(1)}, bf16[16,4096]{1,0:T(8,128)(2,1)S(1)}, u32[]{:S(2)}, u32[]{:S(2)}) collective-permute-start(bf16[16,4096]{1,0:T(8,128)(2,1)S(1)} %pad_maximum_fusion.6), channel_id=1, source_target_pairs={{0,4},{1,9},{2,6},{3,11},{4,0},{5,13},{6,2},{7,15},{8,12},{9,1},{1... | collective-permute-start | bytes 393224 | tf_op jit(solution)/shard_map/ppermute | solution.py:52
  9.2 3.2 %collective-permute-start.3 = (bf16[8,4096]{1,0:T(8,128)(2,1)S(1)}, bf16[8,4096]{1,0:T(8,128)(2,1)S(1)}, u32[]{:S(2)}, u32[]{:S(2)}) collective-permute-start(bf16[8,4096]{1,0:T(8,128)(2,1)S(1)} %copy-done.2), channel_id=1, source_target_pairs={{0,8},{1,3},{2,10},{3,1},{4,12},{5,7},{6,14},{7,5},{8,0},{9,11},{1... | collective-permute-start | bytes 196616 | tf_op jit(solution)/shard_map/ppermute | solution.py:52
  12.5 2.0 %collective-permute-start.2 = (bf16[32,4096]{1,0:T(8,128)(2,1)S(1)}, bf16[32,4096]{1,0:T(8,128)(2,1)S(1)}, u32[]{:S(2)}, u32[]{:S(2)}) collective-permute-start(bf16[32,4096]{1,0:T(8,128)(2,1)S(1)} %pad_maximum_fusion.3.after), channel_id=1, source_target_pairs={{0,2},{1,5},{2,0},{3,7},{4,6},{5,1},{6,4},{7,3},{8,10},{9,13},{10,... | collective-permute-start | bytes 786440 | tf_op jit(solution)/shard_map/ppermute | solution.py:52
  14.5 0.3 collective-permute-done.3
  14.8 1.3 %collective-permute-start.4 = (bf16[16,4096]{1,0:T(8,128)(2,1)S(1)}, bf16[16,4096]{1,0:T(8,128)(2,1)S(1)}, u32[]{:S(2)}, u32[]{:S(2)}) collective-permute-start(bf16[16,4096]{1,0:T(8,128)(2,1)S(1)} %pad_maximum_fusion.7), channel_id=1, source_target_pairs={{0,4},{1,9},{2,6},{3,11},{4,0},{5,13},{6,2},{7,15},{8,12},{9,1},{1... | collective-permute-start | bytes 393224 | tf_op jit(solution)/shard_map/ppermute | solution.py:52
  16.1 3.1 %copy-done = bf16[896,4096]{1,0:T(8,128)(2,1)S(1)} copy-done((bf16[896,4096]{1,0:T(8,128)(2,1)S(1)}, bf16[896,4096]{1,0:T(8,128)(2,1)}, u32[]{:S(2)}) %copy-start) | copy-done | bytes 7340056
  19.2 0.5 shard_map.94
  19.7 0.5 collective-permute-done.4
  20.4 1.6 %collective-permute-start.6 = (bf16[32,4096]{1,0:T(8,128)(2,1)S(1)}, bf16[32,4096]{1,0:T(8,128)(2,1)S(1)}, u32[]{:S(2)}, u32[]{:S(2)}) collective-permute-start(bf16[32,4096]{1,0:T(8,128)(2,1)S(1)} %pad_maximum_fusion.4), channel_id=1, source_target_pairs={{0,2},{1,5},{2,0},{3,7},{4,6},{5,1},{6,4},{7,3},{8,10},{9,13},{10,... | collective-permute-start | bytes 786440 | tf_op jit(solution)/shard_map/ppermute | solution.py:52
  22.3 2.5 %fusion.7 = f32[128,896]{1,0:T(8,128)S(1)} fusion(bf16[128,4096]{1,0:T(8,128)(2,1)S(1)} %constant_dynamic-update-slice_fusion.right, bf16[896,4096]{1,0:T(8,128)(2,1)S(1)} %copy-done.3), kind=kOutput, calls=%fused_computation.44 | convolution fusion | flops 939524096 | bytes 8847360 | tf_op jit(solution)/shard_map/dot_general | solution.py:15
  24.8 2.4 %multiply_convert_fusion.2 = (bf16[128,896]{1,0:T(8,128)(2,1)S(1)}, f32[128,896]{1,0:T(8,128)S(1)}) fusion(f32[128,896]{1,0:T(8,128)S(1)} %fusion.7, bf16[128,4096]{1,0:T(8,128)(2,1)S(1)} %constant_dynamic-update-slice_fusion.right, bf16[896,4096]{1,0:T(8,128)(2,1)S(1)} %shard_map.94), kind=kOutput, calls=%fused_computation.14 | convolution fusion | flops 940212224 | bytes 9535488 | tf_op jit(solution)/shard_map/dot_general | solution.py:15
  27.6 1.3 %fusion.8 = f32[128,4096]{1,0:T(8,128)S(1)} fusion(bf16[128,896]{1,0:T(8,128)(2,1)S(1)} %get-tuple-element.65.left, bf16[896,4096]{1,0:T(8,128)(2,1)S(1)} %bitcast.47), kind=kOutput, calls=%fused_computation.45 | convolution fusion | flops 939524096 | bytes 9666560 | tf_op jit(solution)/shard_map/dot_general | solution.py:128
  28.8 0.5 collective-permute-done.7
  29.6 2.5 %multiply_convert_fusion = (bf16[128,896]{1,0:T(8,128)(2,1)S(1)}, bf16[128,896]{1,0:T(8,128)(2,1)S(1)}) fusion(f32[128,896]{1,0:T(8,128)S(1)} %fusion.7, f32[128,896]{1,0:T(8,128)S(1)} %get-tuple-element.92, bf16[128,4096]{1,0:T(8,128)(2,1)S(1)} %constant_dynamic-update-slice_fusion.2.right, bf16[896,4096]{1,0:T(8,128)(2,1)S(1)} %bitcast.47), kind=kOutput, calls=%fused_computation.12 | convolution fusion | flops 941015040 | bytes 9764864 | tf_op jit(solution)/shard_map/dot_general | solution.py:15
  32.2 1.3 %fusion.9 = f32[128,4096]{1,0:T(8,128)S(1)} fusion(bf16[128,896]{1,0:T(8,128)(2,1)S(1)} %get-tuple-element.67.left, bf16[896,4096]{1,0:T(8,128)(2,1)S(1)} %copy-done.3), kind=kOutput, calls=%fused_computation.46 | convolution fusion | flops 939524096 | bytes 9666560 | tf_op jit(solution)/shard_map/dot_general | solution.py:139
  33.5 1.3 %convolution_add_fusion = f32[128,4096]{1,0:T(8,128)S(1)} fusion(f32[128,4096]{1,0:T(8,128)S(1)} %fusion.9, bf16[128,896]{1,0:T(8,128)(2,1)S(1)} %get-tuple-element.73.left, bf16[896,4096]{1,0:T(8,128)(2,1)S(1)} %shard_map.94), kind=kOutput, calls=%fused_computation | convolution fusion | flops 940048384 | bytes 11763712 | tf_op jit(solution)/shard_map/dot_general | solution.py:140
  34.9 0.4 collective-permute-start.9
  35.3 1.5 %collective-permute-done.9 = bf16[64,4096]{1,0:T(8,128)(2,1)S(1)} collective-permute-done((bf16[64,4096]{1,0:T(8,128)(2,1)S(1)}, bf16[64,4096]{1,0:T(8,128)(2,1)S(1)}, u32[]{:S(2)}, u32[]{:S(2)}) %collective-permute-start.9) | collective-permute-done | bytes 524320 | tf_op jit(solution)/shard_map/ppermute | solution.py:52
  37.0 1.6 %collective-permute-start.10 = (bf16[2,32,4096]{2,1,0:T(8,128)(2,1)S(1)}, bf16[2,32,4096]{2,1,0:T(8,128)(2,1)S(1)}, u32[]{:S(2)}, u32[]{:S(2)}) collective-permute-start(bf16[2,32,4096]{2,1,0:T(8,128)(2,1)S(1)} %pad_maximum_fusion.2), channel_id=1, source_target_pairs={{0,2},{1,5},{2,0},{3,7},{4,6},{5,1},{6,4},{7,3},{8,10},{9,13},{10,... | collective-permute-start | bytes 1572872 | tf_op jit(solution)/shard_map/ppermute | solution.py:52
  38.6 3.5 %shard_map.96 = bf16[896,4096]{1,0:T(8,128)(2,1)} custom-call(bf16[128,896]{1,0:T(8,128)(2,1)S(1)} %get-tuple-element.67.left, bf16[128,4096]{1,0:T(8,128)(2,1)S(1)} %constant_dynamic-update-slice_fusion.right), custom_call_target="tpu_custom_call" | custom-call | flops 939524096 | bytes 7340032 | tf_op jit(solution)/shard_map/pallas_call | solution.py:88
  42.1 3.5 %shard_map.95 = bf16[896,4096]{1,0:T(8,128)(2,1)} custom-call(bf16[128,896]{1,0:T(8,128)(2,1)S(1)} %get-tuple-element.65.left, bf16[128,4096]{1,0:T(8,128)(2,1)S(1)} %constant_dynamic-update-slice_fusion.2.right), custom_call_target="tpu_custom_call" | custom-call | flops 939524096 | bytes 7340032 | tf_op jit(solution)/shard_map/pallas_call | solution.py:88
  45.6 0.6 %collective-permute-done.10 = bf16[2,32,4096]{2,1,0:T(8,128)(2,1)S(1)} collective-permute-done((bf16[2,32,4096]{2,1,0:T(8,128)(2,1)S(1)}, bf16[2,32,4096]{2,1,0:T(8,128)(2,1)S(1)}, u32[]{:S(2)}, u32[]{:S(2)}) %collective-permute-start.10) | collective-permute-done | bytes 524320 | tf_op jit(solution)/shard_map/ppermute | solution.py:52
  46.5 1.3 %collective-permute-start.11 = (bf16[2,16,4096]{2,1,0:T(8,128)(2,1)S(1)}, bf16[2,16,4096]{2,1,0:T(8,128)(2,1)S(1)}, u32[]{:S(2)}, u32[]{:S(2)}) collective-permute-start(bf16[2,16,4096]{2,1,0:T(8,128)(2,1)S(1)} %pad_maximum_fusion.5), channel_id=1, source_target_pairs={{0,4},{1,9},{2,6},{3,11},{4,0},{5,13},{6,2},{7,15},{8,12},{9,1},{1... | collective-permute-start | bytes 786440 | tf_op jit(solution)/shard_map/ppermute | solution.py:52
  47.8 3.5 %shard_map.97 = bf16[896,4096]{1,0:T(8,128)(2,1)} custom-call(bf16[128,896]{1,0:T(8,128)(2,1)S(1)} %get-tuple-element.73.left, bf16[128,4096]{1,0:T(8,128)(2,1)S(1)} %constant_dynamic-update-slice_fusion.right), custom_call_target="tpu_custom_call" | custom-call | flops 939524096 | bytes 7340032 | tf_op jit(solution)/shard_map/pallas_call | solution.py:88
  51.3 2.4 %collective-permute-done.11 = bf16[2,16,4096]{2,1,0:T(8,128)(2,1)S(1)} collective-permute-done((bf16[2,16,4096]{2,1,0:T(8,128)(2,1)S(1)}, bf16[2,16,4096]{2,1,0:T(8,128)(2,1)S(1)}, u32[]{:S(2)}, u32[]{:S(2)}) %collective-permute-start.11) | collective-permute-done | bytes 262176 | tf_op jit(solution)/shard_map/ppermute | solution.py:52
  53.8 3.4 %collective-permute-start.12 = (bf16[2,8,4096]{2,1,0:T(8,128)(2,1)S(1)}, bf16[2,8,4096]{2,1,0:T(8,128)(2,1)S(1)}, u32[]{:S(2)}, u32[]{:S(2)}) collective-permute-start(bf16[2,8,4096]{2,1,0:T(8,128)(2,1)S(1)} %pad_maximum_fusion.8), channel_id=1, source_target_pairs={{0,8},{1,3},{2,10},{3,1},{4,12},{5,7},{6,14},{7,5},{8,0},{9,11},{1... | collective-permute-start | bytes 393224 | tf_op jit(solution)/shard_map/ppermute | solution.py:52
  57.2 2.9 %collective-permute-done.12 = bf16[2,8,4096]{2,1,0:T(8,128)(2,1)S(1)} collective-permute-done((bf16[2,8,4096]{2,1,0:T(8,128)(2,1)S(1)}, bf16[2,8,4096]{2,1,0:T(8,128)(2,1)S(1)}, u32[]{:S(2)}, u32[]{:S(2)}) %collective-permute-start.12) | collective-permute-done | bytes 131104 | tf_op jit(solution)/shard_map/ppermute | solution.py:52
  60.2 0.7 %convert_add_fusion.5 = (bf16[8,4096]{1,0:T(8,128)(2,1)}, bf16[8,4096]{1,0:T(8,128)(2,1)}) fusion(f32[16,4096]{1,0:T(8,128)S(1)} %get-tuple-element.77, bf16[2,8,4096]{2,1,0:T(8,128)(2,1)S(1)} %collective-permute-done.12, f32[16,4096]{1,0:T(8,128)S(1)} %get-tuple-element.76), kind=kLoop, calls=%fused_computation.34 | loop fusion | flops 196608 | bytes 524288 | tf_op jit(solution)/shard_map/add | solution.py:71
  (45 shorter events, 2.0 us)
Async XLA Ops:
  0.6 6.6 %collective-permute-start = (bf16[8,4096]{1,0:T(8,128)(2,1)}, bf16[8,4096]{1,0:T(8,128)(2,1)S(1)}, u32[]{:S(2)}, u32[]{:S(2)}) collective-permute-start(bf16[8,4096]{1,0:T(8,128)(2,1)} %after.2), channel_id=1, source_target_pairs={{0,8},{1,3},{2,10},{3,1},{4,12},{5,7},{6,14},{7,5},{8,0},{9,11},{1... | collective-permute-start | bytes 196616 | tf_op jit(solution)/shard_map/ppermute | solution.py:52
  4.7 0.9 %copy-start.1 = (bf16[8,4096]{1,0:T(8,128)(2,1)S(1)}, bf16[8,4096]{1,0:T(8,128)(2,1)}, u32[]{:S(2)}) copy-start(bf16[8,4096]{1,0:T(8,128)(2,1)} %after.2) | copy-start | bytes 196612
  5.7 0.8 %copy-start.2 = (bf16[8,4096]{1,0:T(8,128)(2,1)S(1)}, bf16[8,4096]{1,0:T(8,128)(2,1)}, u32[]{:S(2)}) copy-start(bf16[8,4096]{1,0:T(8,128)(2,1)} %after.3) | copy-start | bytes 196612
  7.2 5.3 %collective-permute-start.1 = (bf16[16,4096]{1,0:T(8,128)(2,1)S(1)}, bf16[16,4096]{1,0:T(8,128)(2,1)S(1)}, u32[]{:S(2)}, u32[]{:S(2)}) collective-permute-start(bf16[16,4096]{1,0:T(8,128)(2,1)S(1)} %pad_maximum_fusion.6), channel_id=1, source_target_pairs={{0,4},{1,9},{2,6},{3,11},{4,0},{5,13},{6,2},{7,15},{8,12},{9,1},{1... | collective-permute-start | bytes 393224 | tf_op jit(solution)/shard_map/ppermute | solution.py:52
  9.2 5.6 %collective-permute-start.3 = (bf16[8,4096]{1,0:T(8,128)(2,1)S(1)}, bf16[8,4096]{1,0:T(8,128)(2,1)S(1)}, u32[]{:S(2)}, u32[]{:S(2)}) collective-permute-start(bf16[8,4096]{1,0:T(8,128)(2,1)S(1)} %copy-done.2), channel_id=1, source_target_pairs={{0,8},{1,3},{2,10},{3,1},{4,12},{5,7},{6,14},{7,5},{8,0},{9,11},{1... | collective-permute-start | bytes 196616 | tf_op jit(solution)/shard_map/ppermute | solution.py:52
  12.5 7.7 %collective-permute-start.2 = (bf16[32,4096]{1,0:T(8,128)(2,1)S(1)}, bf16[32,4096]{1,0:T(8,128)(2,1)S(1)}, u32[]{:S(2)}, u32[]{:S(2)}) collective-permute-start(bf16[32,4096]{1,0:T(8,128)(2,1)S(1)} %pad_maximum_fusion.3.after), channel_id=1, source_target_pairs={{0,2},{1,5},{2,0},{3,7},{4,6},{5,1},{6,4},{7,3},{8,10},{9,13},{10,... | collective-permute-start | bytes 786440 | tf_op jit(solution)/shard_map/ppermute | solution.py:52
  14.8 5.4 %collective-permute-start.4 = (bf16[16,4096]{1,0:T(8,128)(2,1)S(1)}, bf16[16,4096]{1,0:T(8,128)(2,1)S(1)}, u32[]{:S(2)}, u32[]{:S(2)}) collective-permute-start(bf16[16,4096]{1,0:T(8,128)(2,1)S(1)} %pad_maximum_fusion.7), channel_id=1, source_target_pairs={{0,4},{1,9},{2,6},{3,11},{4,0},{5,13},{6,2},{7,15},{8,12},{9,1},{1... | collective-permute-start | bytes 393224 | tf_op jit(solution)/shard_map/ppermute | solution.py:52
  16.1 3.1 %copy-start = (bf16[896,4096]{1,0:T(8,128)(2,1)S(1)}, bf16[896,4096]{1,0:T(8,128)(2,1)}, u32[]{:S(2)}) copy-start(bf16[896,4096]{1,0:T(8,128)(2,1)} %weight.5) | copy-start | bytes 22020100
  19.2 3.1 %copy-start.3 = (bf16[896,4096]{1,0:T(8,128)(2,1)S(1)}, bf16[896,4096]{1,0:T(8,128)(2,1)}, u32[]{:S(2)}) copy-start(bf16[896,4096]{1,0:T(8,128)(2,1)} %param.6) | copy-start | bytes 22020100
  20.3 2.0 %collective-permute-start.5 = (bf16[64,4096]{1,0:T(8,128)(2,1)S(1)}, bf16[64,4096]{1,0:T(8,128)(2,1)S(1)}, u32[]{:S(2)}, u32[]{:S(2)}) collective-permute-start(bf16[64,4096]{1,0:T(8,128)(2,1)S(1)} %pad_maximum_fusion), channel_id=1, source_target_pairs={{0,1},{1,0},{2,3},{3,2},{4,5},{5,4},{6,7},{7,6},{8,9},{9,8},{10,11... | collective-permute-start | bytes 1572872 | tf_op jit(solution)/shard_map/ppermute | solution.py:52
  20.4 6.9 %collective-permute-start.6 = (bf16[32,4096]{1,0:T(8,128)(2,1)S(1)}, bf16[32,4096]{1,0:T(8,128)(2,1)S(1)}, u32[]{:S(2)}, u32[]{:S(2)}) collective-permute-start(bf16[32,4096]{1,0:T(8,128)(2,1)S(1)} %pad_maximum_fusion.4), channel_id=1, source_target_pairs={{0,2},{1,5},{2,0},{3,7},{4,6},{5,1},{6,4},{7,3},{8,10},{9,13},{10,... | collective-permute-start | bytes 786440 | tf_op jit(solution)/shard_map/ppermute | solution.py:52
  22.3 5.2 %slice-start = ((s8[7340032]{0:T(1024)(128)(4,1)}), s8[4194304]{0:T(1024)(128)(4,1)S(1)}, s32[]{:S(2)}) async-start(s8[7340032]{0:T(1024)(128)(4,1)} %bitcast.46), calls=%async_computation | async-start | bytes 8388608
  24.8 2.8 %slice-start.1 = ((s8[7340032]{0:T(1024)(128)(4,1)}), s8[3145728]{0:T(1024)(128)(4,1)S(1)}, s32[]{:S(2)}) async-start(s8[7340032]{0:T(1024)(128)(4,1)} %bitcast.46), calls=%async_computation.1 | async-start | bytes 6291456
  27.3 2.0 %collective-permute-start.7 = (bf16[64,4096]{1,0:T(8,128)(2,1)S(1)}, bf16[64,4096]{1,0:T(8,128)(2,1)S(1)}, u32[]{:S(2)}, u32[]{:S(2)}) collective-permute-start(bf16[64,4096]{1,0:T(8,128)(2,1)S(1)} %pad_maximum_fusion.1), channel_id=1, source_target_pairs={{0,1},{1,0},{2,3},{3,2},{4,5},{5,4},{6,7},{7,6},{8,9},{9,8},{10,11... | collective-permute-start | bytes 1572872 | tf_op jit(solution)/shard_map/ppermute | solution.py:52
  29.3 2.8 %collective-permute-start.8 = (bf16[64,4096]{1,0:T(8,128)(2,1)S(1)}, bf16[64,4096]{1,0:T(8,128)(2,1)S(1)}, u32[]{:S(2)}, u32[]{:S(2)}) collective-permute-start(bf16[64,4096]{1,0:T(8,128)(2,1)S(1)} %slice.147), channel_id=1, source_target_pairs={{0,1},{1,0},{2,3},{3,2},{4,5},{5,4},{6,7},{7,6},{8,9},{9,8},{10,11... | collective-permute-start | bytes 1572872 | tf_op jit(solution)/shard_map/ppermute | solution.py:52
  34.9 2.0 %collective-permute-start.9 = (bf16[64,4096]{1,0:T(8,128)(2,1)S(1)}, bf16[64,4096]{1,0:T(8,128)(2,1)S(1)}, u32[]{:S(2)}, u32[]{:S(2)}) collective-permute-start(bf16[64,4096]{1,0:T(8,128)(2,1)S(1)} %slice.146), channel_id=1, source_target_pairs={{0,1},{1,0},{2,3},{3,2},{4,5},{5,4},{6,7},{7,6},{8,9},{9,8},{10,11... | collective-permute-start | bytes 1572872 | tf_op jit(solution)/shard_map/ppermute | solution.py:52
  37.0 9.2 %collective-permute-start.10 = (bf16[2,32,4096]{2,1,0:T(8,128)(2,1)S(1)}, bf16[2,32,4096]{2,1,0:T(8,128)(2,1)S(1)}, u32[]{:S(2)}, u32[]{:S(2)}) collective-permute-start(bf16[2,32,4096]{2,1,0:T(8,128)(2,1)S(1)} %pad_maximum_fusion.2), channel_id=1, source_target_pairs={{0,2},{1,5},{2,0},{3,7},{4,6},{5,1},{6,4},{7,3},{8,10},{9,13},{10,... | collective-permute-start | bytes 1572872 | tf_op jit(solution)/shard_map/ppermute | solution.py:52
  46.5 7.2 %collective-permute-start.11 = (bf16[2,16,4096]{2,1,0:T(8,128)(2,1)S(1)}, bf16[2,16,4096]{2,1,0:T(8,128)(2,1)S(1)}, u32[]{:S(2)}, u32[]{:S(2)}) collective-permute-start(bf16[2,16,4096]{2,1,0:T(8,128)(2,1)S(1)} %pad_maximum_fusion.5), channel_id=1, source_target_pairs={{0,4},{1,9},{2,6},{3,11},{4,0},{5,13},{6,2},{7,15},{8,12},{9,1},{1... | collective-permute-start | bytes 786440 | tf_op jit(solution)/shard_map/ppermute | solution.py:52
  53.8 6.4 %collective-permute-start.12 = (bf16[2,8,4096]{2,1,0:T(8,128)(2,1)S(1)}, bf16[2,8,4096]{2,1,0:T(8,128)(2,1)S(1)}, u32[]{:S(2)}, u32[]{:S(2)}) collective-permute-start(bf16[2,8,4096]{2,1,0:T(8,128)(2,1)S(1)} %pad_maximum_fusion.8), channel_id=1, source_target_pairs={{0,8},{1,3},{2,10},{3,1},{4,12},{5,7},{6,14},{7,5},{8,0},{9,11},{1... | collective-permute-start | bytes 393224 | tf_op jit(solution)/shard_map/ppermute | solution.py:52

commit v6 on v5

--- a/solution.py
+++ b/solution.py
@@ -1,3 +1,5 @@
+import functools
+
 import jax
 import jax.numpy as jnp
 from jax import lax
@@ -71,31 +73,37 @@
     return lower(x) + got.astype(F32)
 
 
-def gradient_kernel(left, right, out, held, sems):
-    rows = left.shape[1]
+def gradients_kernel(count, *refs):
+    pairs, outs, held, sems = refs[: 2 * count], refs[2 * count : 3 * count], refs[-2], refs[-1]
     copies = []
-    for k, at in enumerate(range(0, rows, CHUNK)):
-        part = pl.ds(at, min(CHUNK, rows - at))
-        held[part, :] = over_tokens(left[:, part], right[...]).astype(BF16)
-        copies.append(pltpu.make_async_copy(held.at[part, :], out.at[part, :], sems.at[k]))
-        copies[-1].start()
+    for job in range(count):
+        left, right = pairs[2 * job : 2 * job + 2]
+        rows = left.shape[1]
+        for k, at in enumerate(range(0, rows, CHUNK)):
+            part = pl.ds(at, min(CHUNK, rows - at))
+            held[job, part, :] = over_tokens(left[:, part], right[...]).astype(BF16)
+            copies.append(pltpu.make_async_copy(held.at[job, part, :], outs[job].at[part, :], sems.at[job, k]))
+            copies[-1].start()
     for copy in copies:
         copy.wait()
 
 
-def gradient(left, right):
-    rows, width = left.shape[1], right.shape[1]
+def gradients(jobs):
+    count, rows, width = len(jobs), jobs[0][0].shape[1], jobs[0][1].shape[1]
     return pl.pallas_call(
-        gradient_kernel,
-        out_shape=jax.ShapeDtypeStruct((rows, width), BF16),
-        in_specs=[pl.BlockSpec(memory_space=pltpu.VMEM)] * 2,
-        out_specs=pl.BlockSpec(memory_space=pl.ANY),
-        scratch_shapes=[pltpu.VMEM((rows, width), BF16), pltpu.SemaphoreType.DMA((pl.cdiv(rows, CHUNK),))],
-        compiler_params=pltpu.CompilerParams(vmem_limit_bytes=20 * 2**20),
+        functools.partial(gradients_kernel, count),
+        out_shape=[jax.ShapeDtypeStruct((rows, width), BF16)] * count,
+        in_specs=[pl.BlockSpec(memory_space=pltpu.VMEM)] * (2 * count),
+        out_specs=[pl.BlockSpec(memory_space=pl.ANY)] * count,
+        scratch_shapes=[
+            pltpu.VMEM((count, rows, width), BF16),
+            pltpu.SemaphoreType.DMA((count, pl.cdiv(rows, CHUNK))),
+        ],
+        compiler_params=pltpu.CompilerParams(vmem_limit_bytes=(8 + 10 * count) * 2**20),
         cost_estimate=pl.CostEstimate(
-            flops=2 * rows * width * left.shape[0], bytes_accessed=2 * rows * width, transcendentals=0
+            flops=2 * count * rows * width * jobs[0][0].shape[0], bytes_accessed=2 * count * rows * width, transcendentals=0
         ),
-    )(left, right)
+    )(*[ref for job in jobs for ref in job])
 
 
 def solution(mesh):
@@ -136,6 +144,7 @@
         out = add(out, got)
         out, d_gate, d_up = tie((out, d_gate, d_up))
 
+        got_out = swap(upper(out), n, back[1])
         terms = jnp.dot(d_gate, gate_weight, preferred_element_type=F32)
         terms = terms + jnp.dot(d_up, up_weight, preferred_element_type=F32)
         terms = add(terms, swap(upper(terms), n, back[0]))
@@ -143,10 +152,17 @@
         made = []
         for k in range(1, len(back)):
             terms, job = tie((terms, jobs[k - 1] if k <= 2 else ()))
-            sent = jnp.stack([upper(terms), upper(out)])
-            got, work = tie((swap(sent, n, back[k]), tuple(gradient(*one) for one in job)))
+            sent = upper(terms) if k == 1 else jnp.stack([upper(terms), upper(out)])
+            got = swap(sent, n, back[k])
+            work = tuple(gradients(job)) if job else ()
+            if k == 1:
+                got, work, got_out = tie((got, work, got_out))
+                out = add(out, got_out)
+                terms = add(terms, got)
+            else:
+                got, work = tie((got, work))
+                terms, out = tie((add(terms, got[0]), add(out, got[1])))
             made += work
-            terms, out = tie((add(terms, got[0]), add(out, got[1])))
         down_grad, gate_grad, up_grad = made
         return (out.astype(BF16), terms.astype(BF16), gate_grad, up_grad, down_grad)
 

time: 61.4 us -> 59.6 us (0.971)
  waiting for transfers between devices: 9.74 us -> 8.08 us
  starting transfers between devices: 21.3 us -> 22.6 us
  Pallas kernels: 11.1 us -> 9.89 us
    ppermute x13 -> x14, waiting for transfers between devices: 9.74 us -> 8.08 us  [swap(): return lax.ppermute(x, 'tensor', [(i, i ^ stage[i % 2]) for i in range(n)])]
    ppermute x13 -> x14, starting transfers between devices: 21.3 us -> 22.6 us  [swap(): return lax.ppermute(x, 'tensor', [(i, i ^ stage[i % 2]) for i in range(n)])]
    pallas_call x3 -> x2, Pallas kernels: 10.5 us -> 9.27 us  [gradients(): pl.pallas_call(functools.partial(gradients_kernel, count), out_shape=[jax...]
  transfers between devices with their start and end apart: 13 -> 14, of which waited for: 10 -> 9; matrix products, arithmetic and copies ran while one was open for 15% -> 15% of each run, Pallas kernels for 18% -> 17%
where the time goes in v6:
time: 59.6 us; the launch traced here: 59.1 us
  starting transfers between devices  22.6 us (38%)
  matrix products  11.2 us (19%)
  Pallas kernels  9.89 us (17%)
  waiting for transfers between devices  8.08 us (14%)
  local copies, waits for them, and re-layouts  5.19 us (9%)
  other arithmetic  1.17 us (2%)
  between operations  0.96 us (2%)
    ppermute x14, starting transfers between devices, swap(): return lax.ppermute(x, 'tensor', [(i, i ^ stage[i % 2]) for i in range(n)])  22.6 us
    pallas_call x2, Pallas kernels, gradients(): pl.pallas_call(functools.partial(gradients_kernel, count), out_shape=[jax...  9.27 us
    ppermute x14, waiting for transfers between devices, swap(): return lax.ppermute(x, 'tensor', [(i, i ^ stage[i % 2]) for i in range(n)])  8.08 us
    dot_general x3, matrix products, rows_by_weight(): lax.dot_general(left, weight, (((1,), (1,)), ((), ())), preferred_element...  7.42 us
    unnamed x15, local copies, waits for them, and re-layouts  4.9 us
    dot_general x1, matrix products, per_device(): terms = terms + jnp.dot(d_up, up_weight, preferred_element_type=F32)  1.3 us
    dot_general x1, matrix products, per_device(): terms = jnp.dot(d_gate, gate_weight, preferred_element_type=F32)  1.26 us
    dot_general x1, matrix products, per_device(): jnp.dot(hidden, down_weight, preferred_element_type=F32)  1.26 us
  transfers between devices with their start and end apart: 14, of which 9 were waited for; matrix products, arithmetic and copies ran while one was open for 15% of the time, Pallas kernels for 17%

profile of v6, /device:TPU:0, one launch (start us, length us, event | category | flops | bytes accessed | tf_op | source)
XLA Modules:
  0.0 59.1 jit_solution(14997536010848935119)
XLA Ops:
  0.6 4.1 %collective-permute-start = (bf16[8,4096]{1,0:T(8,128)(2,1)}, bf16[8,4096]{1,0:T(8,128)(2,1)S(1)}, u32[]{:S(2)}, u32[]{:S(2)}) collective-permute-start(bf16[8,4096]{1,0:T(8,128)(2,1)} %after.2), channel_id=1, source_target_pairs={{0,8},{1,3},{2,10},{3,1},{4,12},{5,7},{6,14},{7,5},{8,0},{9,11},{1... | collective-permute-start | bytes 196616 | tf_op jit(solution)/shard_map/ppermute | solution.py:54
  4.7 0.9 %copy-done.1 = bf16[8,4096]{1,0:T(8,128)(2,1)S(1)} copy-done((bf16[8,4096]{1,0:T(8,128)(2,1)S(1)}, bf16[8,4096]{1,0:T(8,128)(2,1)}, u32[]{:S(2)}) %copy-start.1) | copy-done | bytes 65560
  5.7 0.8 %copy-done.2 = bf16[8,4096]{1,0:T(8,128)(2,1)S(1)} copy-done((bf16[8,4096]{1,0:T(8,128)(2,1)S(1)}, bf16[8,4096]{1,0:T(8,128)(2,1)}, u32[]{:S(2)}) %copy-start.2) | copy-done | bytes 65560
  6.6 0.6 %collective-permute-done = bf16[8,4096]{1,0:T(8,128)(2,1)S(1)} collective-permute-done((bf16[8,4096]{1,0:T(8,128)(2,1)}, bf16[8,4096]{1,0:T(8,128)(2,1)S(1)}, u32[]{:S(2)}, u32[]{:S(2)}) %collective-permute-start) | collective-permute-done | bytes 65568 | tf_op jit(solution)/shard_map/ppermute | solution.py:54
  7.2 2.0 %collective-permute-start.1 = (bf16[16,4096]{1,0:T(8,128)(2,1)S(1)}, bf16[16,4096]{1,0:T(8,128)(2,1)S(1)}, u32[]{:S(2)}, u32[]{:S(2)}) collective-permute-start(bf16[16,4096]{1,0:T(8,128)(2,1)S(1)} %pad_maximum_fusion.5), channel_id=1, source_target_pairs={{0,4},{1,9},{2,6},{3,11},{4,0},{5,13},{6,2},{7,15},{8,12},{9,1},{1... | collective-permute-start | bytes 393224 | tf_op jit(solution)/shard_map/ppermute | solution.py:54
  9.2 3.2 %collective-permute-start.3 = (bf16[8,4096]{1,0:T(8,128)(2,1)S(1)}, bf16[8,4096]{1,0:T(8,128)(2,1)S(1)}, u32[]{:S(2)}, u32[]{:S(2)}) collective-permute-start(bf16[8,4096]{1,0:T(8,128)(2,1)S(1)} %copy-done.2), channel_id=1, source_target_pairs={{0,8},{1,3},{2,10},{3,1},{4,12},{5,7},{6,14},{7,5},{8,0},{9,11},{1... | collective-permute-start | bytes 196616 | tf_op jit(solution)/shard_map/ppermute | solution.py:54
  12.5 2.0 %collective-permute-start.2 = (bf16[32,4096]{1,0:T(8,128)(2,1)S(1)}, bf16[32,4096]{1,0:T(8,128)(2,1)S(1)}, u32[]{:S(2)}, u32[]{:S(2)}) collective-permute-start(bf16[32,4096]{1,0:T(8,128)(2,1)S(1)} %pad_maximum_fusion.2.after), channel_id=1, source_target_pairs={{0,2},{1,5},{2,0},{3,7},{4,6},{5,1},{6,4},{7,3},{8,10},{9,13},{10,... | collective-permute-start | bytes 786440 | tf_op jit(solution)/shard_map/ppermute | solution.py:54
  14.5 0.3 collective-permute-done.3
  14.8 1.3 %collective-permute-start.4 = (bf16[16,4096]{1,0:T(8,128)(2,1)S(1)}, bf16[16,4096]{1,0:T(8,128)(2,1)S(1)}, u32[]{:S(2)}, u32[]{:S(2)}) collective-permute-start(bf16[16,4096]{1,0:T(8,128)(2,1)S(1)} %pad_maximum_fusion.6), channel_id=1, source_target_pairs={{0,4},{1,9},{2,6},{3,11},{4,0},{5,13},{6,2},{7,15},{8,12},{9,1},{1... | collective-permute-start | bytes 393224 | tf_op jit(solution)/shard_map/ppermute | solution.py:54
  16.1 3.1 %copy-done = bf16[896,4096]{1,0:T(8,128)(2,1)S(1)} copy-done((bf16[896,4096]{1,0:T(8,128)(2,1)S(1)}, bf16[896,4096]{1,0:T(8,128)(2,1)}, u32[]{:S(2)}) %copy-start) | copy-done | bytes 7340056
  19.2 0.5 shard_map.94
  19.7 0.5 collective-permute-done.4
  20.4 1.6 %collective-permute-start.6 = (bf16[32,4096]{1,0:T(8,128)(2,1)S(1)}, bf16[32,4096]{1,0:T(8,128)(2,1)S(1)}, u32[]{:S(2)}, u32[]{:S(2)}) collective-permute-start(bf16[32,4096]{1,0:T(8,128)(2,1)S(1)} %pad_maximum_fusion.3), channel_id=1, source_target_pairs={{0,2},{1,5},{2,0},{3,7},{4,6},{5,1},{6,4},{7,3},{8,10},{9,13},{10,... | collective-permute-start | bytes 786440 | tf_op jit(solution)/shard_map/ppermute | solution.py:54
  22.0 0.2 collective-permute-done.5
  22.3 2.5 %fusion.5 = f32[128,896]{1,0:T(8,128)S(1)} fusion(bf16[128,4096]{1,0:T(8,128)(2,1)S(1)} %constant_dynamic-update-slice_fusion.refs_3_.refs_1_, bf16[896,4096]{1,0:T(8,128)(2,1)S(1)} %copy-done.3), kind=kOutput, calls=%fused_computation.41 | convolution fusion | flops 939524096 | bytes 8847360 | tf_op jit(solution)/shard_map/dot_general | solution.py:17
  24.8 2.4 %multiply_convert_fusion.2 = (bf16[128,896]{1,0:T(8,128)(2,1)S(1)}, f32[128,896]{1,0:T(8,128)S(1)}) fusion(f32[128,896]{1,0:T(8,128)S(1)} %fusion.5, bf16[128,4096]{1,0:T(8,128)(2,1)S(1)} %constant_dynamic-update-slice_fusion.refs_3_.refs_1_, bf16[896,4096]{1,0:T(8,128)(2,1)S(1)} %shard_map.94), kind=kOutput, calls=%fused_computation.13 | convolution fusion | flops 940212224 | bytes 9535488 | tf_op jit(solution)/shard_map/dot_general | solution.py:17
  27.6 1.3 %fusion.6 = f32[128,4096]{1,0:T(8,128)S(1)} fusion(bf16[128,896]{1,0:T(8,128)(2,1)S(1)} %get-tuple-element.65.refs_0_, bf16[896,4096]{1,0:T(8,128)(2,1)S(1)} %bitcast.37), kind=kOutput, calls=%fused_computation.42 | convolution fusion | flops 939524096 | bytes 9666560 | tf_op jit(solution)/shard_map/dot_general | solution.py:136
  28.8 0.5 collective-permute-done.7
  29.6 2.5 %multiply_convert_fusion = (bf16[128,896]{1,0:T(8,128)(2,1)S(1)}, bf16[128,896]{1,0:T(8,128)(2,1)S(1)}) fusion(f32[128,896]{1,0:T(8,128)S(1)} %fusion.5, f32[128,896]{1,0:T(8,128)S(1)} %get-tuple-element.92, bf16[128,4096]{1,0:T(8,128)(2,1)S(1)} %constant_dynamic-update-slice_fusion.2.refs_1_, bf16[896,4096]{1,0:T(8,128)(2,1)S(1)} %bitcast.37), kind=kOutput, calls=%fused_computation.11 | convolution fusion | flops 941015040 | bytes 9764864 | tf_op jit(solution)/shard_map/dot_general | solution.py:17
  32.2 1.3 %fusion.7 = f32[128,4096]{1,0:T(8,128)S(1)} fusion(bf16[128,896]{1,0:T(8,128)(2,1)S(1)} %get-tuple-element.67.refs_2_, bf16[896,4096]{1,0:T(8,128)(2,1)S(1)} %copy-done.3), kind=kOutput, calls=%fused_computation.43 | convolution fusion | flops 939524096 | bytes 9666560 | tf_op jit(solution)/shard_map/dot_general | solution.py:148
  33.5 1.3 %convolution_add_fusion = f32[128,4096]{1,0:T(8,128)S(1)} fusion(f32[128,4096]{1,0:T(8,128)S(1)} %fusion.7, bf16[128,896]{1,0:T(8,128)(2,1)S(1)} %get-tuple-element.75.refs_0_, bf16[896,4096]{1,0:T(8,128)(2,1)S(1)} %shard_map.94), kind=kOutput, calls=%fused_computation | convolution fusion | flops 940048384 | bytes 11763712 | tf_op jit(solution)/shard_map/dot_general | solution.py:149
  34.9 0.4 collective-permute-start.9
  35.3 1.6 %collective-permute-start.11 = (bf16[32,4096]{1,0:T(8,128)(2,1)S(1)}, bf16[32,4096]{1,0:T(8,128)(2,1)S(1)}, u32[]{:S(2)}, u32[]{:S(2)}) collective-permute-start(bf16[32,4096]{1,0:T(8,128)(2,1)S(1)} %slice.135), channel_id=1, source_target_pairs={{0,2},{1,5},{2,0},{3,7},{4,6},{5,1},{6,4},{7,3},{8,10},{9,13},{10,... | collective-permute-start | bytes 786440 | tf_op jit(solution)/shard_map/ppermute | solution.py:54
  37.0 1.5 %collective-permute-start.10 = (bf16[32,4096]{1,0:T(8,128)(2,1)S(1)}, bf16[32,4096]{1,0:T(8,128)(2,1)S(1)}, u32[]{:S(2)}, u32[]{:S(2)}) collective-permute-start(bf16[32,4096]{1,0:T(8,128)(2,1)S(1)} %slice.136), channel_id=1, source_target_pairs={{0,2},{1,5},{2,0},{3,7},{4,6},{5,1},{6,4},{7,3},{8,10},{9,13},{10,... | collective-permute-start | bytes 786440 | tf_op jit(solution)/shard_map/ppermute | solution.py:54
  38.6 5.8 %shard_map.95 = (bf16[896,4096]{1,0:T(8,128)(2,1)}, bf16[896,4096]{1,0:T(8,128)(2,1)}) custom-call(bf16[128,896]{1,0:T(8,128)(2,1)S(1)} %get-tuple-element.65.refs_0_, bf16[128,4096]{1,0:T(8,128)(2,1)S(1)} %constant_dynamic-update-slice_fusion.2.refs_1_, bf16[128,896]{1,0:T(8,128)(2,1)S(1)} %get-tuple-element.67.refs_2_, ...), custom_call_target="tpu_custom_call" | custom-call | flops 1879048192 | bytes 14680064 | tf_op jit(solution)/shard_map/pallas_call | solution.py:93
  44.3 0.2 collective-permute-done.10
  44.7 1.3 %collective-permute-start.12 = (bf16[2,16,4096]{2,1,0:T(8,128)(2,1)S(1)}, bf16[2,16,4096]{2,1,0:T(8,128)(2,1)S(1)}, u32[]{:S(2)}, u32[]{:S(2)}) collective-permute-start(bf16[2,16,4096]{2,1,0:T(8,128)(2,1)S(1)} %pad_maximum_fusion.4), channel_id=1, source_target_pairs={{0,4},{1,9},{2,6},{3,11},{4,0},{5,13},{6,2},{7,15},{8,12},{9,1},{1... | collective-permute-start | bytes 786440 | tf_op jit(solution)/shard_map/ppermute | solution.py:54
  46.1 3.5 %shard_map.96 = bf16[896,4096]{1,0:T(8,128)(2,1)} custom-call(bf16[128,896]{1,0:T(8,128)(2,1)S(1)} %get-tuple-element.75.refs_0_, bf16[128,4096]{1,0:T(8,128)(2,1)S(1)} %constant_dynamic-update-slice_fusion.refs_3_.refs_1_), custom_call_target="tpu_custom_call" | custom-call | flops 939524096 | bytes 7340032 | tf_op jit(solution)/shard_map/pallas_call | solution.py:93
  49.6 2.6 %collective-permute-done.12 = bf16[2,16,4096]{2,1,0:T(8,128)(2,1)S(1)} collective-permute-done((bf16[2,16,4096]{2,1,0:T(8,128)(2,1)S(1)}, bf16[2,16,4096]{2,1,0:T(8,128)(2,1)S(1)}, u32[]{:S(2)}, u32[]{:S(2)}) %collective-permute-start.12) | collective-permute-done | bytes 262176 | tf_op jit(solution)/shard_map/ppermute | solution.py:54
  52.3 3.2 %collective-permute-start.13 = (bf16[2,8,4096]{2,1,0:T(8,128)(2,1)S(1)}, bf16[2,8,4096]{2,1,0:T(8,128)(2,1)S(1)}, u32[]{:S(2)}, u32[]{:S(2)}) collective-permute-start(bf16[2,8,4096]{2,1,0:T(8,128)(2,1)S(1)} %pad_maximum_fusion.7), channel_id=1, source_target_pairs={{0,8},{1,3},{2,10},{3,1},{4,12},{5,7},{6,14},{7,5},{8,0},{9,11},{1... | collective-permute-start | bytes 393224 | tf_op jit(solution)/shard_map/ppermute | solution.py:54
  55.5 2.9 %collective-permute-done.13 = bf16[2,8,4096]{2,1,0:T(8,128)(2,1)S(1)} collective-permute-done((bf16[2,8,4096]{2,1,0:T(8,128)(2,1)S(1)}, bf16[2,8,4096]{2,1,0:T(8,128)(2,1)S(1)}, u32[]{:S(2)}, u32[]{:S(2)}) %collective-permute-start.13) | collective-permute-done | bytes 131104 | tf_op jit(solution)/shard_map/ppermute | solution.py:54
  58.5 0.7 %convert_add_fusion.4 = (bf16[8,4096]{1,0:T(8,128)(2,1)}, bf16[8,4096]{1,0:T(8,128)(2,1)}) fusion(f32[16,4096]{1,0:T(8,128)S(1)} %get-tuple-element.79, bf16[2,8,4096]{2,1,0:T(8,128)(2,1)S(1)} %collective-permute-done.13, f32[16,4096]{1,0:T(8,128)S(1)} %get-tuple-element.78), kind=kLoop, calls=%fused_computation.31 | loop fusion | flops 196608 | bytes 524288 | tf_op jit(solution)/shard_map/add | solution.py:73
  (46 shorter events, 1.6 us)
Async XLA Ops:
  0.6 6.6 %collective-permute-start = (bf16[8,4096]{1,0:T(8,128)(2,1)}, bf16[8,4096]{1,0:T(8,128)(2,1)S(1)}, u32[]{:S(2)}, u32[]{:S(2)}) collective-permute-start(bf16[8,4096]{1,0:T(8,128)(2,1)} %after.2), channel_id=1, source_target_pairs={{0,8},{1,3},{2,10},{3,1},{4,12},{5,7},{6,14},{7,5},{8,0},{9,11},{1... | collective-permute-start | bytes 196616 | tf_op jit(solution)/shard_map/ppermute | solution.py:54
  4.7 0.9 %copy-start.1 = (bf16[8,4096]{1,0:T(8,128)(2,1)S(1)}, bf16[8,4096]{1,0:T(8,128)(2,1)}, u32[]{:S(2)}) copy-start(bf16[8,4096]{1,0:T(8,128)(2,1)} %after.2) | copy-start | bytes 196612
  5.7 0.8 %copy-start.2 = (bf16[8,4096]{1,0:T(8,128)(2,1)S(1)}, bf16[8,4096]{1,0:T(8,128)(2,1)}, u32[]{:S(2)}) copy-start(bf16[8,4096]{1,0:T(8,128)(2,1)} %after.3) | copy-start | bytes 196612
  7.2 5.3 %collective-permute-start.1 = (bf16[16,4096]{1,0:T(8,128)(2,1)S(1)}, bf16[16,4096]{1,0:T(8,128)(2,1)S(1)}, u32[]{:S(2)}, u32[]{:S(2)}) collective-permute-start(bf16[16,4096]{1,0:T(8,128)(2,1)S(1)} %pad_maximum_fusion.5), channel_id=1, source_target_pairs={{0,4},{1,9},{2,6},{3,11},{4,0},{5,13},{6,2},{7,15},{8,12},{9,1},{1... | collective-permute-start | bytes 393224 | tf_op jit(solution)/shard_map/ppermute | solution.py:54
  9.2 5.6 %collective-permute-start.3 = (bf16[8,4096]{1,0:T(8,128)(2,1)S(1)}, bf16[8,4096]{1,0:T(8,128)(2,1)S(1)}, u32[]{:S(2)}, u32[]{:S(2)}) collective-permute-start(bf16[8,4096]{1,0:T(8,128)(2,1)S(1)} %copy-done.2), channel_id=1, source_target_pairs={{0,8},{1,3},{2,10},{3,1},{4,12},{5,7},{6,14},{7,5},{8,0},{9,11},{1... | collective-permute-start | bytes 196616 | tf_op jit(solution)/shard_map/ppermute | solution.py:54
  12.5 7.7 %collective-permute-start.2 = (bf16[32,4096]{1,0:T(8,128)(2,1)S(1)}, bf16[32,4096]{1,0:T(8,128)(2,1)S(1)}, u32[]{:S(2)}, u32[]{:S(2)}) collective-permute-start(bf16[32,4096]{1,0:T(8,128)(2,1)S(1)} %pad_maximum_fusion.2.after), channel_id=1, source_target_pairs={{0,2},{1,5},{2,0},{3,7},{4,6},{5,1},{6,4},{7,3},{8,10},{9,13},{10,... | collective-permute-start | bytes 786440 | tf_op jit(solution)/shard_map/ppermute | solution.py:54
  14.8 5.4 %collective-permute-start.4 = (bf16[16,4096]{1,0:T(8,128)(2,1)S(1)}, bf16[16,4096]{1,0:T(8,128)(2,1)S(1)}, u32[]{:S(2)}, u32[]{:S(2)}) collective-permute-start(bf16[16,4096]{1,0:T(8,128)(2,1)S(1)} %pad_maximum_fusion.6), channel_id=1, source_target_pairs={{0,4},{1,9},{2,6},{3,11},{4,0},{5,13},{6,2},{7,15},{8,12},{9,1},{1... | collective-permute-start | bytes 393224 | tf_op jit(solution)/shard_map/ppermute | solution.py:54
  16.1 3.1 %copy-start = (bf16[896,4096]{1,0:T(8,128)(2,1)S(1)}, bf16[896,4096]{1,0:T(8,128)(2,1)}, u32[]{:S(2)}) copy-start(bf16[896,4096]{1,0:T(8,128)(2,1)} %weight.5) | copy-start | bytes 22020100
  19.2 3.1 %copy-start.3 = (bf16[896,4096]{1,0:T(8,128)(2,1)S(1)}, bf16[896,4096]{1,0:T(8,128)(2,1)}, u32[]{:S(2)}) copy-start(bf16[896,4096]{1,0:T(8,128)(2,1)} %param.6) | copy-start | bytes 22020100
  20.3 2.0 %collective-permute-start.5 = (bf16[64,4096]{1,0:T(8,128)(2,1)S(1)}, bf16[64,4096]{1,0:T(8,128)(2,1)S(1)}, u32[]{:S(2)}, u32[]{:S(2)}) collective-permute-start(bf16[64,4096]{1,0:T(8,128)(2,1)S(1)} %pad_maximum_fusion), channel_id=1, source_target_pairs={{0,1},{1,0},{2,3},{3,2},{4,5},{5,4},{6,7},{7,6},{8,9},{9,8},{10,11... | collective-permute-start | bytes 1572872 | tf_op jit(solution)/shard_map/ppermute | solution.py:54
  20.4 6.9 %collective-permute-start.6 = (bf16[32,4096]{1,0:T(8,128)(2,1)S(1)}, bf16[32,4096]{1,0:T(8,128)(2,1)S(1)}, u32[]{:S(2)}, u32[]{:S(2)}) collective-permute-start(bf16[32,4096]{1,0:T(8,128)(2,1)S(1)} %pad_maximum_fusion.3), channel_id=1, source_target_pairs={{0,2},{1,5},{2,0},{3,7},{4,6},{5,1},{6,4},{7,3},{8,10},{9,13},{10,... | collective-permute-start | bytes 786440 | tf_op jit(solution)/shard_map/ppermute | solution.py:54
  22.3 5.2 %slice-start = ((s8[7340032]{0:T(1024)(128)(4,1)}), s8[4194304]{0:T(1024)(128)(4,1)S(1)}, s32[]{:S(2)}) async-start(s8[7340032]{0:T(1024)(128)(4,1)} %bitcast.36), calls=%async_computation | async-start | bytes 8388608
  24.8 2.8 %slice-start.1 = ((s8[7340032]{0:T(1024)(128)(4,1)}), s8[3145728]{0:T(1024)(128)(4,1)S(1)}, s32[]{:S(2)}) async-start(s8[7340032]{0:T(1024)(128)(4,1)} %bitcast.36), calls=%async_computation.1 | async-start | bytes 6291456
  27.3 2.0 %collective-permute-start.7 = (bf16[64,4096]{1,0:T(8,128)(2,1)S(1)}, bf16[64,4096]{1,0:T(8,128)(2,1)S(1)}, u32[]{:S(2)}, u32[]{:S(2)}) collective-permute-start(bf16[64,4096]{1,0:T(8,128)(2,1)S(1)} %pad_maximum_fusion.1), channel_id=1, source_target_pairs={{0,1},{1,0},{2,3},{3,2},{4,5},{5,4},{6,7},{7,6},{8,9},{9,8},{10,11... | collective-permute-start | bytes 1572872 | tf_op jit(solution)/shard_map/ppermute | solution.py:54
  29.3 2.8 %collective-permute-start.8 = (bf16[64,4096]{1,0:T(8,128)(2,1)S(1)}, bf16[64,4096]{1,0:T(8,128)(2,1)S(1)}, u32[]{:S(2)}, u32[]{:S(2)}) collective-permute-start(bf16[64,4096]{1,0:T(8,128)(2,1)S(1)} %slice.134), channel_id=1, source_target_pairs={{0,1},{1,0},{2,3},{3,2},{4,5},{5,4},{6,7},{7,6},{8,9},{9,8},{10,11... | collective-permute-start | bytes 1572872 | tf_op jit(solution)/shard_map/ppermute | solution.py:54
  34.9 2.1 %collective-permute-start.9 = (bf16[64,4096]{1,0:T(8,128)(2,1)S(1)}, bf16[64,4096]{1,0:T(8,128)(2,1)S(1)}, u32[]{:S(2)}, u32[]{:S(2)}) collective-permute-start(bf16[64,4096]{1,0:T(8,128)(2,1)S(1)} %slice.133), channel_id=1, source_target_pairs={{0,1},{1,0},{2,3},{3,2},{4,5},{5,4},{6,7},{7,6},{8,9},{9,8},{10,11... | collective-permute-start | bytes 1572872 | tf_op jit(solution)/shard_map/ppermute | solution.py:54
  35.3 9.0 %collective-permute-start.11 = (bf16[32,4096]{1,0:T(8,128)(2,1)S(1)}, bf16[32,4096]{1,0:T(8,128)(2,1)S(1)}, u32[]{:S(2)}, u32[]{:S(2)}) collective-permute-start(bf16[32,4096]{1,0:T(8,128)(2,1)S(1)} %slice.135), channel_id=1, source_target_pairs={{0,2},{1,5},{2,0},{3,7},{4,6},{5,1},{6,4},{7,3},{8,10},{9,13},{10,... | collective-permute-start | bytes 786440 | tf_op jit(solution)/shard_map/ppermute | solution.py:54
  37.0 7.5 %collective-permute-start.10 = (bf16[32,4096]{1,0:T(8,128)(2,1)S(1)}, bf16[32,4096]{1,0:T(8,128)(2,1)S(1)}, u32[]{:S(2)}, u32[]{:S(2)}) collective-permute-start(bf16[32,4096]{1,0:T(8,128)(2,1)S(1)} %slice.136), channel_id=1, source_target_pairs={{0,2},{1,5},{2,0},{3,7},{4,6},{5,1},{6,4},{7,3},{8,10},{9,13},{10,... | collective-permute-start | bytes 786440 | tf_op jit(solution)/shard_map/ppermute | solution.py:54
  44.7 7.5 %collective-permute-start.12 = (bf16[2,16,4096]{2,1,0:T(8,128)(2,1)S(1)}, bf16[2,16,4096]{2,1,0:T(8,128)(2,1)S(1)}, u32[]{:S(2)}, u32[]{:S(2)}) collective-permute-start(bf16[2,16,4096]{2,1,0:T(8,128)(2,1)S(1)} %pad_maximum_fusion.4), channel_id=1, source_target_pairs={{0,4},{1,9},{2,6},{3,11},{4,0},{5,13},{6,2},{7,15},{8,12},{9,1},{1... | collective-permute-start | bytes 786440 | tf_op jit(solution)/shard_map/ppermute | solution.py:54
  52.3 6.2 %collective-permute-start.13 = (bf16[2,8,4096]{2,1,0:T(8,128)(2,1)S(1)}, bf16[2,8,4096]{2,1,0:T(8,128)(2,1)S(1)}, u32[]{:S(2)}, u32[]{:S(2)}) collective-permute-start(bf16[2,8,4096]{2,1,0:T(8,128)(2,1)S(1)} %pad_maximum_fusion.7), channel_id=1, source_target_pairs={{0,8},{1,3},{2,10},{3,1},{4,12},{5,7},{6,14},{7,5},{8,0},{9,11},{1... | collective-permute-start | bytes 393224 | tf_op jit(solution)/shard_map/ppermute | solution.py:54

commit v7 on v6

--- a/solution.py
+++ b/solution.py
@@ -152,7 +152,7 @@
         made = []
         for k in range(1, len(back)):
             terms, job = tie((terms, jobs[k - 1] if k <= 2 else ()))
-            sent = upper(terms) if k == 1 else jnp.stack([upper(terms), upper(out)])
+            sent = upper(terms) if k == 1 else join(upper(terms), upper(out))
             got = swap(sent, n, back[k])
             work = tuple(gradients(job)) if job else ()
             if k == 1:
@@ -161,7 +161,7 @@
                 terms = add(terms, got)
             else:
                 got, work = tie((got, work))
-                terms, out = tie((add(terms, got[0]), add(out, got[1])))
+                terms, out = tie((add(terms, lower(got)), add(out, got[got.shape[0] // 2 :])))
             made += work
         down_grad, gate_grad, up_grad = made
         return (out.astype(BF16), terms.astype(BF16), gate_grad, up_grad, down_grad)

time: 59.6 us -> 59.6 us (level)
  no operation moved by 1% of the time
where the time goes in v7:
time: 59.6 us; the launch traced here: 59.1 us
  starting transfers between devices  22.6 us (38%)
  matrix products  11.2 us (19%)
  Pallas kernels  9.89 us (17%)
  waiting for transfers between devices  8.08 us (14%)
  local copies, waits for them, and re-layouts  5.19 us (9%)
  other arithmetic  1.16 us (2%)
  between operations  0.96 us (2%)
    ppermute x14, starting transfers between devices, swap(): return lax.ppermute(x, 'tensor', [(i, i ^ stage[i % 2]) for i in range(n)])  22.6 us
    pallas_call x2, Pallas kernels, gradients(): pl.pallas_call(functools.partial(gradients_kernel, count), out_shape=[jax...  9.27 us
    ppermute x14, waiting for transfers between devices, swap(): return lax.ppermute(x, 'tensor', [(i, i ^ stage[i % 2]) for i in range(n)])  8.08 us
    dot_general x3, matrix products, rows_by_weight(): lax.dot_general(left, weight, (((1,), (1,)), ((), ())), preferred_element...  7.42 us
    unnamed x15, local copies, waits for them, and re-layouts  4.9 us
    dot_general x1, matrix products, per_device(): terms = terms + jnp.dot(d_up, up_weight, preferred_element_type=F32)  1.3 us
    dot_general x1, matrix products, per_device(): terms = jnp.dot(d_gate, gate_weight, preferred_element_type=F32)  1.26 us
    dot_general x1, matrix products, per_device(): jnp.dot(hidden, down_weight, preferred_element_type=F32)  1.26 us
  transfers between devices with their start and end apart: 14, of which 9 were waited for; matrix products, arithmetic and copies ran while one was open for 15% of the time, Pallas kernels for 17%

profile of v7, /device:TPU:0, one launch (start us, length us, event | category | flops | bytes accessed | tf_op | source)
XLA Modules:
  0.0 59.1 jit_solution(2292117244205186313)
XLA Ops:
  0.6 4.1 %collective-permute-start = (bf16[8,4096]{1,0:T(8,128)(2,1)}, bf16[8,4096]{1,0:T(8,128)(2,1)S(1)}, u32[]{:S(2)}, u32[]{:S(2)}) collective-permute-start(bf16[8,4096]{1,0:T(8,128)(2,1)} %after.2), channel_id=1, source_target_pairs={{0,8},{1,3},{2,10},{3,1},{4,12},{5,7},{6,14},{7,5},{8,0},{9,11},{1... | collective-permute-start | bytes 196616 | tf_op jit(solution)/shard_map/ppermute | solution.py:54
  4.7 0.9 %copy-done.1 = bf16[8,4096]{1,0:T(8,128)(2,1)S(1)} copy-done((bf16[8,4096]{1,0:T(8,128)(2,1)S(1)}, bf16[8,4096]{1,0:T(8,128)(2,1)}, u32[]{:S(2)}) %copy-start.1) | copy-done | bytes 65560
  5.7 0.8 %copy-done.2 = bf16[8,4096]{1,0:T(8,128)(2,1)S(1)} copy-done((bf16[8,4096]{1,0:T(8,128)(2,1)S(1)}, bf16[8,4096]{1,0:T(8,128)(2,1)}, u32[]{:S(2)}) %copy-start.2) | copy-done | bytes 65560
  6.6 0.6 %collective-permute-done = bf16[8,4096]{1,0:T(8,128)(2,1)S(1)} collective-permute-done((bf16[8,4096]{1,0:T(8,128)(2,1)}, bf16[8,4096]{1,0:T(8,128)(2,1)S(1)}, u32[]{:S(2)}, u32[]{:S(2)}) %collective-permute-start) | collective-permute-done | bytes 65568 | tf_op jit(solution)/shard_map/ppermute | solution.py:54
  7.2 2.0 %collective-permute-start.1 = (bf16[16,4096]{1,0:T(8,128)(2,1)S(1)}, bf16[16,4096]{1,0:T(8,128)(2,1)S(1)}, u32[]{:S(2)}, u32[]{:S(2)}) collective-permute-start(bf16[16,4096]{1,0:T(8,128)(2,1)S(1)} %pad_maximum_fusion.5), channel_id=1, source_target_pairs={{0,4},{1,9},{2,6},{3,11},{4,0},{5,13},{6,2},{7,15},{8,12},{9,1},{1... | collective-permute-start | bytes 393224 | tf_op jit(solution)/shard_map/ppermute | solution.py:54
  9.2 3.2 %collective-permute-start.3 = (bf16[8,4096]{1,0:T(8,128)(2,1)S(1)}, bf16[8,4096]{1,0:T(8,128)(2,1)S(1)}, u32[]{:S(2)}, u32[]{:S(2)}) collective-permute-start(bf16[8,4096]{1,0:T(8,128)(2,1)S(1)} %copy-done.2), channel_id=1, source_target_pairs={{0,8},{1,3},{2,10},{3,1},{4,12},{5,7},{6,14},{7,5},{8,0},{9,11},{1... | collective-permute-start | bytes 196616 | tf_op jit(solution)/shard_map/ppermute | solution.py:54
  12.5 2.0 %collective-permute-start.2 = (bf16[32,4096]{1,0:T(8,128)(2,1)S(1)}, bf16[32,4096]{1,0:T(8,128)(2,1)S(1)}, u32[]{:S(2)}, u32[]{:S(2)}) collective-permute-start(bf16[32,4096]{1,0:T(8,128)(2,1)S(1)} %pad_maximum_fusion.2.after), channel_id=1, source_target_pairs={{0,2},{1,5},{2,0},{3,7},{4,6},{5,1},{6,4},{7,3},{8,10},{9,13},{10,... | collective-permute-start | bytes 786440 | tf_op jit(solution)/shard_map/ppermute | solution.py:54
  14.5 0.3 collective-permute-done.3
  14.8 1.3 %collective-permute-start.4 = (bf16[16,4096]{1,0:T(8,128)(2,1)S(1)}, bf16[16,4096]{1,0:T(8,128)(2,1)S(1)}, u32[]{:S(2)}, u32[]{:S(2)}) collective-permute-start(bf16[16,4096]{1,0:T(8,128)(2,1)S(1)} %pad_maximum_fusion.6), channel_id=1, source_target_pairs={{0,4},{1,9},{2,6},{3,11},{4,0},{5,13},{6,2},{7,15},{8,12},{9,1},{1... | collective-permute-start | bytes 393224 | tf_op jit(solution)/shard_map/ppermute | solution.py:54
  16.1 3.1 %copy-done = bf16[896,4096]{1,0:T(8,128)(2,1)S(1)} copy-done((bf16[896,4096]{1,0:T(8,128)(2,1)S(1)}, bf16[896,4096]{1,0:T(8,128)(2,1)}, u32[]{:S(2)}) %copy-start) | copy-done | bytes 7340056
  19.2 0.5 shard_map.94
  19.7 0.5 collective-permute-done.4
  20.4 1.6 %collective-permute-start.6 = (bf16[32,4096]{1,0:T(8,128)(2,1)S(1)}, bf16[32,4096]{1,0:T(8,128)(2,1)S(1)}, u32[]{:S(2)}, u32[]{:S(2)}) collective-permute-start(bf16[32,4096]{1,0:T(8,128)(2,1)S(1)} %pad_maximum_fusion.3), channel_id=1, source_target_pairs={{0,2},{1,5},{2,0},{3,7},{4,6},{5,1},{6,4},{7,3},{8,10},{9,13},{10,... | collective-permute-start | bytes 786440 | tf_op jit(solution)/shard_map/ppermute | solution.py:54
  22.0 0.2 collective-permute-done.5
  22.3 2.5 %fusion.1 = f32[128,896]{1,0:T(8,128)S(1)} fusion(bf16[128,4096]{1,0:T(8,128)(2,1)S(1)} %constant_dynamic-update-slice_fusion.refs_3_.refs_1_, bf16[896,4096]{1,0:T(8,128)(2,1)S(1)} %copy-done.3), kind=kOutput, calls=%fused_computation.35 | convolution fusion | flops 939524096 | bytes 8847360 | tf_op jit(solution)/shard_map/dot_general | solution.py:17
  24.8 2.4 %multiply_convert_fusion.2 = (bf16[128,896]{1,0:T(8,128)(2,1)S(1)}, f32[128,896]{1,0:T(8,128)S(1)}) fusion(f32[128,896]{1,0:T(8,128)S(1)} %fusion.1, bf16[128,4096]{1,0:T(8,128)(2,1)S(1)} %constant_dynamic-update-slice_fusion.refs_3_.refs_1_, bf16[896,4096]{1,0:T(8,128)(2,1)S(1)} %shard_map.94), kind=kOutput, calls=%fused_computation.13 | convolution fusion | flops 940212224 | bytes 9535488 | tf_op jit(solution)/shard_map/dot_general | solution.py:17
  27.6 1.3 %fusion.2 = f32[128,4096]{1,0:T(8,128)S(1)} fusion(bf16[128,896]{1,0:T(8,128)(2,1)S(1)} %get-tuple-element.65.refs_0_, bf16[896,4096]{1,0:T(8,128)(2,1)S(1)} %bitcast.13), kind=kOutput, calls=%fused_computation.36 | convolution fusion | flops 939524096 | bytes 9666560 | tf_op jit(solution)/shard_map/dot_general | solution.py:136
  28.8 0.5 collective-permute-done.7
  29.6 2.5 %multiply_convert_fusion = (bf16[128,896]{1,0:T(8,128)(2,1)S(1)}, bf16[128,896]{1,0:T(8,128)(2,1)S(1)}) fusion(f32[128,896]{1,0:T(8,128)S(1)} %fusion.1, f32[128,896]{1,0:T(8,128)S(1)} %get-tuple-element.92, bf16[128,4096]{1,0:T(8,128)(2,1)S(1)} %constant_dynamic-update-slice_fusion.2.refs_1_, bf16[896,4096]{1,0:T(8,128)(2,1)S(1)} %bitcast.13), kind=kOutput, calls=%fused_computation.11 | convolution fusion | flops 941015040 | bytes 9764864 | tf_op jit(solution)/shard_map/dot_general | solution.py:17
  32.2 1.3 %fusion.3 = f32[128,4096]{1,0:T(8,128)S(1)} fusion(bf16[128,896]{1,0:T(8,128)(2,1)S(1)} %get-tuple-element.67.refs_2_, bf16[896,4096]{1,0:T(8,128)(2,1)S(1)} %copy-done.3), kind=kOutput, calls=%fused_computation.37 | convolution fusion | flops 939524096 | bytes 9666560 | tf_op jit(solution)/shard_map/dot_general | solution.py:148
  33.5 1.3 %convolution_add_fusion = f32[128,4096]{1,0:T(8,128)S(1)} fusion(f32[128,4096]{1,0:T(8,128)S(1)} %fusion.3, bf16[128,896]{1,0:T(8,128)(2,1)S(1)} %get-tuple-element.75.refs_0_, bf16[896,4096]{1,0:T(8,128)(2,1)S(1)} %shard_map.94), kind=kOutput, calls=%fused_computation | convolution fusion | flops 940048384 | bytes 11763712 | tf_op jit(solution)/shard_map/dot_general | solution.py:149
  34.9 0.4 collective-permute-start.9
  35.3 1.6 %collective-permute-start.11 = (bf16[32,4096]{1,0:T(8,128)(2,1)S(1)}, bf16[32,4096]{1,0:T(8,128)(2,1)S(1)}, u32[]{:S(2)}, u32[]{:S(2)}) collective-permute-start(bf16[32,4096]{1,0:T(8,128)(2,1)S(1)} %slice.123), channel_id=1, source_target_pairs={{0,2},{1,5},{2,0},{3,7},{4,6},{5,1},{6,4},{7,3},{8,10},{9,13},{10,... | collective-permute-start | bytes 786440 | tf_op jit(solution)/shard_map/ppermute | solution.py:54
  37.0 1.5 %collective-permute-start.10 = (bf16[32,4096]{1,0:T(8,128)(2,1)S(1)}, bf16[32,4096]{1,0:T(8,128)(2,1)S(1)}, u32[]{:S(2)}, u32[]{:S(2)}) collective-permute-start(bf16[32,4096]{1,0:T(8,128)(2,1)S(1)} %slice.124), channel_id=1, source_target_pairs={{0,2},{1,5},{2,0},{3,7},{4,6},{5,1},{6,4},{7,3},{8,10},{9,13},{10,... | collective-permute-start | bytes 786440 | tf_op jit(solution)/shard_map/ppermute | solution.py:54
  38.6 5.8 %shard_map.95 = (bf16[896,4096]{1,0:T(8,128)(2,1)}, bf16[896,4096]{1,0:T(8,128)(2,1)}) custom-call(bf16[128,896]{1,0:T(8,128)(2,1)S(1)} %get-tuple-element.65.refs_0_, bf16[128,4096]{1,0:T(8,128)(2,1)S(1)} %constant_dynamic-update-slice_fusion.2.refs_1_, bf16[128,896]{1,0:T(8,128)(2,1)S(1)} %get-tuple-element.67.refs_2_, ...), custom_call_target="tpu_custom_call" | custom-call | flops 1879048192 | bytes 14680064 | tf_op jit(solution)/shard_map/pallas_call | solution.py:93
  44.3 0.2 collective-permute-done.10
  44.7 1.3 %collective-permute-start.12 = (bf16[32,4096]{1,0:T(8,128)(2,1)S(1)}, bf16[32,4096]{1,0:T(8,128)(2,1)S(1)}, u32[]{:S(2)}, u32[]{:S(2)}) collective-permute-start(bf16[32,4096]{1,0:T(8,128)(2,1)S(1)} %pad_maximum_fusion.4), channel_id=1, source_target_pairs={{0,4},{1,9},{2,6},{3,11},{4,0},{5,13},{6,2},{7,15},{8,12},{9,1},{1... | collective-permute-start | bytes 786440 | tf_op jit(solution)/shard_map/ppermute | solution.py:54
  46.1 3.5 %shard_map.96 = bf16[896,4096]{1,0:T(8,128)(2,1)} custom-call(bf16[128,896]{1,0:T(8,128)(2,1)S(1)} %get-tuple-element.75.refs_0_, bf16[128,4096]{1,0:T(8,128)(2,1)S(1)} %constant_dynamic-update-slice_fusion.refs_3_.refs_1_), custom_call_target="tpu_custom_call" | custom-call | flops 939524096 | bytes 7340032 | tf_op jit(solution)/shard_map/pallas_call | solution.py:93
  49.6 2.6 %collective-permute-done.12 = bf16[32,4096]{1,0:T(8,128)(2,1)S(1)} collective-permute-done((bf16[32,4096]{1,0:T(8,128)(2,1)S(1)}, bf16[32,4096]{1,0:T(8,128)(2,1)S(1)}, u32[]{:S(2)}, u32[]{:S(2)}) %collective-permute-start.12) | collective-permute-done | bytes 262176 | tf_op jit(solution)/shard_map/ppermute | solution.py:54
  52.3 3.2 %collective-permute-start.13 = (bf16[16,4096]{1,0:T(8,128)(2,1)S(1)}, bf16[16,4096]{1,0:T(8,128)(2,1)S(1)}, u32[]{:S(2)}, u32[]{:S(2)}) collective-permute-start(bf16[16,4096]{1,0:T(8,128)(2,1)S(1)} %pad_maximum_fusion.7), channel_id=1, source_target_pairs={{0,8},{1,3},{2,10},{3,1},{4,12},{5,7},{6,14},{7,5},{8,0},{9,11},{1... | collective-permute-start | bytes 393224 | tf_op jit(solution)/shard_map/ppermute | solution.py:54
  55.5 2.9 %collective-permute-done.13 = bf16[16,4096]{1,0:T(8,128)(2,1)S(1)} collective-permute-done((bf16[16,4096]{1,0:T(8,128)(2,1)S(1)}, bf16[16,4096]{1,0:T(8,128)(2,1)S(1)}, u32[]{:S(2)}, u32[]{:S(2)}) %collective-permute-start.13) | collective-permute-done | bytes 131104 | tf_op jit(solution)/shard_map/ppermute | solution.py:54
  58.5 0.7 %convert_add_fusion.4 = (bf16[8,4096]{1,0:T(8,128)(2,1)}, bf16[8,4096]{1,0:T(8,128)(2,1)}) fusion(f32[16,4096]{1,0:T(8,128)S(1)} %get-tuple-element.79, bf16[16,4096]{1,0:T(8,128)(2,1)S(1)} %collective-permute-done.13, f32[16,4096]{1,0:T(8,128)S(1)} %get-tuple-element.78), kind=kLoop, calls=%fused_computation.29 | loop fusion | flops 196608 | bytes 524288 | tf_op jit(solution)/shard_map/add | solution.py:73
  (46 shorter events, 1.6 us)
Async XLA Ops:
  0.6 6.6 %collective-permute-start = (bf16[8,4096]{1,0:T(8,128)(2,1)}, bf16[8,4096]{1,0:T(8,128)(2,1)S(1)}, u32[]{:S(2)}, u32[]{:S(2)}) collective-permute-start(bf16[8,4096]{1,0:T(8,128)(2,1)} %after.2), channel_id=1, source_target_pairs={{0,8},{1,3},{2,10},{3,1},{4,12},{5,7},{6,14},{7,5},{8,0},{9,11},{1... | collective-permute-start | bytes 196616 | tf_op jit(solution)/shard_map/ppermute | solution.py:54
  4.7 0.9 %copy-start.1 = (bf16[8,4096]{1,0:T(8,128)(2,1)S(1)}, bf16[8,4096]{1,0:T(8,128)(2,1)}, u32[]{:S(2)}) copy-start(bf16[8,4096]{1,0:T(8,128)(2,1)} %after.2) | copy-start | bytes 196612
  5.7 0.8 %copy-start.2 = (bf16[8,4096]{1,0:T(8,128)(2,1)S(1)}, bf16[8,4096]{1,0:T(8,128)(2,1)}, u32[]{:S(2)}) copy-start(bf16[8,4096]{1,0:T(8,128)(2,1)} %after.3) | copy-start | bytes 196612
  7.2 5.3 %collective-permute-start.1 = (bf16[16,4096]{1,0:T(8,128)(2,1)S(1)}, bf16[16,4096]{1,0:T(8,128)(2,1)S(1)}, u32[]{:S(2)}, u32[]{:S(2)}) collective-permute-start(bf16[16,4096]{1,0:T(8,128)(2,1)S(1)} %pad_maximum_fusion.5), channel_id=1, source_target_pairs={{0,4},{1,9},{2,6},{3,11},{4,0},{5,13},{6,2},{7,15},{8,12},{9,1},{1... | collective-permute-start | bytes 393224 | tf_op jit(solution)/shard_map/ppermute | solution.py:54
  9.2 5.6 %collective-permute-start.3 = (bf16[8,4096]{1,0:T(8,128)(2,1)S(1)}, bf16[8,4096]{1,0:T(8,128)(2,1)S(1)}, u32[]{:S(2)}, u32[]{:S(2)}) collective-permute-start(bf16[8,4096]{1,0:T(8,128)(2,1)S(1)} %copy-done.2), channel_id=1, source_target_pairs={{0,8},{1,3},{2,10},{3,1},{4,12},{5,7},{6,14},{7,5},{8,0},{9,11},{1... | collective-permute-start | bytes 196616 | tf_op jit(solution)/shard_map/ppermute | solution.py:54
  12.5 7.7 %collective-permute-start.2 = (bf16[32,4096]{1,0:T(8,128)(2,1)S(1)}, bf16[32,4096]{1,0:T(8,128)(2,1)S(1)}, u32[]{:S(2)}, u32[]{:S(2)}) collective-permute-start(bf16[32,4096]{1,0:T(8,128)(2,1)S(1)} %pad_maximum_fusion.2.after), channel_id=1, source_target_pairs={{0,2},{1,5},{2,0},{3,7},{4,6},{5,1},{6,4},{7,3},{8,10},{9,13},{10,... | collective-permute-start | bytes 786440 | tf_op jit(solution)/shard_map/ppermute | solution.py:54
  14.8 5.4 %collective-permute-start.4 = (bf16[16,4096]{1,0:T(8,128)(2,1)S(1)}, bf16[16,4096]{1,0:T(8,128)(2,1)S(1)}, u32[]{:S(2)}, u32[]{:S(2)}) collective-permute-start(bf16[16,4096]{1,0:T(8,128)(2,1)S(1)} %pad_maximum_fusion.6), channel_id=1, source_target_pairs={{0,4},{1,9},{2,6},{3,11},{4,0},{5,13},{6,2},{7,15},{8,12},{9,1},{1... | collective-permute-start | bytes 393224 | tf_op jit(solution)/shard_map/ppermute | solution.py:54
  16.1 3.1 %copy-start = (bf16[896,4096]{1,0:T(8,128)(2,1)S(1)}, bf16[896,4096]{1,0:T(8,128)(2,1)}, u32[]{:S(2)}) copy-start(bf16[896,4096]{1,0:T(8,128)(2,1)} %weight.5) | copy-start | bytes 22020100
  19.2 3.1 %copy-start.3 = (bf16[896,4096]{1,0:T(8,128)(2,1)S(1)}, bf16[896,4096]{1,0:T(8,128)(2,1)}, u32[]{:S(2)}) copy-start(bf16[896,4096]{1,0:T(8,128)(2,1)} %param.6) | copy-start | bytes 22020100
  20.3 2.0 %collective-permute-start.5 = (bf16[64,4096]{1,0:T(8,128)(2,1)S(1)}, bf16[64,4096]{1,0:T(8,128)(2,1)S(1)}, u32[]{:S(2)}, u32[]{:S(2)}) collective-permute-start(bf16[64,4096]{1,0:T(8,128)(2,1)S(1)} %pad_maximum_fusion), channel_id=1, source_target_pairs={{0,1},{1,0},{2,3},{3,2},{4,5},{5,4},{6,7},{7,6},{8,9},{9,8},{10,11... | collective-permute-start | bytes 1572872 | tf_op jit(solution)/shard_map/ppermute | solution.py:54
  20.4 6.9 %collective-permute-start.6 = (bf16[32,4096]{1,0:T(8,128)(2,1)S(1)}, bf16[32,4096]{1,0:T(8,128)(2,1)S(1)}, u32[]{:S(2)}, u32[]{:S(2)}) collective-permute-start(bf16[32,4096]{1,0:T(8,128)(2,1)S(1)} %pad_maximum_fusion.3), channel_id=1, source_target_pairs={{0,2},{1,5},{2,0},{3,7},{4,6},{5,1},{6,4},{7,3},{8,10},{9,13},{10,... | collective-permute-start | bytes 786440 | tf_op jit(solution)/shard_map/ppermute | solution.py:54
  22.3 5.2 %slice-start = ((s8[7340032]{0:T(1024)(128)(4,1)}), s8[4194304]{0:T(1024)(128)(4,1)S(1)}, s32[]{:S(2)}) async-start(s8[7340032]{0:T(1024)(128)(4,1)} %bitcast.12), calls=%async_computation | async-start | bytes 8388608
  24.8 2.8 %slice-start.1 = ((s8[7340032]{0:T(1024)(128)(4,1)}), s8[3145728]{0:T(1024)(128)(4,1)S(1)}, s32[]{:S(2)}) async-start(s8[7340032]{0:T(1024)(128)(4,1)} %bitcast.12), calls=%async_computation.1 | async-start | bytes 6291456
  27.3 2.0 %collective-permute-start.7 = (bf16[64,4096]{1,0:T(8,128)(2,1)S(1)}, bf16[64,4096]{1,0:T(8,128)(2,1)S(1)}, u32[]{:S(2)}, u32[]{:S(2)}) collective-permute-start(bf16[64,4096]{1,0:T(8,128)(2,1)S(1)} %pad_maximum_fusion.1), channel_id=1, source_target_pairs={{0,1},{1,0},{2,3},{3,2},{4,5},{5,4},{6,7},{7,6},{8,9},{9,8},{10,11... | collective-permute-start | bytes 1572872 | tf_op jit(solution)/shard_map/ppermute | solution.py:54
  29.3 2.8 %collective-permute-start.8 = (bf16[64,4096]{1,0:T(8,128)(2,1)S(1)}, bf16[64,4096]{1,0:T(8,128)(2,1)S(1)}, u32[]{:S(2)}, u32[]{:S(2)}) collective-permute-start(bf16[64,4096]{1,0:T(8,128)(2,1)S(1)} %slice.122), channel_id=1, source_target_pairs={{0,1},{1,0},{2,3},{3,2},{4,5},{5,4},{6,7},{7,6},{8,9},{9,8},{10,11... | collective-permute-start | bytes 1572872 | tf_op jit(solution)/shard_map/ppermute | solution.py:54
  34.9 2.1 %collective-permute-start.9 = (bf16[64,4096]{1,0:T(8,128)(2,1)S(1)}, bf16[64,4096]{1,0:T(8,128)(2,1)S(1)}, u32[]{:S(2)}, u32[]{:S(2)}) collective-permute-start(bf16[64,4096]{1,0:T(8,128)(2,1)S(1)} %slice.121), channel_id=1, source_target_pairs={{0,1},{1,0},{2,3},{3,2},{4,5},{5,4},{6,7},{7,6},{8,9},{9,8},{10,11... | collective-permute-start | bytes 1572872 | tf_op jit(solution)/shard_map/ppermute | solution.py:54
  35.3 9.0 %collective-permute-start.11 = (bf16[32,4096]{1,0:T(8,128)(2,1)S(1)}, bf16[32,4096]{1,0:T(8,128)(2,1)S(1)}, u32[]{:S(2)}, u32[]{:S(2)}) collective-permute-start(bf16[32,4096]{1,0:T(8,128)(2,1)S(1)} %slice.123), channel_id=1, source_target_pairs={{0,2},{1,5},{2,0},{3,7},{4,6},{5,1},{6,4},{7,3},{8,10},{9,13},{10,... | collective-permute-start | bytes 786440 | tf_op jit(solution)/shard_map/ppermute | solution.py:54
  37.0 7.5 %collective-permute-start.10 = (bf16[32,4096]{1,0:T(8,128)(2,1)S(1)}, bf16[32,4096]{1,0:T(8,128)(2,1)S(1)}, u32[]{:S(2)}, u32[]{:S(2)}) collective-permute-start(bf16[32,4096]{1,0:T(8,128)(2,1)S(1)} %slice.124), channel_id=1, source_target_pairs={{0,2},{1,5},{2,0},{3,7},{4,6},{5,1},{6,4},{7,3},{8,10},{9,13},{10,... | collective-permute-start | bytes 786440 | tf_op jit(solution)/shard_map/ppermute | solution.py:54
  44.7 7.5 %collective-permute-start.12 = (bf16[32,4096]{1,0:T(8,128)(2,1)S(1)}, bf16[32,4096]{1,0:T(8,128)(2,1)S(1)}, u32[]{:S(2)}, u32[]{:S(2)}) collective-permute-start(bf16[32,4096]{1,0:T(8,128)(2,1)S(1)} %pad_maximum_fusion.4), channel_id=1, source_target_pairs={{0,4},{1,9},{2,6},{3,11},{4,0},{5,13},{6,2},{7,15},{8,12},{9,1},{1... | collective-permute-start | bytes 786440 | tf_op jit(solution)/shard_map/ppermute | solution.py:54
  52.3 6.2 %collective-permute-start.13 = (bf16[16,4096]{1,0:T(8,128)(2,1)S(1)}, bf16[16,4096]{1,0:T(8,128)(2,1)S(1)}, u32[]{:S(2)}, u32[]{:S(2)}) collective-permute-start(bf16[16,4096]{1,0:T(8,128)(2,1)S(1)} %pad_maximum_fusion.7), channel_id=1, source_target_pairs={{0,8},{1,3},{2,10},{3,1},{4,12},{5,7},{6,14},{7,5},{8,0},{9,11},{1... | collective-permute-start | bytes 393224 | tf_op jit(solution)/shard_map/ppermute | solution.py:54
